TPU v7x, 32 devices: a whole 2x2x4 slice. The times are simulated.
32 devices in a mesh: geom: 2 (over x), row: 8 (over z, y), col: 2 (over core).
Axes of the slice: x: 2, y: 2, z: 4, core: 2. Of those that a mesh axis runs over, the one named last changes fastest.
Arguments:
- matrix: bfloat16 [128, 8, 128, 128], P(('geom', 'row'), 'col'), parts along dimension 0, may hold values from -1.5 to 1.5
- columns: int32 [64, 8], P('row'), may hold values from -1 to 63, as said below
Outputs:
- purified: bfloat16 [128, 8, 128, 128], P(('geom', 'row'), 'col'), parts along dimension 0
There are 2 independent parts, one for each index of `geom`. A program takes and returns all parts, laid end to end along the dimension named above; an argument that names none is the same for every part. Nothing has to cross between parts.
Inputs may be any that keep to these rules, and one draw needn't show every extreme that they name: In block row i the valid slots come first and slot 0 holds i; valid slots hold distinct columns (i + d) mod 64 with -4 <= d <= 4, and the others hold -1. A block row has 1 to 8 valid slots, and some block row has 8.
All inputs are finite; a program needn't handle non-finite values.
Results may differ from a plain program's by a relative error of at most 0.0049.
Values may be sent and summed in bfloat16 or wider, within the bound.
No kernel may reach another device: no remote copies, remote signals or barrier semaphores. Data moves between devices by JAX's collectives and lax.ppermute only.
A program may use at most 64 MiB of HBM per device.

v0:
```python
import jax
import jax.numpy as jnp
from jax import lax
from jax.sharding import PartitionSpec as P

REACH = 4


group_rows = 8


def from_behind(value, axis, by):
    devices = lax.axis_size(axis)
    return lax.ppermute(value, axis, [(i, (i + by) % devices) for i in range(devices)])


def local(matrix, columns):
    local_rows = matrix.shape[0]
    own_slots = matrix.shape[1]
    block_size = matrix.shape[2]
    slot_count = columns.shape[1]
    reach_rows = REACH
    total_rows = local_rows * lax.axis_size("row")
    row_start = lax.axis_index("row") * local_rows
    first_slot = lax.axis_index("col") * own_slots
    whole_rows = lax.all_gather(matrix, "col", axis=1, tiled=True)
    from_below = from_behind(
        (whole_rows[local_rows - reach_rows :], columns[local_rows - reach_rows :]), "row", 1
    )
    from_above = from_behind((whole_rows[:reach_rows], columns[:reach_rows]), "row", -1)
    panel_rows = jnp.concatenate([from_below[0], whole_rows, from_above[0]], axis=0)
    panel_cols = jnp.concatenate([from_below[1], columns, from_above[1]], axis=0)
    own_targets = lax.dynamic_slice_in_dim(columns, first_slot, own_slots, 1)
    slot_ids = jnp.arange(slot_count, dtype=jnp.int32)
    empty_index = panel_rows.shape[0] * slot_count
    flat_blocks = jnp.concatenate(
        [
            panel_rows.reshape(-1, block_size, block_size),
            jnp.zeros((1, block_size, block_size), panel_rows.dtype),
        ],
        axis=0,
    )

    def partial_product(left_blocks, index_table):
        left_slots = left_blocks.shape[1]
        out_slots = index_table.shape[2]
        groups = local_rows // group_rows

        def one_group(inputs):
            left_group, index_group = inputs
            picked = flat_blocks[index_group]
            return jnp.einsum(
                "ijab,ijsbc->isac", left_group, picked, preferred_element_type=jnp.float32
            )

        stacked = lax.map(
            one_group,
            (
                left_blocks.reshape(groups, group_rows, left_slots, block_size, block_size),
                index_table.reshape(groups, group_rows, left_slots, out_slots),
            ),
        )
        return stacked.reshape(local_rows, out_slots, block_size, block_size)

    has_source = columns >= 0
    position = jnp.where(has_source, (columns - row_start + reach_rows) % total_rows, 0)
    source_cols = panel_cols[position]
    matches = (
        (source_cols[:, :, None, :] == own_targets[:, None, :, None])
        & (own_targets[:, None, :, None] >= 0)
        & has_source[:, :, None, None]
    )
    chosen = jnp.sum(jnp.where(matches, slot_ids, 0), axis=3)
    found_match = jnp.any(matches, axis=3)
    index_table = jnp.where(found_match, position[:, :, None] * slot_count + chosen, empty_index)
    live_count = jnp.sum(has_source.astype(jnp.int32), axis=1)
    index_table, live_count = (index_table, live_count)
    square = partial_product(whole_rows, index_table).astype(jnp.bfloat16)
    square_whole = lax.all_gather(square, "col", axis=1, tiled=True)
    cube_sum = partial_product(square_whole, index_table)
    return (3.0 * square.astype(jnp.float32) - 2.0 * cube_sum).astype(jnp.bfloat16)


def solution(mesh):
    placed = (P(("geom", "row"), "col", None, None), P("row", None))
    return jax.shard_map(
        local,
        mesh=mesh,
        in_specs=placed,
        out_specs=P(("geom", "row"), "col", None, None),
        check_vma=False,
    )
```

profile of v0, /device:TPU:0, one launch (start us, length us, event | category | flops | bytes accessed | tf_op | source)
XLA Modules:
  0.0 122.6 jit_solution(10887109171620727217)
XLA Ops:
  6.5 0.7 all-gather.3.cloned.1.call-update
  7.3 0.8 fusion.19
  8.1 3.0 %collective-permute-start.2 = (s32[4,8]{1,0:T(4,128)S(1)}, s32[4,8]{1,0:T(4,128)S(1)}, u32[]{:S(2)}, u32[]{:S(2)}) collective-permute-start(s32[4,8]{1,0:T(4,128)S(1)} %get-tuple-element.34), channel_id=1, source_target_pairs={{0,2},{2,4},{4,6},{6,8},{8,10},{10,12},{12,14},{14,0},{1,3},{3,5},... | collective-permute-start | bytes 392 | tf_op jit(solution)/shard_map/ppermute | solution.py:14
  11.0 3.0 %collective-permute-start.3 = (s32[4,8]{1,0:T(4,128)S(1)}, s32[4,8]{1,0:T(4,128)S(1)}, u32[]{:S(2)}, u32[]{:S(2)}) collective-permute-start(s32[4,8]{1,0:T(4,128)S(1)} %get-tuple-element.40), channel_id=1, source_target_pairs={{0,14},{2,0},{4,2},{6,4},{8,6},{10,8},{12,10},{14,12},{1,15},{3,1}... | collective-permute-start | bytes 392 | tf_op jit(solution)/shard_map/ppermute | solution.py:14
  14.1 0.7 broadcast_multiply_fusion
  14.8 7.4 %all-gather.3.cloned.1.call-done = bf16[8,8,128,128]{3,2,1,0:T(8,128)(2,1)} async-done(((bf16[8,4,128,128]{3,2,1,0:T(8,128)(2,1)}), bf16[8,8,128,128]{3,2,1,0:T(8,128)(2,1)}) %all-gather.3.cloned.1.call-update) | async-done | bytes 2097168 | tf_op jit(solution)/shard_map/all_gather | solution.py:26
  22.2 2.9 %fusion.18 = (bf16[4,8,128,128]{3,2,1,0:T(8,128)(2,1)}, bf16[4,8,128,128]{3,2,1,0:T(8,128)(2,1)S(1)}) fusion(bf16[8,8,128,128]{3,2,1,0:T(8,128)(2,1)} %all-gather.3.cloned.1.call-done), kind=kLoop, calls=%fused_computation.32 | loop fusion | bytes 4194304 | tf_op jit(solution)/shard_map/slice | solution.py:28
  25.1 1.7 %collective-permute-start = (bf16[4,8,128,128]{3,2,1,0:T(8,128)(2,1)}, bf16[4,8,128,128]{3,2,1,0:T(8,128)(2,1)}, u32[]{:S(2)}, u32[]{:S(2)}) collective-permute-start(bf16[4,8,128,128]{3,2,1,0:T(8,128)(2,1)} %get-tuple-element.30), channel_id=1, source_target_pairs={{0,2},{2,4},{4,6},{6,8},{8,10},{10,12},{12,14},{14,0},{1,3},{3,5},... | collective-permute-start | bytes 3145736 | tf_op jit(solution)/shard_map/ppermute | solution.py:14
  26.9 3.0 %collective-permute-start.1 = (bf16[4,8,128,128]{3,2,1,0:T(8,128)(2,1)S(1)}, bf16[4,8,128,128]{3,2,1,0:T(8,128)(2,1)}, u32[]{:S(2)}, u32[]{:S(2)}) collective-permute-start(bf16[4,8,128,128]{3,2,1,0:T(8,128)(2,1)S(1)} %get-tuple-element.31), channel_id=1, source_target_pairs={{0,14},{2,0},{4,2},{6,4},{8,6},{10,8},{12,10},{14,12},{1,15},{3,1}... | collective-permute-start | bytes 3145736 | tf_op jit(solution)/shard_map/ppermute | solution.py:14
  29.9 0.1 reshape.50
  30.1 0.6 gather_fusion
  30.7 0.7 fusion.14
  31.4 0.7 select_reduce_fusion
  32.1 0.1 copy.9
  32.3 0.1 reshape.58
  32.4 40.1 %collective-permute-done = bf16[4,8,128,128]{3,2,1,0:T(8,128)(2,1)} collective-permute-done((bf16[4,8,128,128]{3,2,1,0:T(8,128)(2,1)}, bf16[4,8,128,128]{3,2,1,0:T(8,128)(2,1)}, u32[]{:S(2)}, u32[]{:S(2)}) %collective-permute-start) | collective-permute-done | bytes 1048608 | tf_op jit(solution)/shard_map/ppermute | solution.py:14
  72.5 2.0 %collective-permute-done.1 = bf16[4,8,128,128]{3,2,1,0:T(8,128)(2,1)} collective-permute-done((bf16[4,8,128,128]{3,2,1,0:T(8,128)(2,1)S(1)}, bf16[4,8,128,128]{3,2,1,0:T(8,128)(2,1)}, u32[]{:S(2)}, u32[]{:S(2)}) %collective-permute-start.1) | collective-permute-done | bytes 1048608 | tf_op jit(solution)/shard_map/ppermute | solution.py:14
  74.5 1.8 %pad_maximum_fusion = bf16[16,8,128,128]{3,2,1,0:T(8,128)(2,1)S(1)} fusion(bf16[4,8,128,128]{3,2,1,0:T(8,128)(2,1)} %collective-permute-done.1, bf16[8,8,128,128]{3,2,1,0:T(8,128)(2,1)S(1)} %copy-done, bf16[4,8,128,128]{3,2,1,0:T(8,128)(2,1)} %collective-permute-done), kind=kLoop, calls=%fused_computation.2 | loop fusion | flops 4194304 | bytes 8388608 | tf_op jit(solution)/shard_map/concatenate | solution.py:31
  76.3 2.8 %concatenate.10 = bf16[129,128,128]{2,1,0:T(8,128)(2,1)} pad(bf16[128,128,128]{2,1,0:T(8,128)(2,1)S(1)} %bitcast.63, bf16[]{:T(256)} %constant.26.clone.1), padding=0_1x0_0x0_0 | pad | bytes 8421378 | tf_op jit(solution)/shard_map/concatenate | solution.py:36
  79.1 10.7 %gather_fusion.1 = bf16[256,128,128]{2,1,0:T(8,128)(2,1)} fusion(bf16[129,128,128]{2,1,0:T(8,128)(2,1)} %concatenate.10, s32[1024]{0:T(1024)S(1)} %pad_clamp_fusion), kind=kCustom, calls=%fused_computation.1 | custom fusion | bytes 16778240 | tf_op jit(solution)/shard_map/while/body/eval_jaxpr/gather | solution.py:51
  89.8 7.1 %fusion.11 = bf16[8,4,128,128]{2,3,1,0:T(8,128)(2,1)} fusion(bf16[8,8,4,128,128]{4,3,2,1,0:T(8,128)(2,1)} %bitcast.64, bf16[8,8,128,128]{3,2,1,0:T(8,128)(2,1)S(1)} %copy-done), kind=kOutput, calls=%fused_computation.12 | convolution fusion | flops 1074266112 | bytes 11534336 | tf_op jit(solution)/shard_map/while/body/eval_jaxpr/ijab,ijsbc->isac/dot_general | solution.py:52
  96.9 10.6 %all-gather.5.cloned.1.call-done = bf16[8,8,128,128]{2,3,1,0:T(8,128)(2,1)} async-done(((bf16[8,4,128,128]{2,3,1,0:T(8,128)(2,1)}), bf16[8,8,128,128]{2,3,1,0:T(8,128)(2,1)}) %all-gather.5.cloned.1.call-update) | async-done | bytes 2097168 | tf_op jit(solution)/shard_map/all_gather | solution.py:79
  107.5 7.0 %fusion.2 = bf16[8,4,128,128]{2,3,1,0:T(8,128)(2,1)S(1)} fusion(bf16[8,4,128,128]{2,3,1,0:T(8,128)(2,1)} %fusion.11, bf16[8,8,4,128,128]{4,3,2,1,0:T(8,128)(2,1)} %bitcast.65, bf16[8,8,128,128]{2,3,1,0:T(8,128)(2,1)} %all-gather.5.cloned.1.call-done), kind=kOutput, calls=%fused_computation.6 | convolution fusion | flops 1076363264 | bytes 12582912 | tf_op jit(solution)/shard_map/while/body/eval_jaxpr/ijab,ijsbc->isac/dot_general | solution.py:52
  114.5 1.3 %copy.13 = bf16[8,4,128,128]{3,2,1,0:T(8,128)(2,1)} copy(bf16[8,4,128,128]{2,3,1,0:T(8,128)(2,1)S(1)} %fusion.2) | data formatting | bytes 2097152 | tf_op jit(solution)/shard_map/convert_element_type | solution.py:81
  (15 shorter events, 0.2 us)
Async XLA Ops:
  6.5 23.3 %copy-start.1 = (s32[8,8]{1,0:T(8,128)S(1)}, s32[8,8]{1,0:T(8,128)}, u32[]{:S(2)}) copy-start(s32[8,8]{1,0:T(8,128)} %param.3) | copy-start | bytes 772
  6.5 15.7 %all-gather.3.cloned.1.call-start = ((), (), s32[]{:S(2)}) async-start(), calls=%async_computation | async-start | bytes 3145728 | tf_op jit(solution)/shard_map/all_gather | solution.py:26
  7.3 100.3 %all-gather.5.cloned.1.call-start = ((), (), s32[]{:S(2)}) async-start(), calls=%async_computation.1 | async-start | bytes 3145728 | tf_op jit(solution)/shard_map/all_gather | solution.py:79
  8.1 22.0 %collective-permute-start.2 = (s32[4,8]{1,0:T(4,128)S(1)}, s32[4,8]{1,0:T(4,128)S(1)}, u32[]{:S(2)}, u32[]{:S(2)}) collective-permute-start(s32[4,8]{1,0:T(4,128)S(1)} %get-tuple-element.34), channel_id=1, source_target_pairs={{0,2},{2,4},{4,6},{6,8},{8,10},{10,12},{12,14},{14,0},{1,3},{3,5},... | collective-permute-start | bytes 392 | tf_op jit(solution)/shard_map/ppermute | solution.py:14
  11.0 19.0 %collective-permute-start.3 = (s32[4,8]{1,0:T(4,128)S(1)}, s32[4,8]{1,0:T(4,128)S(1)}, u32[]{:S(2)}, u32[]{:S(2)}) collective-permute-start(s32[4,8]{1,0:T(4,128)S(1)} %get-tuple-element.40), channel_id=1, source_target_pairs={{0,14},{2,0},{4,2},{6,4},{8,6},{10,8},{12,10},{14,12},{1,15},{3,1}... | collective-permute-start | bytes 392 | tf_op jit(solution)/shard_map/ppermute | solution.py:14
  22.2 52.3 %copy-start = (bf16[8,8,128,128]{3,2,1,0:T(8,128)(2,1)S(1)}, bf16[8,8,128,128]{3,2,1,0:T(8,128)(2,1)}, u32[]{:S(2)}) copy-start(bf16[8,8,128,128]{3,2,1,0:T(8,128)(2,1)} %all-gather.3.cloned.1.call-done) | copy-start | bytes 6291460
  25.1 47.4 %collective-permute-start = (bf16[4,8,128,128]{3,2,1,0:T(8,128)(2,1)}, bf16[4,8,128,128]{3,2,1,0:T(8,128)(2,1)}, u32[]{:S(2)}, u32[]{:S(2)}) collective-permute-start(bf16[4,8,128,128]{3,2,1,0:T(8,128)(2,1)} %get-tuple-element.30), channel_id=1, source_target_pairs={{0,2},{2,4},{4,6},{6,8},{8,10},{10,12},{12,14},{14,0},{1,3},{3,5},... | collective-permute-start | bytes 3145736 | tf_op jit(solution)/shard_map/ppermute | solution.py:14
  26.9 47.7 %collective-permute-start.1 = (bf16[4,8,128,128]{3,2,1,0:T(8,128)(2,1)S(1)}, bf16[4,8,128,128]{3,2,1,0:T(8,128)(2,1)}, u32[]{:S(2)}, u32[]{:S(2)}) collective-permute-start(bf16[4,8,128,128]{3,2,1,0:T(8,128)(2,1)S(1)} %get-tuple-element.31), channel_id=1, source_target_pairs={{0,14},{2,0},{4,2},{6,4},{8,6},{10,8},{12,10},{14,12},{1,15},{3,1}... | collective-permute-start | bytes 3145736 | tf_op jit(solution)/shard_map/ppermute | solution.py:14
Sparse Core Ops, SparseCore 0:
  8.9 13.2 all-gather.2
  97.0 10.4 all-gather.4
where the time goes:
time: 123 us
  waiting for transfers between devices  60.9 us (50%)
  local copies, waits for them, and re-layouts  19.4 us (16%)
  matrix products  14 us (11%)
  between operations  13.5 us (11%)
  starting transfers between devices  10.8 us (9%)
  other arithmetic  4.05 us (3%)
    ppermute x4, waiting for transfers between devices, from_behind(): lax.ppermute(value, axis, [(i, (i + by) % devices) for i in range(devices)])  42.1 us
    dot_general x2, matrix products, one_group(): jnp.einsum('ijab,ijsbc->isac', left_group, picked, preferred_element_type...  14 us
    ppermute x4, starting transfers between devices, from_behind(): lax.ppermute(value, axis, [(i, (i + by) % devices) for i in range(devices)])  10.7 us
    gather x1, local copies, waits for them, and re-layouts, one_group(): picked = flat_blocks[index_group]  10.7 us
    all_gather x1, waiting for transfers between devices, local(): square_whole = lax.all_gather(square, 'col', axis=1, tiled=True)  10.6 us
    all_gather x1, waiting for transfers between devices, local(): whole_rows = lax.all_gather(matrix, 'col', axis=1, tiled=True)  7.43 us
    slice x1, local copies, waits for them, and re-layouts, local(): whole_rows[local_rows - reach_rows:]  2.91 us
    concatenate x1, local copies, waits for them, and re-layouts, local(): jnp.concatenate([panel_rows.reshape(-1, block_size, block_size), jnp.zero...  2.8 us
  transfers between devices with their start and end apart: 6, of which 4 were waited for; matrix products, arithmetic and copies ran while one was open for 6% of the time, Pallas kernels for 0%

commit v1 on v0

v1 whole, which is shorter than its diff:
```python
import functools

import jax
import jax.numpy as jnp
from jax import lax
from jax.experimental import pallas as pl
from jax.experimental.pallas import tpu as pltpu
from jax.sharding import PartitionSpec as P

REACH = 4
ABSENT = 64


def purify_kernel(
    reach, flip_ref, table_ref, keep_ref, own_ref, other_ref, near_ref, cross_ref,
    stay_ref, leave_ref, own, other, near, cross, panel, square, result, sems
):
    rows, half, size = own.shape[0], own.shape[1], own.shape[2]
    width = rows + reach
    copies = []
    for n, (src, dst) in enumerate(
        [(own_ref, own), (other_ref, other), (near_ref, near), (cross_ref, cross)]
    ):
        copy = pltpu.make_async_copy(src, dst, sems.at[n])
        copy.start()
        copies.append(copy)
    panel[...] = jnp.zeros_like(panel)
    result[:, width * size :] = jnp.zeros((reach * size, size), result.dtype)
    flip = flip_ref[0]
    for copy in copies:
        copy.wait()

    for q in range(width):
        if q < reach:
            first, second = near, cross
            index = jnp.where(flip == 0, q, reach - 1 - q)
        else:
            first, second = own, other
            index = jnp.where(flip == 0, q - reach, width - 1 - q)
        for s in range(2 * half):
            place = pl.multiple_of(table_ref[q, s] * size, size)
            source = first if s < half else second
            panel[q * size : (q + 1) * size, pl.ds(place, size)] = source[index, s % half]

    def band_product(left, p):
        low = max(0, 2 * p - reach) * size
        high = min(width, 2 * p + 2 + reach) * size
        return jnp.dot(
            left[:, low:high],
            panel[low:high, 2 * p * size : (2 * p + 2) * size],
            preferred_element_type=jnp.float32,
        )

    left = panel.at[reach * size : 2 * reach * size]
    for p in range(width // 2):
        value = band_product(left, p)
        for i in range(reach):
            for k in (2 * p, 2 * p + 1):
                at = (slice(i * size, (i + 1) * size), slice(k * size, (k + 1) * size))
                if abs(i + reach - k) <= reach:
                    block = value[i * size : (i + 1) * size, (k - 2 * p) * size : (k - 2 * p + 1) * size]
                    square[at] = jnp.where(keep_ref[i, k] > 0, block, 0.0).astype(square.dtype)
                else:
                    square[at] = jnp.zeros((size, size), square.dtype)
    for p in range(width // 2):
        value = band_product(square, p)
        cols = slice(2 * p * size, (2 * p + 2) * size)
        result[:, cols] = (3.0 * square[:, cols].astype(jnp.float32) - 2.0 * value).astype(result.dtype)
    for i in range(reach):
        index = jnp.where(flip == 0, i, reach - 1 - i)
        for s in range(2 * half):
            place = pl.multiple_of(table_ref[i + reach, s] * size, size)
            target = stay_ref if s < half else leave_ref
            target[index, s % half] = result[i * size : (i + 1) * size, pl.ds(place, size)]


def purify(flip, table, keep, own, other, near, cross):
    rows, half, size = own.shape[:3]
    reach = near.shape[0]
    width = rows + reach
    smem = pl.BlockSpec(memory_space=pltpu.SMEM)
    anywhere = pl.BlockSpec(memory_space=pl.ANY)
    vmem = pl.BlockSpec(memory_space=pltpu.VMEM)
    out = jax.ShapeDtypeStruct((reach, half, size, size), own.dtype)
    return pl.pallas_call(
        functools.partial(purify_kernel, reach),
        out_shape=(out, out),
        in_specs=[smem] * 3 + [anywhere] * 4,
        out_specs=(vmem, vmem),
        scratch_shapes=[
            pltpu.VMEM(own.shape, own.dtype),
            pltpu.VMEM(own.shape, own.dtype),
            pltpu.VMEM(near.shape, own.dtype),
            pltpu.VMEM(near.shape, own.dtype),
            pltpu.VMEM((width * size, (width + 1) * size), own.dtype),
            pltpu.VMEM((reach * size, width * size), own.dtype),
            pltpu.VMEM((reach * size, (width + 1) * size), own.dtype),
            pltpu.SemaphoreType.DMA((4,)),
        ],
        compiler_params=pltpu.CompilerParams(vmem_limit_bytes=40 * 1024 * 1024),
        name="purify",
    )(flip, table, keep, own, other, near, cross)


def local(matrix, columns):
    local_rows, own_slots = matrix.shape[:2]
    reach = REACH
    cols = lax.axis_size("col")
    ring = lax.axis_size("row")
    total_rows = local_rows * ring
    row_start = lax.axis_index("row") * local_rows
    c = lax.axis_index("col")
    straight = c == 0
    width = local_rows + reach
    same = [(r * cols, (r + 1) % ring * cols) for r in range(ring)] + [
        (r * cols + 1, (r - 1) % ring * cols + 1) for r in range(ring)
    ]
    swap = [(r * cols + 1, (r + 1) % ring * cols) for r in range(ring)] + [
        (r * cols, (r - 1) % ring * cols + 1) for r in range(ring)
    ]
    axes = ("row", "col")
    start = jnp.where(straight, local_rows - reach, 0)
    other = lax.ppermute(matrix, "col", [(i, (i + 1) % cols) for i in range(cols)])
    near = lax.ppermute(lax.dynamic_slice_in_dim(matrix, start, reach, 0), axes, same)
    cross = lax.ppermute(
        lax.dynamic_slice_in_dim(matrix, local_rows - reach - start, reach, 0), axes, swap
    )
    row_ids = row_start + jnp.arange(local_rows, dtype=jnp.int32)[:, None]
    shift = (columns - row_ids + reach) % total_rows - reach
    shift = jnp.where(straight, shift, -shift)
    shift = jnp.where(columns >= 0, shift, ABSENT)
    halo_shift = lax.ppermute(lax.dynamic_slice_in_dim(shift, start, reach, 0), axes, same)
    both = jnp.concatenate(
        [jnp.where(straight, halo_shift, halo_shift[::-1]), jnp.where(straight, shift, shift[::-1])], axis=0
    )
    both = jnp.where(straight, both, jnp.roll(both, own_slots, axis=1))
    table = both + jnp.arange(width, dtype=jnp.int32)[:, None]
    table = jnp.where((table >= 0) & (table < width), table, width)
    keep = jnp.any(
        table[reach : 2 * reach, :, None] == jnp.arange(width, dtype=jnp.int32), axis=1
    ).astype(jnp.int32)
    flip = c.astype(jnp.int32).reshape(1)
    stay, leave = purify(flip, table, keep, matrix, other, near, cross)
    arrived = lax.ppermute(leave, "col", [(i, (i + 1) % cols) for i in range(cols)])
    return jnp.where(
        straight, jnp.concatenate([stay, arrived], axis=0), jnp.concatenate([arrived, stay], axis=0)
    )


def solution(mesh):
    placed = (P(("geom", "row"), "col", None, None), P("row", None))
    return jax.shard_map(
        local,
        mesh=mesh,
        in_specs=placed,
        out_specs=P(("geom", "row"), "col", None, None),
        check_vma=False,
    )
```

time: 123 us -> 42.7 us (0.35)
  waiting for transfers between devices: 60.9 us -> 21.2 us
  local copies, waits for them, and re-layouts: 19.4 us -> 3.1 us
  matrix products: 14 us -> 0 us
  between operations: 13.5 us -> 0.03 us
  Pallas kernels: 0 us -> 5.44 us
  other arithmetic: 4.05 us -> 1.56 us
    ppermute x4 -> x5, waiting for transfers between devices: 42.1 us -> 21.2 us  [the longest x1 10.3 us: local(): lax.ppermute(lax.dynamic_slice_in_dim(matrix, local_rows - reach - start,...]
    all_gather x2 -> x0, waiting for transfers between devices: 18 us -> none  [the longest x1 10.6 us: local(): square_whole = lax.all_gather(square, 'col', axis=1, tiled=True)]
    dot_general x2 -> x0, matrix products: 14 us -> none  [one_group(): jnp.einsum('ijab,ijsbc->isac', left_group, picked, preferred_element_type...]
    gather x2 -> x0, local copies, waits for them, and re-layouts: 11.3 us -> none  [the longest x1 10.7 us: one_group(): picked = flat_blocks[index_group]]
    pallas_call x0 -> x1, Pallas kernels: none -> 5.44 us  [purify(): pl.pallas_call(functools.partial(purify_kernel, reach), out_shape=(out, o...]
    slice x2 -> x1, local copies, waits for them, and re-layouts: 3.68 us -> 0.01 us  [local(): table[reach:2 * reach, :, None] == jnp.arange(width, dtype=jnp.int32)]
    concatenate x1 -> x0, local copies, waits for them, and re-layouts: 2.8 us -> none  [local(): jnp.concatenate([panel_rows.reshape(-1, block_size, block_size), jnp.zero...]
    dynamic_slice x0 -> x2, local copies, waits for them, and re-layouts: none -> 2.37 us  [the longest x1 2.36 us: local(): lax.dynamic_slice_in_dim(matrix, local_rows - reach - start, reach, 0)]
  transfers between devices with their start and end apart: 6 -> 5, of which waited for: 4 -> 3; matrix products, arithmetic and copies ran while one was open for 6% -> 7% of each run, Pallas kernels for 0% -> 0%
where the time goes in v1:
time: 42.7 us; the launch traced here: 42.6 us
  waiting for transfers between devices  21.2 us (50%)
  starting transfers between devices  11.3 us (26%)
  Pallas kernels  5.44 us (13%)
  local copies, waits for them, and re-layouts  3.1 us (7%)
  other arithmetic  1.56 us (4%)
    ppermute x1, waiting for transfers between devices, local(): lax.ppermute(lax.dynamic_slice_in_dim(matrix, local_rows - reach - start,...  10.3 us
    ppermute x1, waiting for transfers between devices, local(): lax.ppermute(lax.dynamic_slice_in_dim(matrix, start, reach, 0), axes, same)  9.32 us
    pallas_call x1, Pallas kernels, purify(): pl.pallas_call(functools.partial(purify_kernel, reach), out_shape=(out, o...  5.44 us
    ppermute x1, starting transfers between devices, local(): lax.ppermute(lax.dynamic_slice_in_dim(matrix, local_rows - reach - start,...  3.38 us
    ppermute x1, starting transfers between devices, local(): lax.ppermute(leave, 'col', [(i, (i + 1) % cols) for i in range(cols)])  3.35 us
    ppermute x1, starting transfers between devices, local(): lax.ppermute(lax.dynamic_slice_in_dim(shift, start, reach, 0), axes, same)  2.57 us
    dynamic_slice x1, local copies, waits for them, and re-layouts, local(): lax.dynamic_slice_in_dim(matrix, local_rows - reach - start, reach, 0)  2.36 us
    ppermute x1, waiting for transfers between devices, local(): lax.ppermute(leave, 'col', [(i, (i + 1) % cols) for i in range(cols)])  1.54 us
  transfers between devices with their start and end apart: 5, of which 3 were waited for; matrix products, arithmetic and copies ran while one was open for 7% of the time, Pallas kernels for 0%

profile of v1, /device:TPU:0, one launch (start us, length us, event | category | flops | bytes accessed | tf_op | source)
XLA Modules:
  0.0 42.6 jit_solution(13444523371495561913)
XLA Ops:
  0.0 0.5 %collective-permute-start.1 = (bf16[8,4,128,128]{3,2,1,0:T(8,128)(2,1)}, bf16[8,4,128,128]{3,2,1,0:T(8,128)(2,1)S(1)}, u32[]{:S(2)}, u32[]{:S(2)}) collective-permute-start(bf16[8,4,128,128]{3,2,1,0:T(8,128)(2,1)} %own_ref.1), channel_id=1, source_target_pairs={{0,1},{1,0},{2,3},{3,2},{4,5},{5,4},{6,7},{7,6},{8,9},{9,8},{10,11... | collective-permute-start | bytes 3145736 | tf_op jit(solution)/shard_map/ppermute | solution.py:123
  0.5 0.0 copy-start.1
  0.5 0.7 %copy-done.1 = s32[8,8]{1,0:T(8,128)S(1)} copy-done((s32[8,8]{1,0:T(8,128)S(1)}, s32[8,8]{1,0:T(8,128)}, u32[]{:S(2)}) %copy-start.1) | copy-done | bytes 280
  1.1 0.1 fusion.7
  1.2 2.6 %collective-permute-start = (s32[4,8]{1,0:T(4,128)S(1)}, s32[4,8]{1,0:T(4,128)S(1)}, u32[]{:S(2)}, u32[]{:S(2)}) collective-permute-start(s32[4,8]{1,0:T(4,128)S(1)} %constant_dynamic-slice_fusion.2), channel_id=1, source_target_pairs={{0,2},{2,4},{4,6},{6,8},{8,10},{10,12},{12,14},{14,0},{1,15},{3,1}... | collective-permute-start | bytes 392 | tf_op jit(solution)/shard_map/ppermute | solution.py:132
  3.8 0.0 copy-start
  3.8 2.4 %constant_dynamic-slice_fusion = (bf16[4,4,128,128]{3,2,1,0:T(8,128)(2,1)}, bf16[4,4,128,128]{3,2,1,0:T(8,128)(2,1)}) fusion(bf16[8,4,128,128]{3,2,1,0:T(8,128)(2,1)} %own_ref.1, s32[]{:T(128)S(6)} %select_n.72, s32[]{:T(128)S(6)} %select_n.67), kind=kLoop, calls=%fused_computation.22 | loop fusion | bytes 2097160 | tf_op jit(solution)/shard_map/dynamic_slice | solution.py:126
  6.2 3.4 %collective-permute-start.3 = (bf16[4,4,128,128]{3,2,1,0:T(8,128)(2,1)}, bf16[4,4,128,128]{3,2,1,0:T(8,128)(2,1)S(1)}, u32[]{:S(2)}, u32[]{:S(2)}) collective-permute-start(bf16[4,4,128,128]{3,2,1,0:T(8,128)(2,1)} %get-tuple-element.9), channel_id=1, source_target_pairs={{1,2},{3,4},{5,6},{7,8},{9,10},{11,12},{13,14},{15,0},{0,15},{2,1}... | collective-permute-start | bytes 1572872 | tf_op jit(solution)/shard_map/ppermute | solution.py:125
  9.5 1.5 %collective-permute-start.2 = (bf16[4,4,128,128]{3,2,1,0:T(8,128)(2,1)}, bf16[4,4,128,128]{3,2,1,0:T(8,128)(2,1)S(1)}, u32[]{:S(2)}, u32[]{:S(2)}) collective-permute-start(bf16[4,4,128,128]{3,2,1,0:T(8,128)(2,1)} %get-tuple-element.10), channel_id=1, source_target_pairs={{0,2},{2,4},{4,6},{6,8},{8,10},{10,12},{12,14},{14,0},{1,15},{3,1}... | collective-permute-start | bytes 1572872 | tf_op jit(solution)/shard_map/ppermute | solution.py:124
  11.1 0.1 broadcast_select_fusion
  11.2 0.0 collective-permute-done
  11.2 0.1 fusion.1
  11.3 0.1 and_select_fusion.table_ref
  11.4 0.1 fusion
  11.5 10.3 %collective-permute-done.3.cross_ref = bf16[4,4,128,128]{3,2,1,0:T(8,128)(2,1)S(1)} collective-permute-done((bf16[4,4,128,128]{3,2,1,0:T(8,128)(2,1)}, bf16[4,4,128,128]{3,2,1,0:T(8,128)(2,1)S(1)}, u32[]{:S(2)}, u32[]{:S(2)}) %collective-permute-start.3) | collective-permute-done | bytes 524320 | tf_op jit(solution)/shard_map/ppermute | solution.py:125
  21.8 9.3 %collective-permute-done.2.near_ref = bf16[4,4,128,128]{3,2,1,0:T(8,128)(2,1)S(1)} collective-permute-done((bf16[4,4,128,128]{3,2,1,0:T(8,128)(2,1)}, bf16[4,4,128,128]{3,2,1,0:T(8,128)(2,1)S(1)}, u32[]{:S(2)}, u32[]{:S(2)}) %collective-permute-start.2) | collective-permute-done | bytes 524320 | tf_op jit(solution)/shard_map/ppermute | solution.py:124
  31.1 0.0 collective-permute-done.1.other_ref
  31.1 0.0 copy-done
  31.1 5.4 %purify.1 = (bf16[4,4,128,128]{3,2,1,0:T(8,128)(2,1)S(1)}, bf16[4,4,128,128]{3,2,1,0:T(8,128)(2,1)S(1)}) custom-call(s32[1]{0:T(128)} %bitcast.flip_ref, s32[12,8]{1,0:T(8,128)S(1)} %and_select_fusion.table_ref, s32[4,12]{1,0:T(4,128)S(1)} %convert_element_type.3.keep_ref, bf16[8,4,128,128]{3,2,1,0:T(8,128)(2,1)S(1)} %copy-done, ...), custom_call_target="tpu_custom_call" | custom-call | tf_op jit(solution)/shard_map/purify/pallas_call | solution.py:85
  36.5 3.4 %collective-permute-start.4 = (bf16[4,4,128,128]{3,2,1,0:T(8,128)(2,1)S(1)}, bf16[4,4,128,128]{3,2,1,0:T(8,128)(2,1)S(1)}, u32[]{:S(2)}, u32[]{:S(2)}) collective-permute-start(bf16[4,4,128,128]{3,2,1,0:T(8,128)(2,1)S(1)} %get-tuple-element.8), channel_id=1, source_target_pairs={{0,1},{1,0},{2,3},{3,2},{4,5},{5,4},{6,7},{7,6},{8,9},{9,8},{10,11... | collective-permute-start | bytes 1572872 | tf_op jit(solution)/shard_map/ppermute | solution.py:144
  39.9 1.5 %collective-permute-done.4 = bf16[4,4,128,128]{3,2,1,0:T(8,128)(2,1)S(1)} collective-permute-done((bf16[4,4,128,128]{3,2,1,0:T(8,128)(2,1)S(1)}, bf16[4,4,128,128]{3,2,1,0:T(8,128)(2,1)S(1)}, u32[]{:S(2)}, u32[]{:S(2)}) %collective-permute-start.4) | collective-permute-done | bytes 524320 | tf_op jit(solution)/shard_map/ppermute | solution.py:144
  41.4 1.1 %maximum_select_fusion = bf16[8,4,128,128]{3,2,1,0:T(8,128)(2,1)} fusion(bf16[4,4,128,128]{3,2,1,0:T(8,128)(2,1)S(1)} %collective-permute-done.4, bf16[4,4,128,128]{3,2,1,0:T(8,128)(2,1)S(1)} %get-tuple-element.7, pred[]{:T(512)S(6)} %eq.18), kind=kLoop, calls=%fused_computation | loop fusion | flops 1572864 | bytes 2097153 | tf_op jit(solution)/shard_map/jit(_where)/select_n | solution.py:145
  (7 shorter events, 0.1 us)
Async XLA Ops:
  0.0 31.1 %collective-permute-start.1 = (bf16[8,4,128,128]{3,2,1,0:T(8,128)(2,1)}, bf16[8,4,128,128]{3,2,1,0:T(8,128)(2,1)S(1)}, u32[]{:S(2)}, u32[]{:S(2)}) collective-permute-start(bf16[8,4,128,128]{3,2,1,0:T(8,128)(2,1)} %own_ref.1), channel_id=1, source_target_pairs={{0,1},{1,0},{2,3},{3,2},{4,5},{5,4},{6,7},{7,6},{8,9},{9,8},{10,11... | collective-permute-start | bytes 3145736 | tf_op jit(solution)/shard_map/ppermute | solution.py:123
  0.5 0.7 %copy-start.1 = (s32[8,8]{1,0:T(8,128)S(1)}, s32[8,8]{1,0:T(8,128)}, u32[]{:S(2)}) copy-start(s32[8,8]{1,0:T(8,128)} %param.3) | copy-start | bytes 772
  1.2 9.9 %collective-permute-start = (s32[4,8]{1,0:T(4,128)S(1)}, s32[4,8]{1,0:T(4,128)S(1)}, u32[]{:S(2)}, u32[]{:S(2)}) collective-permute-start(s32[4,8]{1,0:T(4,128)S(1)} %constant_dynamic-slice_fusion.2), channel_id=1, source_target_pairs={{0,2},{2,4},{4,6},{6,8},{8,10},{10,12},{12,14},{14,0},{1,15},{3,1}... | collective-permute-start | bytes 392 | tf_op jit(solution)/shard_map/ppermute | solution.py:132
  3.8 27.3 %copy-start = (bf16[8,4,128,128]{3,2,1,0:T(8,128)(2,1)S(1)}, bf16[8,4,128,128]{3,2,1,0:T(8,128)(2,1)}, u32[]{:S(2)}) copy-start(bf16[8,4,128,128]{3,2,1,0:T(8,128)(2,1)} %own_ref.1) | copy-start | bytes 3145732
  6.2 15.6 %collective-permute-start.3 = (bf16[4,4,128,128]{3,2,1,0:T(8,128)(2,1)}, bf16[4,4,128,128]{3,2,1,0:T(8,128)(2,1)S(1)}, u32[]{:S(2)}, u32[]{:S(2)}) collective-permute-start(bf16[4,4,128,128]{3,2,1,0:T(8,128)(2,1)} %get-tuple-element.9), channel_id=1, source_target_pairs={{1,2},{3,4},{5,6},{7,8},{9,10},{11,12},{13,14},{15,0},{0,15},{2,1}... | collective-permute-start | bytes 1572872 | tf_op jit(solution)/shard_map/ppermute | solution.py:125
  9.5 21.5 %collective-permute-start.2 = (bf16[4,4,128,128]{3,2,1,0:T(8,128)(2,1)}, bf16[4,4,128,128]{3,2,1,0:T(8,128)(2,1)S(1)}, u32[]{:S(2)}, u32[]{:S(2)}) collective-permute-start(bf16[4,4,128,128]{3,2,1,0:T(8,128)(2,1)} %get-tuple-element.10), channel_id=1, source_target_pairs={{0,2},{2,4},{4,6},{6,8},{8,10},{10,12},{12,14},{14,0},{1,15},{3,1}... | collective-permute-start | bytes 1572872 | tf_op jit(solution)/shard_map/ppermute | solution.py:124
  36.5 4.9 %collective-permute-start.4 = (bf16[4,4,128,128]{3,2,1,0:T(8,128)(2,1)S(1)}, bf16[4,4,128,128]{3,2,1,0:T(8,128)(2,1)S(1)}, u32[]{:S(2)}, u32[]{:S(2)}) collective-permute-start(bf16[4,4,128,128]{3,2,1,0:T(8,128)(2,1)S(1)} %get-tuple-element.8), channel_id=1, source_target_pairs={{0,1},{1,0},{2,3},{3,2},{4,5},{5,4},{6,7},{7,6},{8,9},{9,8},{10,11... | collective-permute-start | bytes 1572872 | tf_op jit(solution)/shard_map/ppermute | solution.py:144

commit v2 on v1

v2 whole, which is shorter than its diff:
```python
import functools

import jax
import jax.numpy as jnp
from jax import lax
from jax.experimental import pallas as pl
from jax.experimental.pallas import tpu as pltpu
from jax.sharding import PartitionSpec as P

REACH = 4
ABSENT = 64
MIB = 1024 * 1024

SMEM = pl.BlockSpec(memory_space=pltpu.SMEM)
VMEM = pl.BlockSpec(memory_space=pltpu.VMEM)


def blocks(first, last, size):
    return slice(first * size, last * size)


def place_blocks(panel, base, q, index, table_ref, row, first, second):
    half, size = first.shape[1], first.shape[2]
    for s in range(2 * half):
        place = pl.multiple_of(table_ref[row, s] * size, size)
        source = first if s < half else second
        panel[blocks(q - base, q - base + 1, size), pl.ds(place, size)] = source[index, s % half]


def pack_kernel(far, reach, flip_ref, table_ref, own_ref, other_ref, out_ref):
    rows, half = own_ref.shape[:2]
    out_ref[...] = jnp.zeros_like(out_ref)
    for f in range(far):
        index = jnp.where(flip_ref[0] == 0, reach + f, rows - 1 - reach - f)
        for s in range(2 * half):
            place = table_ref[f, s]
            source = own_ref if s < half else other_ref

            @pl.when(place < out_ref.shape[0])
            def _(place=place, source=source, index=index, s=s):
                out_ref[place] = source[index, s % half]


def near_kernel(
    reach, far, flip_ref, table_ref, keep_ref, own_ref, other_ref, near_ref, cross_ref,
    stay_ref, leave_ref, part_ref, high_ref, cube_ref, lower_ref, panel, square, result
):
    rows, half, size = own_ref.shape[0], own_ref.shape[1], own_ref.shape[2]
    width = rows + reach
    low_cols = reach + far
    far_cols = 2 * reach + far
    near = reach - far
    flip = flip_ref[0]
    panel[...] = jnp.zeros_like(panel)
    result[:, blocks(width, width + 1, size)] = jnp.zeros((near * size, size), result.dtype)
    for q in range(far, width):
        if q < reach:
            index = jnp.where(flip == 0, q - far, reach - 1 - q)
            place_blocks(panel, far, q, index, table_ref, q, near_ref, cross_ref)
        else:
            index = jnp.where(flip == 0, q - reach, width - 1 - q)
            place_blocks(panel, far, q, index, table_ref, q, own_ref, other_ref)

    def band_product(left, p):
        low = max(far, 2 * p - reach)
        high = min(width, 2 * p + 2 + reach)
        return jnp.dot(
            left[:, blocks(low, high, size)],
            panel[blocks(low - far, high - far, size), blocks(2 * p, 2 * p + 2, size)],
            preferred_element_type=jnp.float32,
        )

    left = panel.at[blocks(reach - far, 2 * reach - far, size)]
    for p in range(width // 2):
        value = band_product(left, p)
        for i in range(reach):
            for k in (2 * p, 2 * p + 1):
                block = value[blocks(i, i + 1, size), blocks(k - 2 * p, k - 2 * p + 1, size)]
                at = (blocks(i, i + 1, size), blocks(k, k + 1, size))
                if i < far and k < low_cols:
                    part_ref[at] = block
                    square[at] = jnp.zeros((size, size), square.dtype)
                elif abs(i + reach - k) <= reach:
                    square[at] = jnp.where(keep_ref[i, k] > 0, block, 0.0).astype(square.dtype)
                else:
                    square[at] = jnp.zeros((size, size), square.dtype)
    for p in range(width // 2):
        value = band_product(square, p)
        cols = blocks(2 * p, 2 * p + 2, size)
        if 2 * p < far_cols:
            cube_ref[:, cols] = value[: far * size]
        result[:, cols] = (
            3.0 * square[far * size :, cols].astype(jnp.float32) - 2.0 * value[far * size :]
        ).astype(result.dtype)
    high_ref[...] = square[: far * size, blocks(low_cols, far_cols, size)]
    lower_ref[...] = panel[blocks(0, low_cols - far, size), blocks(0, far_cols, size)]
    for i in range(near):
        index = jnp.where(flip == 0, i, near - 1 - i)
        for s in range(2 * half):
            place = pl.multiple_of(table_ref[i + reach + far, s] * size, size)
            target = stay_ref if s < half else leave_ref
            target[index, s % half] = result[blocks(i, i + 1, size), pl.ds(place, size)]


def far_kernel(
    reach, far, flip_ref, table_ref, keep_ref, far_ref, part_ref, high_ref, cube_ref, lower_ref,
    stay_ref, leave_ref, panel, square, result
):
    half, size = stay_ref.shape[1], stay_ref.shape[2]
    low_cols = reach + far
    far_cols = 2 * reach + far
    at = 0
    for f in range(far):
        for k in range(low_cols):
            here = (blocks(f, f + 1, size), blocks(k, k + 1, size))
            if k <= f + reach:
                panel[here] = far_ref[at]
                at += 1
            else:
                panel[here] = jnp.zeros((size, size), panel.dtype)
    result[:, blocks(far_cols, far_cols + 1, size)] = jnp.zeros((far * size, size), result.dtype)
    left = lower_ref[blocks(reach - far, reach, size), blocks(0, far, size)]
    for p in range(low_cols // 2):
        cols = blocks(2 * p, 2 * p + 2, size)
        value = part_ref[:, cols] + jnp.dot(left, panel[:, cols], preferred_element_type=jnp.float32)
        for i in range(far):
            for k in (2 * p, 2 * p + 1):
                block = value[blocks(i, i + 1, size), blocks(k - 2 * p, k - 2 * p + 1, size)]
                here = (blocks(i, i + 1, size), blocks(k, k + 1, size))
                if abs(i + reach - k) <= reach:
                    square[here] = jnp.where(keep_ref[i, k] > 0, block, 0.0).astype(square.dtype)
                else:
                    square[here] = jnp.zeros((size, size), square.dtype)
    for p in range(far_cols // 2):
        cols = blocks(2 * p, 2 * p + 2, size)
        value = cube_ref[:, cols] + jnp.dot(
            square[:, blocks(far, low_cols, size)], lower_ref[:, cols], preferred_element_type=jnp.float32
        )
        if 2 * p < low_cols:
            value = value + jnp.dot(
                square[:, blocks(0, far, size)], panel[:, cols], preferred_element_type=jnp.float32
            )
            kept = square[:, cols]
        else:
            kept = high_ref[:, blocks(2 * p - low_cols, 2 * p + 2 - low_cols, size)]
        result[:, cols] = (3.0 * kept.astype(jnp.float32) - 2.0 * value).astype(result.dtype)
    for i in range(far):
        index = jnp.where(flip_ref[0] == 0, i, far - 1 - i)
        for s in range(2 * half):
            place = pl.multiple_of(table_ref[i, s] * size, size)
            target = stay_ref if s < half else leave_ref
            target[index, s % half] = result[blocks(i, i + 1, size), pl.ds(place, size)]


def local(matrix, columns):
    local_rows, own_slots, size = matrix.shape[:3]
    dtype = matrix.dtype
    reach = REACH
    far = reach // 2
    near = reach - far
    cols = lax.axis_size("col")
    ring = lax.axis_size("row")
    total_rows = local_rows * ring
    row_start = lax.axis_index("row") * local_rows
    c = lax.axis_index("col")
    straight = c == 0
    flip = c.astype(jnp.int32).reshape(1)
    width = local_rows + reach
    same = [(r * cols, (r + 1) % ring * cols) for r in range(ring)] + [
        (r * cols + 1, (r - 1) % ring * cols + 1) for r in range(ring)
    ]
    swap = [(r * cols + 1, (r + 1) % ring * cols) for r in range(ring)] + [
        (r * cols, (r - 1) % ring * cols + 1) for r in range(ring)
    ]
    beside = [(i, (i + 1) % cols) for i in range(cols)]
    axes = ("row", "col")
    start = jnp.where(straight, local_rows - near, 0)
    other = lax.ppermute(matrix, "col", beside)
    near_rows = lax.ppermute(lax.dynamic_slice_in_dim(matrix, start, near, 0), axes, same)
    cross_rows = lax.ppermute(
        lax.dynamic_slice_in_dim(matrix, local_rows - near - start, near, 0), axes, swap
    )
    row_ids = row_start + jnp.arange(local_rows, dtype=jnp.int32)[:, None]
    shift = (columns - row_ids + reach) % total_rows - reach
    shift = jnp.where(straight, shift, -shift)
    shift = jnp.where(columns >= 0, shift, ABSENT)

    def arrange(rows):
        rows = jnp.where(straight, rows, rows[::-1])
        return jnp.where(straight, rows, jnp.roll(rows, own_slots, axis=1))

    own_shift = arrange(shift)
    count = [reach + 1 + f for f in range(far)]
    first = jnp.array([sum(count[:f]) for f in range(far)], jnp.int32)[:, None]
    f_ids = jnp.arange(far, dtype=jnp.int32)[:, None]
    sent = own_shift[reach : reach + far] + f_ids
    pack_table = jnp.where((sent >= 0) & (sent <= reach + f_ids), first + sent, ABSENT)
    packed = pl.pallas_call(
        functools.partial(pack_kernel, far, reach),
        out_shape=jax.ShapeDtypeStruct((sum(count), size, size), dtype),
        in_specs=[SMEM, SMEM, VMEM, VMEM],
        out_specs=VMEM,
        name="pack",
    )(flip, pack_table, matrix, other)
    far_blocks = lax.ppermute(packed, axes, same)

    halo_shift = arrange(lax.ppermute(lax.dynamic_slice_in_dim(shift, start, near, 0), axes, same))
    table = jnp.concatenate([jnp.full((far, 2 * own_slots), ABSENT, jnp.int32), halo_shift, own_shift], axis=0)
    table = table + jnp.arange(width, dtype=jnp.int32)[:, None]
    table = jnp.where((table >= 0) & (table < width), table, width)
    own_table = table[reach : 2 * reach]
    keep = jnp.any(own_table[:, :, None] == jnp.arange(width, dtype=jnp.int32), axis=1).astype(jnp.int32)

    low_cols = reach + far
    far_cols = 2 * reach + far
    rows_out = jax.ShapeDtypeStruct((near, own_slots, size, size), dtype)
    stay_near, leave_near, part, high, cube, lower = pl.pallas_call(
        functools.partial(near_kernel, reach, far),
        out_shape=(
            rows_out,
            rows_out,
            jax.ShapeDtypeStruct((far * size, low_cols * size), jnp.float32),
            jax.ShapeDtypeStruct((far * size, (far_cols - low_cols) * size), dtype),
            jax.ShapeDtypeStruct((far * size, far_cols * size), jnp.float32),
            jax.ShapeDtypeStruct(((low_cols - far) * size, far_cols * size), dtype),
        ),
        in_specs=[SMEM] * 3 + [VMEM] * 4,
        out_specs=(VMEM,) * 6,
        scratch_shapes=[
            pltpu.VMEM(((width - far) * size, (width + 1) * size), dtype),
            pltpu.VMEM((reach * size, width * size), dtype),
            pltpu.VMEM((near * size, (width + 1) * size), dtype),
        ],
        compiler_params=pltpu.CompilerParams(vmem_limit_bytes=24 * MIB),
        name="near",
    )(flip, table, keep, matrix, other, near_rows, cross_rows)
    arrived_near = lax.ppermute(leave_near, "col", beside)

    far_table = own_table[:far]
    far_table = jnp.where(far_table < width, far_table, far_cols)
    far_out = jax.ShapeDtypeStruct((far, own_slots, size, size), dtype)
    stay_far, leave_far = pl.pallas_call(
        functools.partial(far_kernel, reach, far),
        out_shape=(far_out, far_out),
        in_specs=[SMEM] * 3 + [VMEM] * 5,
        out_specs=(VMEM,) * 2,
        scratch_shapes=[
            pltpu.VMEM((far * size, low_cols * size), dtype),
            pltpu.VMEM((far * size, low_cols * size), dtype),
            pltpu.VMEM((far * size, (far_cols + 1) * size), dtype),
        ],
        compiler_params=pltpu.CompilerParams(vmem_limit_bytes=24 * MIB),
        name="far",
    )(flip, far_table, keep, far_blocks, part, high, cube, lower)
    arrived_far = lax.ppermute(leave_far, "col", beside)
    return jnp.where(
        straight,
        jnp.concatenate([stay_far, stay_near, arrived_near, arrived_far], axis=0),
        jnp.concatenate([arrived_far, arrived_near, stay_near, stay_far], axis=0),
    )


def solution(mesh):
    placed = (P(("geom", "row"), "col", None, None), P("row", None))
    return jax.shard_map(
        local,
        mesh=mesh,
        in_specs=placed,
        out_specs=P(("geom", "row"), "col", None, None),
        check_vma=False,
    )
```

time: 42.7 us -> 37.1 us (0.87)
  waiting for transfers between devices: 21.2 us -> 9.33 us
  Pallas kernels: 5.44 us -> 8.77 us
  other arithmetic: 1.56 us -> 3.71 us
    ppermute x5 -> x7, waiting for transfers between devices: 21.2 us -> 9.33 us  [the longest x1 7.81 us: local(): lax.ppermute(lax.dynamic_slice_in_dim(matrix, start, near, 0), axes, same)]
    pallas_call x1 -> x3, Pallas kernels: 5.44 us -> 8.77 us  [the longest x1 4.69 us: local(): pl.pallas_call(functools.partial(near_kernel, reach, far), out_shape=(row...]
    select_n x3 -> x7, other arithmetic: 1.22 us -> 2.82 us  [the longest x1 1.23 us: local(): jnp.where(straight, jnp.concatenate([stay_far, stay_near, arrived_near, a...]
    unnamed x4 -> x6, local copies, waits for them, and re-layouts: 0.69 us -> 2.2 us
    dynamic_slice x2, local copies, waits for them, and re-layouts: 2.37 us -> 1.07 us  [the longest x1 1.06 us: local(): lax.dynamic_slice_in_dim(matrix, local_rows - near - start, near, 0)]
    select_n x1, other arithmetic: 0.08 us -> 0.77 us  [local(): shift = jnp.where(columns >= 0, shift, ABSENT)]
    ppermute x5 -> x7, starting transfers between devices: 11.3 us -> 11.5 us  [the longest x1 3.4 us: local(): arrived_near = lax.ppermute(leave_near, 'col', beside)]
  transfers between devices with their start and end apart: 5 -> 7, of which waited for: 3 -> 2; matrix products, arithmetic and copies ran while one was open for 7% -> 8% of each run, Pallas kernels for 0% -> 24%
where the time goes in v2:
time: 37.1 us; the launch traced here: 36.9 us
  starting transfers between devices  11.5 us (31%)
  waiting for transfers between devices  9.33 us (25%)
  Pallas kernels  8.77 us (24%)
  other arithmetic  3.71 us (10%)
  local copies, waits for them, and re-layouts  3.47 us (9%)
    ppermute x1, waiting for transfers between devices, local(): lax.ppermute(lax.dynamic_slice_in_dim(matrix, start, near, 0), axes, same)  7.81 us
    pallas_call x1, Pallas kernels, local(): pl.pallas_call(functools.partial(near_kernel, reach, far), out_shape=(row...  4.69 us
    ppermute x1, starting transfers between devices, local(): arrived_near = lax.ppermute(leave_near, 'col', beside)  3.4 us
    ppermute x1, starting transfers between devices, local(): lax.ppermute(lax.dynamic_slice_in_dim(shift, start, near, 0), axes, same)  3.02 us
    ppermute x1, starting transfers between devices, local(): other = lax.ppermute(matrix, 'col', beside)  2.59 us
    pallas_call x1, Pallas kernels, local(): pl.pallas_call(functools.partial(pack_kernel, far, reach), out_shape=jax....  2.46 us
    ppermute x1, starting transfers between devices, local(): lax.ppermute(lax.dynamic_slice_in_dim(matrix, local_rows - near - start,...  2.29 us
    unnamed x6, local copies, waits for them, and re-layouts  2.2 us
  transfers between devices with their start and end apart: 7, of which 2 were waited for; matrix products, arithmetic and copies ran while one was open for 8% of the time, Pallas kernels for 24%

profile of v2, /device:TPU:0, one launch (start us, length us, event | category | flops | bytes accessed | tf_op | source)
XLA Modules:
  0.0 36.9 jit_solution(12730679750428813170)
XLA Ops:
  0.0 0.8 %fusion.3 = s32[8,8]{1,0:T(8,128)S(1)} fusion(s32[8,8]{1,0:T(8,128)} %param.4, s32[8]{0:T(128)S(1)} %iota_add_fusion.1, pred[]{:T(512)S(6)} %eq.18), kind=kLoop, calls=%fused_computation.11 | loop fusion | flops 1152 | bytes 545 | tf_op jit(solution)/shard_map/jit(_where)/select_n | solution.py:186
  0.8 3.0 %collective-permute-start = (s32[2,8]{1,0:T(2,128)S(1)}, s32[2,8]{1,0:T(2,128)S(1)}, u32[]{:S(2)}, u32[]{:S(2)}) collective-permute-start(s32[2,8]{1,0:T(2,128)S(1)} %constant_dynamic-slice_fusion.2), channel_id=1, source_target_pairs={{0,2},{2,4},{4,6},{6,8},{8,10},{10,12},{12,14},{14,0},{1,15},{3,1}... | collective-permute-start | bytes 200 | tf_op jit(solution)/shard_map/ppermute | solution.py:207
  3.8 2.6 %collective-permute-start.1 = (bf16[8,4,128,128]{3,2,1,0:T(8,128)(2,1)}, bf16[8,4,128,128]{3,2,1,0:T(8,128)(2,1)S(1)}, u32[]{:S(2)}, u32[]{:S(2)}) collective-permute-start(bf16[8,4,128,128]{3,2,1,0:T(8,128)(2,1)} %own_ref.3), channel_id=1, source_target_pairs={{0,1},{1,0},{2,3},{3,2},{4,5},{5,4},{6,7},{7,6},{8,9},{9,8},{10,11... | collective-permute-start | bytes 3145736 | tf_op jit(solution)/shard_map/ppermute | solution.py:178
  6.4 1.1 %constant_dynamic-slice_fusion = (bf16[2,4,128,128]{3,2,1,0:T(8,128)(2,1)S(1)}, bf16[2,4,128,128]{3,2,1,0:T(8,128)(2,1)S(1)}) fusion(bf16[8,4,128,128]{3,2,1,0:T(8,128)(2,1)} %own_ref.3, s32[]{:T(128)S(6)} %select_n.81, s32[]{:T(128)S(6)} %select_n.73), kind=kLoop, calls=%fused_computation.18 | loop fusion | bytes 1048584 | tf_op jit(solution)/shard_map/dynamic_slice | solution.py:181
  7.5 0.1 collective-permute-start.3
  7.5 2.3 %collective-permute-start.4 = (bf16[2,4,128,128]{3,2,1,0:T(8,128)(2,1)S(1)}, bf16[2,4,128,128]{3,2,1,0:T(8,128)(2,1)S(1)}, u32[]{:S(2)}, u32[]{:S(2)}) collective-permute-start(bf16[2,4,128,128]{3,2,1,0:T(8,128)(2,1)S(1)} %get-tuple-element.21), channel_id=1, source_target_pairs={{1,2},{3,4},{5,6},{7,8},{9,10},{11,12},{13,14},{15,0},{0,15},{2,1}... | collective-permute-start | bytes 786440 | tf_op jit(solution)/shard_map/ppermute | solution.py:180
  9.8 0.8 %broadcast_select_fusion = s32[8,8]{1,0:T(8,128)S(1)} fusion(s32[8,8]{1,0:T(8,128)S(1)} %rev.7, pred[]{:T(512)S(6)} %eq.18, s32[8,8]{1,0:T(8,128)} %param.4, s32[8]{0:T(128)S(1)} %iota_add_fusion.1), kind=kLoop, calls=%fused_computation.15 | loop fusion | flops 1216 | bytes 801 | tf_op jit(solution)/shard_map/jit(_where)/select_n | solution.py:189
  10.6 0.1 fusion.4
  10.7 0.1 add_select_fusion.1
  10.8 0.7 %and_select_fusion.1.table_ref = s32[2,8]{1,0:T(2,128)} fusion(s32[8,8]{1,0:T(8,128)S(1)} %add_select_fusion.1, s32[2]{0:T(128)S(1)} %get-tuple-element.28, s32[2]{0:T(128)S(1)} %get-tuple-element.27), kind=kLoop, calls=%fused_computation.14 | loop fusion | flops 96 | bytes 144 | tf_op jit(solution)/shard_map/jit(_where)/select_n | solution.py:197
  11.5 0.1 fusion.5
  11.5 0.1 add_select_fusion.2
  11.6 1.0 %copy-done.1 = bf16[8,4,128,128]{3,2,1,0:T(8,128)(2,1)} copy-done((bf16[8,4,128,128]{3,2,1,0:T(8,128)(2,1)}, bf16[8,4,128,128]{3,2,1,0:T(8,128)(2,1)S(1)}, u32[]{:S(2)}) %copy-start.1) | copy-done | bytes 1048600
  12.6 2.5 %pack.1 = bf16[11,128,128]{2,1,0:T(8,128)(2,1)} custom-call(s32[1]{0:T(128)} %bitcast.flip_ref, s32[2,8]{1,0:T(2,128)} %and_select_fusion.1.table_ref, bf16[8,4,128,128]{3,2,1,0:T(8,128)(2,1)} %own_ref.3, bf16[8,4,128,128]{3,2,1,0:T(8,128)(2,1)} %copy-done.1), custom_call_target="tpu_custom_call" | custom-call | tf_op jit(solution)/shard_map/pack/pallas_call | solution.py:198
  15.0 0.1 collective-permute-start.2
  15.2 0.1 fusion
  15.3 7.8 %collective-permute-done.3.near_ref = bf16[2,4,128,128]{3,2,1,0:T(8,128)(2,1)S(1)} collective-permute-done((bf16[2,4,128,128]{3,2,1,0:T(8,128)(2,1)S(1)}, bf16[2,4,128,128]{3,2,1,0:T(8,128)(2,1)S(1)}, u32[]{:S(2)}, u32[]{:S(2)}) %collective-permute-start.3) | collective-permute-done | bytes 262176 | tf_op jit(solution)/shard_map/ppermute | solution.py:179
  23.1 1.2 %copy-done.2 = bf16[8,4,128,128]{3,2,1,0:T(8,128)(2,1)S(1)} copy-done((bf16[8,4,128,128]{3,2,1,0:T(8,128)(2,1)S(1)}, bf16[8,4,128,128]{3,2,1,0:T(8,128)(2,1)}, u32[]{:S(2)}) %copy-start.2) | copy-done | bytes 1048600
  24.3 4.7 %near.1 = (bf16[2,4,128,128]{3,2,1,0:T(8,128)(2,1)S(1)}, bf16[2,4,128,128]{3,2,1,0:T(8,128)(2,1)S(1)}, f32[256,768]{1,0:T(8,128)S(1)}, bf16[256,512]{1,0:T(8,128...) custom-call(s32[1]{0:T(128)} %bitcast.flip_ref, s32[12,8]{1,0:T(8,128)S(1)} %and_select_fusion.table_ref, ...), custom_call_target="tpu_custom_call" | custom-call | tf_op jit(solution)/shard_map/near/pallas_call | solution.py:217
  29.0 3.4 %collective-permute-start.5 = (bf16[2,4,128,128]{3,2,1,0:T(8,128)(2,1)S(1)}, bf16[2,4,128,128]{3,2,1,0:T(8,128)(2,1)S(1)}, u32[]{:S(2)}, u32[]{:S(2)}) collective-permute-start(bf16[2,4,128,128]{3,2,1,0:T(8,128)(2,1)S(1)} %get-tuple-element.19), channel_id=1, source_target_pairs={{0,1},{1,0},{2,3},{3,2},{4,5},{5,4},{6,7},{7,6},{8,9},{9,8},{10,11... | collective-permute-start | bytes 786440 | tf_op jit(solution)/shard_map/ppermute | solution.py:237
  32.4 1.6 %far.1 = (bf16[2,4,128,128]{3,2,1,0:T(8,128)(2,1)S(1)}, bf16[2,4,128,128]{3,2,1,0:T(8,128)(2,1)S(1)}) custom-call(s32[1]{0:T(128)} %bitcast.flip_ref, s32[2,8]{1,0:T(2,128)S(1)} %compare_select_fusion.table_ref, s32[4,12]{1,0:T(4,128)S(1)} %convert_element_type.3.keep_ref, bf16[11,128,128]{2,1,0:T(8,128)(2,1)S(1)} %collective-permute-done.2.far_ref, ...), custom_call_target="tpu_custom_call" | custom-call | tf_op jit(solution)/shard_map/far/pallas_call | solution.py:242
  34.0 0.1 collective-permute-start.6
  34.1 1.5 %collective-permute-done.6 = bf16[2,4,128,128]{3,2,1,0:T(8,128)(2,1)S(1)} collective-permute-done((bf16[2,4,128,128]{3,2,1,0:T(8,128)(2,1)S(1)}, bf16[2,4,128,128]{3,2,1,0:T(8,128)(2,1)S(1)}, u32[]{:S(2)}, u32[]{:S(2)}) %collective-permute-start.6) | collective-permute-done | bytes 262176 | tf_op jit(solution)/shard_map/ppermute | solution.py:255
  35.6 1.2 %maximum_select_fusion = bf16[8,4,128,128]{3,2,1,0:T(8,128)(2,1)} fusion(bf16[2,4,128,128]{3,2,1,0:T(8,128)(2,1)S(1)} %collective-permute-done.6, bf16[2,4,128,128]{3,2,1,0:T(8,128)(2,1)S(1)} %collective-permute-done.5, bf16[2,4,128,128]{3,2,1,0:T(8,128)(2,1)S(1)} %get-tuple-element.18, bf16[2,4,128,128]{3,2,1,0:T(8,128)(2,1)S(1)} %get-tuple-element.17, pred[]{:T(512)S(6)} %eq.18), kind=kLoop, calls=%fused_computation | loop fusion | flops 3670016 | bytes 2097153 | tf_op jit(solution)/shard_map/jit(_where)/select_n | solution.py:256
  (20 shorter events, 0.1 us)
Async XLA Ops:
  0.8 10.6 %collective-permute-start = (s32[2,8]{1,0:T(2,128)S(1)}, s32[2,8]{1,0:T(2,128)S(1)}, u32[]{:S(2)}, u32[]{:S(2)}) collective-permute-start(s32[2,8]{1,0:T(2,128)S(1)} %constant_dynamic-slice_fusion.2), channel_id=1, source_target_pairs={{0,2},{2,4},{4,6},{6,8},{8,10},{10,12},{12,14},{14,0},{1,15},{3,1}... | collective-permute-start | bytes 200 | tf_op jit(solution)/shard_map/ppermute | solution.py:207
  3.8 7.8 %collective-permute-start.1 = (bf16[8,4,128,128]{3,2,1,0:T(8,128)(2,1)}, bf16[8,4,128,128]{3,2,1,0:T(8,128)(2,1)S(1)}, u32[]{:S(2)}, u32[]{:S(2)}) collective-permute-start(bf16[8,4,128,128]{3,2,1,0:T(8,128)(2,1)} %own_ref.3), channel_id=1, source_target_pairs={{0,1},{1,0},{2,3},{3,2},{4,5},{5,4},{6,7},{7,6},{8,9},{9,8},{10,11... | collective-permute-start | bytes 3145736 | tf_op jit(solution)/shard_map/ppermute | solution.py:178
  7.5 15.6 %copy-start = (bf16[8,4,128,128]{3,2,1,0:T(8,128)(2,1)S(1)}, bf16[8,4,128,128]{3,2,1,0:T(8,128)(2,1)}, u32[]{:S(2)}) copy-start(bf16[8,4,128,128]{3,2,1,0:T(8,128)(2,1)} %own_ref.3) | copy-start | bytes 3145732
  7.5 15.6 %collective-permute-start.3 = (bf16[2,4,128,128]{3,2,1,0:T(8,128)(2,1)S(1)}, bf16[2,4,128,128]{3,2,1,0:T(8,128)(2,1)S(1)}, u32[]{:S(2)}, u32[]{:S(2)}) collective-permute-start(bf16[2,4,128,128]{3,2,1,0:T(8,128)(2,1)S(1)} %get-tuple-element.22), channel_id=1, source_target_pairs={{0,2},{2,4},{4,6},{6,8},{8,10},{10,12},{12,14},{14,0},{1,15},{3,1}... | collective-permute-start | bytes 786440 | tf_op jit(solution)/shard_map/ppermute | solution.py:179
  7.5 15.5 %collective-permute-start.4 = (bf16[2,4,128,128]{3,2,1,0:T(8,128)(2,1)S(1)}, bf16[2,4,128,128]{3,2,1,0:T(8,128)(2,1)S(1)}, u32[]{:S(2)}, u32[]{:S(2)}) collective-permute-start(bf16[2,4,128,128]{3,2,1,0:T(8,128)(2,1)S(1)} %get-tuple-element.21), channel_id=1, source_target_pairs={{1,2},{3,4},{5,6},{7,8},{9,10},{11,12},{13,14},{15,0},{0,15},{2,1}... | collective-permute-start | bytes 786440 | tf_op jit(solution)/shard_map/ppermute | solution.py:180
  11.6 1.0 %copy-start.1 = (bf16[8,4,128,128]{3,2,1,0:T(8,128)(2,1)}, bf16[8,4,128,128]{3,2,1,0:T(8,128)(2,1)S(1)}, u32[]{:S(2)}) copy-start(bf16[8,4,128,128]{3,2,1,0:T(8,128)(2,1)S(1)} %collective-permute-done.1.other_ref) | copy-start | bytes 3145732
  15.0 17.4 %collective-permute-start.2 = (bf16[11,128,128]{2,1,0:T(8,128)(2,1)}, bf16[11,128,128]{2,1,0:T(8,128)(2,1)S(1)}, u32[]{:S(2)}, u32[]{:S(2)}) collective-permute-start(bf16[11,128,128]{2,1,0:T(8,128)(2,1)} %pack.1), channel_id=1, source_target_pairs={{0,2},{2,4},{4,6},{6,8},{8,10},{10,12},{12,14},{14,0},{1,15},{3,1}... | collective-permute-start | bytes 1081352 | tf_op jit(solution)/shard_map/ppermute | solution.py:205
  23.1 1.2 %copy-start.2 = (bf16[8,4,128,128]{3,2,1,0:T(8,128)(2,1)S(1)}, bf16[8,4,128,128]{3,2,1,0:T(8,128)(2,1)}, u32[]{:S(2)}) copy-start(bf16[8,4,128,128]{3,2,1,0:T(8,128)(2,1)} %copy-done.1) | copy-start | bytes 3145732
  29.0 5.1 %collective-permute-start.5 = (bf16[2,4,128,128]{3,2,1,0:T(8,128)(2,1)S(1)}, bf16[2,4,128,128]{3,2,1,0:T(8,128)(2,1)S(1)}, u32[]{:S(2)}, u32[]{:S(2)}) collective-permute-start(bf16[2,4,128,128]{3,2,1,0:T(8,128)(2,1)S(1)} %get-tuple-element.19), channel_id=1, source_target_pairs={{0,1},{1,0},{2,3},{3,2},{4,5},{5,4},{6,7},{7,6},{8,9},{9,8},{10,11... | collective-permute-start | bytes 786440 | tf_op jit(solution)/shard_map/ppermute | solution.py:237
  34.0 1.6 %collective-permute-start.6 = (bf16[2,4,128,128]{3,2,1,0:T(8,128)(2,1)S(1)}, bf16[2,4,128,128]{3,2,1,0:T(8,128)(2,1)S(1)}, u32[]{:S(2)}, u32[]{:S(2)}) collective-permute-start(bf16[2,4,128,128]{3,2,1,0:T(8,128)(2,1)S(1)} %get-tuple-element.20), channel_id=1, source_target_pairs={{0,1},{1,0},{2,3},{3,2},{4,5},{5,4},{6,7},{7,6},{8,9},{9,8},{10,11... | collective-permute-start | bytes 786440 | tf_op jit(solution)/shard_map/ppermute | solution.py:255

commit v3 on v2

v3 whole, which is shorter than its diff:
```python
import functools

import jax
import jax.numpy as jnp
from jax import lax
from jax.experimental import pallas as pl
from jax.experimental.pallas import tpu as pltpu
from jax.sharding import PartitionSpec as P

REACH = 4
MIB = 1024 * 1024
ABSENT = 64
TILE = 16

HEAVY = pl.CostEstimate(flops=20_000_000_000, bytes_accessed=0, transcendentals=0)
LIGHT = pl.CostEstimate(flops=0, bytes_accessed=0, transcendentals=0)

SMEM = pl.BlockSpec(memory_space=pltpu.SMEM)
VMEM = pl.BlockSpec(memory_space=pltpu.VMEM)
ANY = pl.BlockSpec(memory_space=pl.ANY)
HBM = pl.BlockSpec(memory_space=pltpu.HBM)


def limit(mib):
    return pltpu.CompilerParams(vmem_limit_bytes=mib * MIB)


def blocks(first, last, size):
    return slice(first * size, last * size)


def own_place(columns_ref, q, s, limit):
    rows, slots = columns_ref.shape
    flip = lax.axis_index("col")
    row = jnp.where(flip == 0, q - REACH, rows + REACH - 1 - q)
    slot = lax.rem(s + flip * (slots // 2), slots)
    total = rows * lax.axis_size("row")
    column = columns_ref[row, slot]
    step = column - lax.axis_index("row") * rows - row
    step = jnp.where(step > REACH, step - total, step)
    step = jnp.where(step < -REACH, step + total, step)
    place = jnp.where(flip == 0, q + step, q - step)
    inside = (column >= 0) & (place >= 0) & (place < limit)
    return jnp.where(inside, place, limit)


def halo_place(steps_ref, rows, slots, q, s, limit):
    flip = lax.axis_index("col")
    row = jnp.where(flip == 0, rows - REACH + q, REACH - 1 - q)
    slot = lax.rem(s + flip * (slots // 2), slots)
    step = steps_ref[row, slot]
    place = jnp.where(flip == 0, q + step, q - step)
    inside = (step <= REACH) & (place >= 0) & (place < limit)
    return jnp.where(inside, place, limit)


def edge_kernel(near, columns_ref, matrix_ref, same_ref, swap_ref, copied_ref, steps, sems):
    rows, half, size = matrix_ref.shape[:3]
    start = jnp.where(lax.axis_index("col") == 0, rows - near, 0)
    copies = []
    for n in range(near):
        for s in range(half):
            at = blocks(n * half + s, n * half + s + 1, size)
            copies.append(pltpu.make_async_copy(matrix_ref.at[start + n, s], same_ref.at[at], sems.at[0]))
            copies.append(
                pltpu.make_async_copy(
                    matrix_ref.at[rows - near - start + n, s], swap_ref.at[at], sems.at[1]
                )
            )
    held = pltpu.make_async_copy(columns_ref, copied_ref, sems.at[2])
    held.start()
    for copy in copies:
        copy.start()
    held.wait()
    column = copied_ref[...]
    row = lax.broadcasted_iota(jnp.int32, column.shape, 0) + lax.axis_index("row") * rows
    total = rows * lax.axis_size("row")
    step = column - row
    step = jnp.where(step > REACH, step - total, step)
    step = jnp.where(step < -REACH, step + total, step)
    step = jnp.where(column >= 0, step, ABSENT)
    steps[...] = jnp.zeros_like(steps)
    steps[:rows, : column.shape[1]] = step.astype(jnp.float32)
    same_ref[near * half * size :, :] = steps[...].astype(same_ref.dtype)
    for copy in copies:
        copy.wait()


def base_kernel(far, columns_ref, own_ref, other_ref, panel_ref, first_ref):
    rows, half, size = own_ref.shape[0], own_ref.shape[1], own_ref.shape[2]
    reach = REACH
    width = rows + reach
    panel_ref[...] = jnp.zeros_like(panel_ref)
    for q in reversed(range(reach, width)):
        index = jnp.where(lax.axis_index("col") == 0, q - reach, width - 1 - q)
        for s in range(2 * half):
            place = pl.multiple_of(own_place(columns_ref, q, s, width + far) * size, size)
            source = own_ref if s < half else other_ref
            panel_ref[blocks(q - reach, q - reach + 1, size), pl.ds(place, size)] = source[index, s % half]
    for p in range(width // 2):
        low = max(reach, 2 * p - reach)
        high = min(width, 2 * p + 2 + reach)
        cols = blocks(2 * p, 2 * p + 2, size)
        first_ref[:, cols] = jnp.dot(
            panel_ref[blocks(0, reach, size), blocks(low, high, size)],
            panel_ref[blocks(low - reach, high - reach, size), cols],
            preferred_element_type=jnp.float32,
        )


def pack_kernel(far, panel_ref, after_ref, out_ref):
    size = out_ref.shape[1]
    at = 0
    for f in range(far):
        row = REACH + f
        for k in range(2 * REACH, 3 * REACH + 1 + f):
            out_ref[at] = panel_ref[blocks(row, row + 1, size), blocks(k, k + 1, size)]
            at += 1


def mark_kept(columns_ref, keep_ref, count):
    width = columns_ref.shape[0] + REACH
    for i in range(count):
        for k in range(width + 1):
            keep_ref[i, k] = 0
        for s in range(columns_ref.shape[1]):
            keep_ref[i, own_place(columns_ref, i + REACH, s, width)] = 1


def near_kernel(
    far, columns_ref, panel_ref, first_ref, near_ref, cross_ref,
    stay_ref, leave_ref, part_ref, high_ref, cube_ref, lower_ref,
    square, result, keep_ref, steps, halo_ref, sem
):
    reach = REACH
    half, size = stay_ref.shape[1], stay_ref.shape[2]
    steps[...] = near_ref[(reach - far) * half * size :, :].astype(jnp.float32).astype(jnp.int32)
    copy = pltpu.make_async_copy(steps, halo_ref, sem)
    copy.start()
    width = panel_ref.shape[0] // size + reach
    near = reach - far
    low_cols = reach + far
    far_cols = 2 * reach + far
    near_cols = 2 * reach
    flip = lax.axis_index("col")
    mark_kept(columns_ref, keep_ref, reach)
    lower_ref[...] = jnp.zeros_like(lower_ref)
    result[:, blocks(width, width + 1, size)] = jnp.zeros((near * size, size), result.dtype)
    copy.wait()
    for n in range(near):
        index = jnp.where(flip == 0, n, near - 1 - n)
        for s in range(2 * half):
            place = halo_place(halo_ref, *columns_ref.shape, n + far, s, near_cols)
            place = pl.multiple_of(place * size, size)
            source = near_ref if s < half else cross_ref
            at = pl.multiple_of((index * half + s % half) * size, size)
            lower_ref[blocks(n, n + 1, size), pl.ds(place, size)] = source[pl.ds(at, size)]
    left = panel_ref.at[blocks(0, reach, size), blocks(far, reach, size)]
    for p in range(width // 2):
        cols = blocks(2 * p, 2 * p + 2, size)
        value = first_ref[:, cols]
        if 2 * p < near_cols:
            value = value + jnp.dot(left[...], lower_ref[:, cols], preferred_element_type=jnp.float32)
        for i in range(reach):
            for k in (2 * p, 2 * p + 1):
                block = value[blocks(i, i + 1, size), blocks(k - 2 * p, k - 2 * p + 1, size)]
                at = (blocks(i, i + 1, size), blocks(k, k + 1, size))
                if i < far and k < low_cols:
                    part_ref[at] = block
                    square[at] = jnp.zeros((size, size), square.dtype)
                elif abs(i + reach - k) <= reach:
                    square[at] = jnp.where(keep_ref[i, k] > 0, block, 0.0).astype(square.dtype)
                else:
                    square[at] = jnp.zeros((size, size), square.dtype)
    for p in range(width // 2):
        cols = blocks(2 * p, 2 * p + 2, size)
        low = max(reach, 2 * p - reach)
        high = min(width, 2 * p + 2 + reach)
        value = jnp.dot(
            square[:, blocks(low, high, size)],
            panel_ref[blocks(low - reach, high - reach, size), cols],
            preferred_element_type=jnp.float32,
        )
        if 2 * p < near_cols:
            value = value + jnp.dot(
                square[:, blocks(far, reach, size)], lower_ref[:, cols], preferred_element_type=jnp.float32
            )
        if 2 * p < far_cols:
            cube_ref[:, cols] = value[: far * size]
        result[:, cols] = (
            3.0 * square[far * size :, cols].astype(jnp.float32) - 2.0 * value[far * size :]
        ).astype(result.dtype)
    high_ref[...] = square[: far * size, blocks(low_cols, far_cols, size)]
    for i in range(near):
        index = jnp.where(flip == 0, i, near - 1 - i)
        for s in range(2 * half):
            place = pl.multiple_of(own_place(columns_ref, i + reach + far, s, width) * size, size)
            target = stay_ref if s < half else leave_ref
            target[index, s % half] = result[blocks(i, i + 1, size), pl.ds(place, size)]


def far_kernel(
    columns_ref, far_ref, part_ref, high_ref, cube_ref, lower_ref, panel_ref, kept_near_ref, got_near_ref,
    stay_ref, leave_ref, out_ref, farthest, square, result, keep_ref, sems
):
    reach, far = REACH, stay_ref.shape[0]
    copies = placed(kept_near_ref, got_near_ref, out_ref, far, sems)
    half, size = stay_ref.shape[1], stay_ref.shape[2]
    low_cols = reach + far
    far_cols = 2 * reach + far
    near_cols = 2 * reach
    mark_kept(columns_ref, keep_ref, far)
    at = 0
    for f in range(far):
        for k in range(low_cols):
            here = (blocks(f, f + 1, size), blocks(k, k + 1, size))
            if k <= f + reach:
                farthest[here] = far_ref[at]
                at += 1
            else:
                farthest[here] = jnp.zeros((size, size), farthest.dtype)
    result[:, blocks(far_cols, far_cols + 1, size)] = jnp.zeros((far * size, size), result.dtype)
    left = panel_ref[blocks(0, far, size), blocks(0, far, size)]
    for p in range(low_cols // 2):
        cols = blocks(2 * p, 2 * p + 2, size)
        value = part_ref[:, cols] + jnp.dot(left, farthest[:, cols], preferred_element_type=jnp.float32)
        for i in range(far):
            for k in (2 * p, 2 * p + 1):
                block = value[blocks(i, i + 1, size), blocks(k - 2 * p, k - 2 * p + 1, size)]
                here = (blocks(i, i + 1, size), blocks(k, k + 1, size))
                if abs(i + reach - k) <= reach:
                    square[here] = jnp.where(keep_ref[i, k] > 0, block, 0.0).astype(square.dtype)
                else:
                    square[here] = jnp.zeros((size, size), square.dtype)
    for p in range(far_cols // 2):
        cols = blocks(2 * p, 2 * p + 2, size)
        value = cube_ref[:, cols] + jnp.dot(
            square[:, blocks(reach, low_cols, size)],
            panel_ref[blocks(0, far, size), cols],
            preferred_element_type=jnp.float32,
        )
        if 2 * p < near_cols:
            value = value + jnp.dot(
                square[:, blocks(far, reach, size)], lower_ref[:, cols], preferred_element_type=jnp.float32
            )
        if 2 * p < low_cols:
            value = value + jnp.dot(
                square[:, blocks(0, far, size)], farthest[:, cols], preferred_element_type=jnp.float32
            )
            kept = square[:, cols]
        else:
            kept = high_ref[:, blocks(2 * p - low_cols, 2 * p + 2 - low_cols, size)]
        result[:, cols] = (3.0 * kept.astype(jnp.float32) - 2.0 * value).astype(result.dtype)
    for i in range(far):
        index = jnp.where(lax.axis_index("col") == 0, i, far - 1 - i)
        for s in range(2 * half):
            place = pl.multiple_of(own_place(columns_ref, i + reach, s, far_cols) * size, size)
            target = stay_ref if s < half else leave_ref
            target[index, s % half] = result[blocks(i, i + 1, size), pl.ds(place, size)]
    for copy in copies:
        copy.wait()


def placed(kept_ref, got_ref, out_ref, inner, sems):
    rows, count = out_ref.shape[0], kept_ref.shape[0]
    straight = lax.axis_index("col") == 0
    low, high = inner, rows - inner - count
    copies = []
    for n in range(count):
        copies.append(
            pltpu.make_async_copy(
                kept_ref.at[n], out_ref.at[jnp.where(straight, low, high) + n], sems.at[0]
            )
        )
        copies.append(
            pltpu.make_async_copy(got_ref.at[n], out_ref.at[jnp.where(straight, high, low) + n], sems.at[1])
        )
    for copy in copies:
        copy.start()
    return copies


def finish_kernel(kept_ref, got_ref, before_ref, out_ref, sems):
    for copy in placed(kept_ref, got_ref, out_ref, 0, sems):
        copy.wait()


def local(matrix, columns):
    local_rows, own_slots, size = matrix.shape[:3]
    dtype = matrix.dtype
    reach = REACH
    far = reach // 2
    near = reach - far
    cols = lax.axis_size("col")
    ring = lax.axis_size("row")
    width = local_rows + reach
    low_cols = reach + far
    far_cols = 2 * reach + far
    near_cols = 2 * reach
    same = [(r * cols, (r + 1) % ring * cols) for r in range(ring)] + [
        (r * cols + 1, (r - 1) % ring * cols + 1) for r in range(ring)
    ]
    swap = [(r * cols + 1, (r + 1) % ring * cols) for r in range(ring)] + [
        (r * cols, (r - 1) % ring * cols + 1) for r in range(ring)
    ]
    beside = [(i, (i + 1) % cols) for i in range(cols)]
    axes = ("row", "col")
    edge_rows = near * own_slots * size
    to_same, to_swap, held = pl.pallas_call(
        functools.partial(edge_kernel, near),
        out_shape=(
            jax.ShapeDtypeStruct((edge_rows + TILE, size), dtype),
            jax.ShapeDtypeStruct((edge_rows, size), dtype),
            jax.ShapeDtypeStruct(columns.shape, columns.dtype),
        ),
        in_specs=[HBM, HBM],
        out_specs=(VMEM, VMEM, VMEM),
        scratch_shapes=[pltpu.VMEM((TILE, size), jnp.float32), pltpu.SemaphoreType.DMA((3,))],
        compiler_params=limit(1),
        cost_estimate=LIGHT,
        name="edge",
    )(
        pltpu.with_memory_space_constraint(columns, pltpu.HBM),
        pltpu.with_memory_space_constraint(matrix, pltpu.HBM),
    )
    near_rows = lax.ppermute(to_same, axes, same)
    cross_rows = lax.ppermute(to_swap, axes, swap)
    other = lax.ppermute(matrix, "col", beside)

    panel, first_part = pl.pallas_call(
        functools.partial(base_kernel, far),
        out_shape=(
            jax.ShapeDtypeStruct((local_rows * size, (width + far + 1) * size), dtype),
            jax.ShapeDtypeStruct((reach * size, width * size), jnp.float32),
        ),
        in_specs=[SMEM, VMEM, VMEM],
        out_specs=(VMEM, VMEM),
        compiler_params=limit(12),
        cost_estimate=LIGHT,
        name="base",
    )(held, matrix, other)
    packed = pl.pallas_call(
        functools.partial(pack_kernel, far),
        out_shape=jax.ShapeDtypeStruct((sum(reach + 1 + f for f in range(far)), size, size), dtype),
        in_specs=[VMEM, ANY],
        out_specs=VMEM,
        compiler_params=limit(1),
        cost_estimate=LIGHT,
        name="pack",
    )(panel, cross_rows)
    far_blocks = lax.ppermute(packed, axes, same)

    rows_out = jax.ShapeDtypeStruct((near, own_slots, size, size), dtype)
    stay_near, leave_near, part, high, cube, lower = pl.pallas_call(
        functools.partial(near_kernel, far),
        out_shape=(
            rows_out,
            rows_out,
            jax.ShapeDtypeStruct((far * size, low_cols * size), jnp.float32),
            jax.ShapeDtypeStruct((far * size, (far_cols - low_cols) * size), dtype),
            jax.ShapeDtypeStruct((far * size, far_cols * size), jnp.float32),
            jax.ShapeDtypeStruct((near * size, (near_cols + 1) * size), dtype),
        ),
        in_specs=[SMEM] + [VMEM] * 4,
        out_specs=(VMEM,) * 6,
        scratch_shapes=[
            pltpu.VMEM((reach * size, width * size), dtype),
            pltpu.VMEM((near * size, (width + 1) * size), dtype),
            pltpu.SMEM((reach, width + 1), jnp.int32),
            pltpu.VMEM((TILE, size), jnp.int32),
            pltpu.SMEM((TILE, size), jnp.int32),
            pltpu.SemaphoreType.DMA,
        ],
        compiler_params=limit(16),
        cost_estimate=HEAVY,
        name="near",
    )(held, panel, first_part, near_rows, cross_rows)
    arrived_near = lax.ppermute(leave_near, "col", beside)

    far_out = jax.ShapeDtypeStruct((far, own_slots, size, size), dtype)
    stay_far, leave_far, out = pl.pallas_call(
        far_kernel,
        out_shape=(far_out, far_out, jax.ShapeDtypeStruct(matrix.shape, dtype)),
        in_specs=[SMEM] + [VMEM] * 8,
        out_specs=(VMEM, VMEM, HBM),
        scratch_shapes=[
            pltpu.VMEM((far * size, low_cols * size), dtype),
            pltpu.VMEM((far * size, low_cols * size), dtype),
            pltpu.VMEM((far * size, (far_cols + 1) * size), dtype),
            pltpu.SMEM((far, width + 1), jnp.int32),
            pltpu.SemaphoreType.DMA((2,)),
        ],
        compiler_params=limit(16),
        cost_estimate=LIGHT,
        name="far",
    )(held, far_blocks, part, high, cube, lower, panel, stay_near, arrived_near)
    arrived_far = lax.ppermute(leave_far, "col", beside)
    return pl.pallas_call(
        finish_kernel,
        out_shape=jax.ShapeDtypeStruct(matrix.shape, dtype),
        in_specs=[VMEM, VMEM, HBM],
        out_specs=HBM,
        input_output_aliases={2: 0},
        scratch_shapes=[pltpu.SemaphoreType.DMA((2,))],
        compiler_params=limit(1),
        cost_estimate=LIGHT,
        name="finish",
    )(stay_far, arrived_far, out)


def solution(mesh):
    placed = (P(("geom", "row"), "col", None, None), P("row", None))
    return jax.shard_map(
        local,
        mesh=mesh,
        in_specs=placed,
        out_specs=P(("geom", "row"), "col", None, None),
        check_vma=False,
    )
```

time: 37.1 us -> 31.7 us (0.85)
  other arithmetic: 3.71 us -> 0 us
  local copies, waits for them, and re-layouts: 3.47 us -> 1.23 us
  Pallas kernels: 8.77 us -> 10.4 us
  waiting for transfers between devices: 9.33 us -> 8.14 us
    ppermute x3 -> x2, waiting for transfers between devices: 7.81 us -> 3.06 us  [the longest x1 3.06 us: local(): cross_rows = lax.ppermute(to_swap, axes, swap)]
    ppermute x1, starting transfers between devices: 0.08 us -> 4.59 us  [local(): far_blocks = lax.ppermute(packed, axes, same)]
    select_n x9 -> x0, other arithmetic: 3.61 us -> none  [the longest x1 1.23 us: local(): jnp.where(straight, jnp.concatenate([stay_far, stay_near, arrived_near, a...]
    ppermute x1, starting transfers between devices: 3.4 us -> 0.07 us  [local(): arrived_near = lax.ppermute(leave_near, 'col', beside)]
    ppermute x1, waiting for transfers between devices: 0.01 us -> 2.4 us  [local(): far_blocks = lax.ppermute(packed, axes, same)]
    ppermute x1, starting transfers between devices: 2.59 us -> 0.45 us  [local(): other = lax.ppermute(matrix, 'col', beside)]
    pallas_call x3 -> x6, Pallas kernels: 8.77 us -> 10.4 us  [the longest x1 3.58 us: local(): pl.pallas_call(functools.partial(near_kernel, far), out_shape=(rows_out,...]
    ppermute x1, waiting for transfers between devices: 0.01 us -> 1.52 us  [local(): arrived_near = lax.ppermute(leave_near, 'col', beside)]
  transfers between devices with their start and end apart: 7 -> 6, of which waited for: 2 -> 4; matrix products, arithmetic and copies ran while one was open for 8% -> 0% of each run, Pallas kernels for 24% -> 23%
where the time goes in v3:
time: 31.7 us; the launch traced here: 31.4 us
  starting transfers between devices  11.7 us (37%)
  Pallas kernels  10.4 us (33%)
  waiting for transfers between devices  8.14 us (26%)
  local copies, waits for them, and re-layouts  1.23 us (4%)
    ppermute x1, starting transfers between devices, local(): far_blocks = lax.ppermute(packed, axes, same)  4.59 us
    pallas_call x1, Pallas kernels, local(): pl.pallas_call(functools.partial(near_kernel, far), out_shape=(rows_out,...  3.58 us
    ppermute x1, starting transfers between devices, local(): cross_rows = lax.ppermute(to_swap, axes, swap)  3.38 us
    ppermute x1, waiting for transfers between devices, local(): cross_rows = lax.ppermute(to_swap, axes, swap)  3.06 us
    pallas_call x1, Pallas kernels, local(): pl.pallas_call(functools.partial(base_kernel, far), out_shape=(jax.ShapeD...  2.68 us
    ppermute x1, starting transfers between devices, local(): near_rows = lax.ppermute(to_same, axes, same)  2.57 us
    ppermute x1, waiting for transfers between devices, local(): far_blocks = lax.ppermute(packed, axes, same)  2.4 us
    pallas_call x1, Pallas kernels, local(): pl.pallas_call(far_kernel, out_shape=(far_out, far_out, jax.ShapeDtypeStr...  2.22 us
  transfers between devices with their start and end apart: 6, of which 4 were waited for; matrix products, arithmetic and copies ran while one was open for 0% of the time, Pallas kernels for 23%

profile of v3, /device:TPU:0, one launch (start us, length us, event | category | flops | bytes accessed | tf_op | source)
XLA Modules:
  0.0 31.4 jit_solution(6893611038150240018)
XLA Ops:
  0.0 0.5 %collective-permute-start = (bf16[8,4,128,128]{3,2,1,0:T(8,128)(2,1)}, bf16[8,4,128,128]{3,2,1,0:T(8,128)(2,1)S(1)}, u32[]{:S(2)}, u32[]{:S(2)}) collective-permute-start(bf16[8,4,128,128]{3,2,1,0:T(8,128)(2,1)} %own_ref.1), channel_id=1, source_target_pairs={{0,1},{1,0},{2,3},{3,2},{4,5},{5,4},{6,7},{7,6},{8,9},{9,8},{10,11... | collective-permute-start | bytes 3145736 | tf_op jit(solution)/shard_map/ppermute | solution.py:328
  0.5 1.0 %edge.1 = (bf16[1040,128]{1,0:T(8,128)(2,1)S(1)}, bf16[1024,128]{1,0:T(8,128)(2,1)S(1)}, s32[8,8]{1,0:T(8,128)S(1)}) custom-call(s32[8,8]{1,0:T(8,128)} %columns_ref.1, bf16[8,4,128,128]{3,2,1,0:T(8,128)(2,1)} %own_ref.1), custom_call_target="tpu_custom_call" | custom-call | tf_op jit(solution)/shard_map/edge/pallas_call | solution.py:309
  1.5 2.6 %collective-permute-start.3 = (bf16[1040,128]{1,0:T(8,128)(2,1)S(1)}, bf16[1040,128]{1,0:T(8,128)(2,1)S(1)}, u32[]{:S(2)}, u32[]{:S(2)}) collective-permute-start(bf16[1040,128]{1,0:T(8,128)(2,1)S(1)} %get-tuple-element.23), channel_id=1, source_target_pairs={{0,2},{2,4},{4,6},{6,8},{8,10},{10,12},{12,14},{14,0},{1,15},{3,1}... | collective-permute-start | bytes 798728 | tf_op jit(solution)/shard_map/ppermute | solution.py:326
  4.1 3.4 %collective-permute-start.1 = (bf16[1024,128]{1,0:T(8,128)(2,1)S(1)}, bf16[1024,128]{1,0:T(8,128)(2,1)S(1)}, u32[]{:S(2)}, u32[]{:S(2)}) collective-permute-start(bf16[1024,128]{1,0:T(8,128)(2,1)S(1)} %get-tuple-element.21), channel_id=1, source_target_pairs={{1,2},{3,4},{5,6},{7,8},{9,10},{11,12},{13,14},{15,0},{0,15},{2,1}... | collective-permute-start | bytes 786440 | tf_op jit(solution)/shard_map/ppermute | solution.py:327
  7.4 0.0 collective-permute-done.other_ref
  7.4 0.0 copy-start
  7.4 1.2 %copy-done = bf16[8,4,128,128]{3,2,1,0:T(8,128)(2,1)S(1)} copy-done((bf16[8,4,128,128]{3,2,1,0:T(8,128)(2,1)S(1)}, bf16[8,4,128,128]{3,2,1,0:T(8,128)(2,1)}, u32[]{:S(2)}) %copy-start) | copy-done | bytes 1048600
  8.7 2.7 %base.1 = (bf16[1024,1920]{1,0:T(8,128)(2,1)S(1)}, f32[512,1536]{1,0:T(8,128)S(1)}) custom-call(s32[8,8]{1,0:T(8,128)S(1)} %get-tuple-element.19.columns_ref, bf16[8,4,128,128]{3,2,1,0:T(8,128)(2,1)S(1)} %copy-done, bf16[8,4,128,128]{3,2,1,0:T(8,128)(2,1)S(1)} %collective-permute-done.other_ref), custom_call_target="tpu_custom_call" | custom-call | tf_op jit(solution)/shard_map/base/pallas_call | solution.py:330
  11.4 3.1 %collective-permute-done.1.after_ref.cross_ref = bf16[1024,128]{1,0:T(8,128)(2,1)S(1)} collective-permute-done((bf16[1024,128]{1,0:T(8,128)(2,1)S(1)}, bf16[1024,128]{1,0:T(8,128)(2,1)S(1)}, u32[]{:S(2)}, u32[]{:S(2)}) %collective-permute-start.1) | collective-permute-done | bytes 262176 | tf_op jit(solution)/shard_map/ppermute | solution.py:327
  14.4 0.1 pack.1
  14.5 4.6 %collective-permute-start.2 = (bf16[11,128,128]{2,1,0:T(8,128)(2,1)S(1)}, bf16[11,128,128]{2,1,0:T(8,128)(2,1)S(1)}, u32[]{:S(2)}, u32[]{:S(2)}) collective-permute-start(bf16[11,128,128]{2,1,0:T(8,128)(2,1)S(1)} %pack.1), channel_id=1, source_target_pairs={{0,2},{2,4},{4,6},{6,8},{8,10},{10,12},{12,14},{14,0},{1,15},{3,1}... | collective-permute-start | bytes 1081352 | tf_op jit(solution)/shard_map/ppermute | solution.py:351
  19.1 0.0 collective-permute-done.3.near_ref
  19.1 3.6 %near.1 = (bf16[2,4,128,128]{3,2,1,0:T(8,128)(2,1)S(1)}, bf16[2,4,128,128]{3,2,1,0:T(8,128)(2,1)S(1)}, f32[256,768]{1,0:T(8,128)S(1)}, bf16[256,512]{1,0:T(8,128...) custom-call(s32[8,8]{1,0:T(8,128)S(1)} %get-tuple-element.19.columns_ref, ...), custom_call_target="tpu_custom_call" | custom-call | flops 20000000000 | tf_op jit(solution)/shard_map/near/pallas_call | solution.py:354
  22.7 0.1 collective-permute-start.4
  22.7 1.5 %collective-permute-done.4.got_near_ref = bf16[2,4,128,128]{3,2,1,0:T(8,128)(2,1)S(1)} collective-permute-done((bf16[2,4,128,128]{3,2,1,0:T(8,128)(2,1)S(1)}, bf16[2,4,128,128]{3,2,1,0:T(8,128)(2,1)S(1)}, u32[]{:S(2)}, u32[]{:S(2)}) %collective-permute-start.4) | collective-permute-done | bytes 262176 | tf_op jit(solution)/shard_map/ppermute | solution.py:378
  24.3 2.4 %collective-permute-done.2.far_ref = bf16[11,128,128]{2,1,0:T(8,128)(2,1)S(1)} collective-permute-done((bf16[11,128,128]{2,1,0:T(8,128)(2,1)S(1)}, bf16[11,128,128]{2,1,0:T(8,128)(2,1)S(1)}, u32[]{:S(2)}, u32[]{:S(2)}) %collective-permute-start.2) | collective-permute-done | bytes 360480 | tf_op jit(solution)/shard_map/ppermute | solution.py:351
  26.7 2.2 %far.1 = (bf16[2,4,128,128]{3,2,1,0:T(8,128)(2,1)S(1)}, bf16[2,4,128,128]{3,2,1,0:T(8,128)(2,1)S(1)}, bf16[8,4,128,128]{3,2,1,0:T(8,128)(2,1)}) custom-call(s32[8,8]{1,0:T(8,128)S(1)} %get-tuple-element.19.columns_ref, bf16[11,128,128]{2,1,0:T(8,128)(2,1)S(1)} %collective-permute-done.2.far_ref, f32[256,768]{1,0:T(8,128)S(1)} %get-tuple-element.24.part_ref, ...), custom_call_target="tpu_custom_call" | custom-call | tf_op jit(solution)/shard_map/far/pallas_call | solution.py:381
  28.9 0.6 %collective-permute-start.5 = (bf16[2,4,128,128]{3,2,1,0:T(8,128)(2,1)S(1)}, bf16[2,4,128,128]{3,2,1,0:T(8,128)(2,1)S(1)}, u32[]{:S(2)}, u32[]{:S(2)}) collective-permute-start(bf16[2,4,128,128]{3,2,1,0:T(8,128)(2,1)S(1)} %get-tuple-element.31), channel_id=1, source_target_pairs={{0,1},{1,0},{2,3},{3,2},{4,5},{5,4},{6,7},{7,6},{8,9},{9,8},{10,11... | collective-permute-start | bytes 786440 | tf_op jit(solution)/shard_map/ppermute | solution.py:397
  29.5 1.2 %collective-permute-done.5.got_ref = bf16[2,4,128,128]{3,2,1,0:T(8,128)(2,1)S(1)} collective-permute-done((bf16[2,4,128,128]{3,2,1,0:T(8,128)(2,1)S(1)}, bf16[2,4,128,128]{3,2,1,0:T(8,128)(2,1)S(1)}, u32[]{:S(2)}, u32[]{:S(2)}) %collective-permute-start.5) | collective-permute-done | bytes 262176 | tf_op jit(solution)/shard_map/ppermute | solution.py:397
  30.6 0.8 %finish.1 = bf16[8,4,128,128]{3,2,1,0:T(8,128)(2,1)} custom-call(bf16[2,4,128,128]{3,2,1,0:T(8,128)(2,1)S(1)} %get-tuple-element.30.kept_ref, bf16[2,4,128,128]{3,2,1,0:T(8,128)(2,1)S(1)} %collective-permute-done.5.got_ref, bf16[8,4,128,128]{3,2,1,0:T(8,128)(2,1)} %get-tuple-element.32.before_ref), custom_call_target="tpu_custom_call", output_to_operand_aliasing={{}: (2, {})} | custom-call | tf_op jit(solution)/shard_map/finish/pallas_call | solution.py:398
Async XLA Ops:
  0.0 7.4 %collective-permute-start = (bf16[8,4,128,128]{3,2,1,0:T(8,128)(2,1)}, bf16[8,4,128,128]{3,2,1,0:T(8,128)(2,1)S(1)}, u32[]{:S(2)}, u32[]{:S(2)}) collective-permute-start(bf16[8,4,128,128]{3,2,1,0:T(8,128)(2,1)} %own_ref.1), channel_id=1, source_target_pairs={{0,1},{1,0},{2,3},{3,2},{4,5},{5,4},{6,7},{7,6},{8,9},{9,8},{10,11... | collective-permute-start | bytes 3145736 | tf_op jit(solution)/shard_map/ppermute | solution.py:328
  1.5 17.6 %collective-permute-start.3 = (bf16[1040,128]{1,0:T(8,128)(2,1)S(1)}, bf16[1040,128]{1,0:T(8,128)(2,1)S(1)}, u32[]{:S(2)}, u32[]{:S(2)}) collective-permute-start(bf16[1040,128]{1,0:T(8,128)(2,1)S(1)} %get-tuple-element.23), channel_id=1, source_target_pairs={{0,2},{2,4},{4,6},{6,8},{8,10},{10,12},{12,14},{14,0},{1,15},{3,1}... | collective-permute-start | bytes 798728 | tf_op jit(solution)/shard_map/ppermute | solution.py:326
  4.1 10.3 %collective-permute-start.1 = (bf16[1024,128]{1,0:T(8,128)(2,1)S(1)}, bf16[1024,128]{1,0:T(8,128)(2,1)S(1)}, u32[]{:S(2)}, u32[]{:S(2)}) collective-permute-start(bf16[1024,128]{1,0:T(8,128)(2,1)S(1)} %get-tuple-element.21), channel_id=1, source_target_pairs={{1,2},{3,4},{5,6},{7,8},{9,10},{11,12},{13,14},{15,0},{0,15},{2,1}... | collective-permute-start | bytes 786440 | tf_op jit(solution)/shard_map/ppermute | solution.py:327
  7.4 1.2 %copy-start = (bf16[8,4,128,128]{3,2,1,0:T(8,128)(2,1)S(1)}, bf16[8,4,128,128]{3,2,1,0:T(8,128)(2,1)}, u32[]{:S(2)}) copy-start(bf16[8,4,128,128]{3,2,1,0:T(8,128)(2,1)} %own_ref.1) | copy-start | bytes 3145732
  14.5 12.2 %collective-permute-start.2 = (bf16[11,128,128]{2,1,0:T(8,128)(2,1)S(1)}, bf16[11,128,128]{2,1,0:T(8,128)(2,1)S(1)}, u32[]{:S(2)}, u32[]{:S(2)}) collective-permute-start(bf16[11,128,128]{2,1,0:T(8,128)(2,1)S(1)} %pack.1), channel_id=1, source_target_pairs={{0,2},{2,4},{4,6},{6,8},{8,10},{10,12},{12,14},{14,0},{1,15},{3,1}... | collective-permute-start | bytes 1081352 | tf_op jit(solution)/shard_map/ppermute | solution.py:351
  22.7 1.6 %collective-permute-start.4 = (bf16[2,4,128,128]{3,2,1,0:T(8,128)(2,1)S(1)}, bf16[2,4,128,128]{3,2,1,0:T(8,128)(2,1)S(1)}, u32[]{:S(2)}, u32[]{:S(2)}) collective-permute-start(bf16[2,4,128,128]{3,2,1,0:T(8,128)(2,1)S(1)} %get-tuple-element.29), channel_id=1, source_target_pairs={{0,1},{1,0},{2,3},{3,2},{4,5},{5,4},{6,7},{7,6},{8,9},{9,8},{10,11... | collective-permute-start | bytes 786440 | tf_op jit(solution)/shard_map/ppermute | solution.py:378
  28.9 1.8 %collective-permute-start.5 = (bf16[2,4,128,128]{3,2,1,0:T(8,128)(2,1)S(1)}, bf16[2,4,128,128]{3,2,1,0:T(8,128)(2,1)S(1)}, u32[]{:S(2)}, u32[]{:S(2)}) collective-permute-start(bf16[2,4,128,128]{3,2,1,0:T(8,128)(2,1)S(1)} %get-tuple-element.31), channel_id=1, source_target_pairs={{0,1},{1,0},{2,3},{3,2},{4,5},{5,4},{6,7},{7,6},{8,9},{9,8},{10,11... | collective-permute-start | bytes 786440 | tf_op jit(solution)/shard_map/ppermute | solution.py:397

commit v4 on v3

--- a/solution.py
+++ b/solution.py
@@ -54,19 +54,20 @@
     return jnp.where(inside, place, limit)
 
 
-def edge_kernel(near, columns_ref, matrix_ref, same_ref, swap_ref, copied_ref, steps, sems):
+def edge_kernel(near, columns_ref, matrix_ref, *refs):
     rows, half, size = matrix_ref.shape[:3]
-    start = jnp.where(lax.axis_index("col") == 0, rows - near, 0)
+    same_refs, swap_refs = refs[:near], refs[near : 2 * near]
+    copied_ref, steps, sems = refs[2 * near :]
+    straight = lax.axis_index("col") == 0
     copies = []
     for n in range(near):
+        up, down = rows - 1 - n, n
         for s in range(half):
-            at = blocks(n * half + s, n * half + s + 1, size)
-            copies.append(pltpu.make_async_copy(matrix_ref.at[start + n, s], same_ref.at[at], sems.at[0]))
-            copies.append(
-                pltpu.make_async_copy(
-                    matrix_ref.at[rows - near - start + n, s], swap_ref.at[at], sems.at[1]
-                )
-            )
+            at = blocks(s, s + 1, size)
+            source = matrix_ref.at[jnp.where(straight, up, down), s]
+            copies.append(pltpu.make_async_copy(source, same_refs[n].at[at], sems.at[0]))
+            source = matrix_ref.at[jnp.where(straight, down, up), s]
+            copies.append(pltpu.make_async_copy(source, swap_refs[n].at[at], sems.at[1]))
     held = pltpu.make_async_copy(columns_ref, copied_ref, sems.at[2])
     held.start()
     for copy in copies:
@@ -81,7 +82,7 @@
     step = jnp.where(column >= 0, step, ABSENT)
     steps[...] = jnp.zeros_like(steps)
     steps[:rows, : column.shape[1]] = step.astype(jnp.float32)
-    same_ref[near * half * size :, :] = steps[...].astype(same_ref.dtype)
+    same_refs[0][half * size :, :] = steps[...].astype(same_refs[0].dtype)
     for copy in copies:
         copy.wait()
 
@@ -94,7 +95,7 @@
     for q in reversed(range(reach, width)):
         index = jnp.where(lax.axis_index("col") == 0, q - reach, width - 1 - q)
         for s in range(2 * half):
-            place = pl.multiple_of(own_place(columns_ref, q, s, width + far) * size, size)
+            place = pl.multiple_of(own_place(columns_ref, q, s, width) * size, size)
             source = own_ref if s < half else other_ref
             panel_ref[blocks(q - reach, q - reach + 1, size), pl.ds(place, size)] = source[index, s % half]
     for p in range(width // 2):
@@ -112,8 +113,8 @@
     size = out_ref.shape[1]
     at = 0
     for f in range(far):
-        row = REACH + f
-        for k in range(2 * REACH, 3 * REACH + 1 + f):
+        row = REACH - 1 - f
+        for k in range(2 * REACH - 1, REACH - 2 - f, -1):
             out_ref[at] = panel_ref[blocks(row, row + 1, size), blocks(k, k + 1, size)]
             at += 1
 
@@ -128,33 +129,40 @@
 
 
 def near_kernel(
-    far, columns_ref, panel_ref, first_ref, near_ref, cross_ref,
-    stay_ref, leave_ref, part_ref, high_ref, cube_ref, lower_ref,
-    square, result, keep_ref, steps, halo_ref, sem
+    far, held_ref, panel_ref, first_ref, *refs
 ):
     reach = REACH
+    same_refs, swap_refs = refs[: reach - far], refs[reach - far : 2 * (reach - far)]
+    (
+        stay_ref, leave_ref, mask_ref, part_ref, high_ref, cube_ref, lower_ref,
+        square, result, keep_ref, columns_ref, steps, halo_ref, sems,
+    ) = refs[2 * (reach - far) :]
     half, size = stay_ref.shape[1], stay_ref.shape[2]
-    steps[...] = near_ref[(reach - far) * half * size :, :].astype(jnp.float32).astype(jnp.int32)
-    copy = pltpu.make_async_copy(steps, halo_ref, sem)
-    copy.start()
+    steps[...] = same_refs[0][half * size :, :].astype(jnp.float32).astype(jnp.int32)
+    copies = [
+        pltpu.make_async_copy(held_ref, columns_ref, sems.at[0]),
+        pltpu.make_async_copy(steps, halo_ref, sems.at[1]),
+    ]
+    for copy in copies:
+        copy.start()
     width = panel_ref.shape[0] // size + reach
     near = reach - far
     low_cols = reach + far
     far_cols = 2 * reach + far
     near_cols = 2 * reach
     flip = lax.axis_index("col")
-    mark_kept(columns_ref, keep_ref, reach)
     lower_ref[...] = jnp.zeros_like(lower_ref)
     result[:, blocks(width, width + 1, size)] = jnp.zeros((near * size, size), result.dtype)
-    copy.wait()
+    for copy in copies:
+        copy.wait()
+    mark_kept(columns_ref, keep_ref, reach)
     for n in range(near):
-        index = jnp.where(flip == 0, n, near - 1 - n)
+        sources = same_refs[near - 1 - n], swap_refs[near - 1 - n]
         for s in range(2 * half):
             place = halo_place(halo_ref, *columns_ref.shape, n + far, s, near_cols)
             place = pl.multiple_of(place * size, size)
-            source = near_ref if s < half else cross_ref
-            at = pl.multiple_of((index * half + s % half) * size, size)
-            lower_ref[blocks(n, n + 1, size), pl.ds(place, size)] = source[pl.ds(at, size)]
+            at = blocks(s % half, s % half + 1, size)
+            lower_ref[blocks(n, n + 1, size), pl.ds(place, size)] = sources[s // half][at, :]
     left = panel_ref.at[blocks(0, reach, size), blocks(far, reach, size)]
     for p in range(width // 2):
         cols = blocks(2 * p, 2 * p + 2, size)
@@ -167,6 +175,8 @@
                 at = (blocks(i, i + 1, size), blocks(k, k + 1, size))
                 if i < far and k < low_cols:
                     part_ref[at] = block
+                    kept = jnp.full((1, size), keep_ref[i, k], jnp.float32)
+                    mask_ref[i * low_cols + k : i * low_cols + k + 1, :] = kept
                     square[at] = jnp.zeros((size, size), square.dtype)
                 elif abs(i + reach - k) <= reach:
                     square[at] = jnp.where(keep_ref[i, k] > 0, block, 0.0).astype(square.dtype)
@@ -176,20 +186,28 @@
         cols = blocks(2 * p, 2 * p + 2, size)
         low = max(reach, 2 * p - reach)
         high = min(width, 2 * p + 2 + reach)
+        rest = slice(far * size, reach * size)
         value = jnp.dot(
-            square[:, blocks(low, high, size)],
+            square[rest, blocks(low, high, size)],
             panel_ref[blocks(low - reach, high - reach, size), cols],
             preferred_element_type=jnp.float32,
         )
         if 2 * p < near_cols:
             value = value + jnp.dot(
-                square[:, blocks(far, reach, size)], lower_ref[:, cols], preferred_element_type=jnp.float32
+                square[rest, blocks(far, reach, size)], lower_ref[:, cols], preferred_element_type=jnp.float32
             )
+        result[:, cols] = (3.0 * square[rest, cols].astype(jnp.float32) - 2.0 * value).astype(result.dtype)
+        low = max(low_cols, 2 * p - reach)
+        high = min(far_cols, 2 * p + 2 + reach)
         if 2 * p < far_cols:
-            cube_ref[:, cols] = value[: far * size]
-        result[:, cols] = (
-            3.0 * square[far * size :, cols].astype(jnp.float32) - 2.0 * value[far * size :]
-        ).astype(result.dtype)
+            if low < high:
+                cube_ref[:, cols] = jnp.dot(
+                    square[: far * size, blocks(low, high, size)],
+                    panel_ref[blocks(low - reach, high - reach, size), cols],
+                    preferred_element_type=jnp.float32,
+                )
+            else:
+                cube_ref[:, cols] = jnp.zeros((far * size, 2 * size), jnp.float32)
     high_ref[...] = square[: far * size, blocks(low_cols, far_cols, size)]
     for i in range(near):
         index = jnp.where(flip == 0, i, near - 1 - i)
@@ -200,16 +218,16 @@
 
 
 def far_kernel(
-    columns_ref, far_ref, part_ref, high_ref, cube_ref, lower_ref, panel_ref, kept_near_ref, got_near_ref,
-    stay_ref, leave_ref, out_ref, farthest, square, result, keep_ref, sems
+    held_ref, mask_ref, part_ref, high_ref, cube_ref, lower_ref, panel_ref, far_ref,
+    stay_ref, leave_ref, farthest, square, result, columns_ref, sem
 ):
     reach, far = REACH, stay_ref.shape[0]
-    copies = placed(kept_near_ref, got_near_ref, out_ref, far, sems)
+    scalars = pltpu.make_async_copy(held_ref, columns_ref, sem)
+    scalars.start()
     half, size = stay_ref.shape[1], stay_ref.shape[2]
     low_cols = reach + far
     far_cols = 2 * reach + far
     near_cols = 2 * reach
-    mark_kept(columns_ref, keep_ref, far)
     at = 0
     for f in range(far):
         for k in range(low_cols):
@@ -229,7 +247,8 @@
                 block = value[blocks(i, i + 1, size), blocks(k - 2 * p, k - 2 * p + 1, size)]
                 here = (blocks(i, i + 1, size), blocks(k, k + 1, size))
                 if abs(i + reach - k) <= reach:
-                    square[here] = jnp.where(keep_ref[i, k] > 0, block, 0.0).astype(square.dtype)
+                    mask = mask_ref[i * low_cols + k : i * low_cols + k + 1, :]
+                    square[here] = jnp.where(mask > 0, block, 0.0).astype(square.dtype)
                 else:
                     square[here] = jnp.zeros((size, size), square.dtype)
     for p in range(far_cols // 2):
@@ -251,38 +270,40 @@
         else:
             kept = high_ref[:, blocks(2 * p - low_cols, 2 * p + 2 - low_cols, size)]
         result[:, cols] = (3.0 * kept.astype(jnp.float32) - 2.0 * value).astype(result.dtype)
+    scalars.wait()
     for i in range(far):
         index = jnp.where(lax.axis_index("col") == 0, i, far - 1 - i)
         for s in range(2 * half):
             place = pl.multiple_of(own_place(columns_ref, i + reach, s, far_cols) * size, size)
             target = stay_ref if s < half else leave_ref
             target[index, s % half] = result[blocks(i, i + 1, size), pl.ds(place, size)]
+
+
+def write_rows(pieces, out_ref, sems):
+    straight = lax.axis_index("col") == 0
+    copies = []
+    for rows_ref, here, there in pieces:
+        for n in range(rows_ref.shape[0]):
+            to = out_ref.at[jnp.where(straight, here, there) + n]
+            copies.append(pltpu.make_async_copy(rows_ref.at[n], to, sems.at[len(copies)]))
+    for copy in copies:
+        copy.start()
     for copy in copies:
         copy.wait()
 
 
-def placed(kept_ref, got_ref, out_ref, inner, sems):
-    rows, count = out_ref.shape[0], kept_ref.shape[0]
-    straight = lax.axis_index("col") == 0
-    low, high = inner, rows - inner - count
-    copies = []
-    for n in range(count):
-        copies.append(
-            pltpu.make_async_copy(
-                kept_ref.at[n], out_ref.at[jnp.where(straight, low, high) + n], sems.at[0]
-            )
-        )
-        copies.append(
-            pltpu.make_async_copy(got_ref.at[n], out_ref.at[jnp.where(straight, high, low) + n], sems.at[1])
-        )
-    for copy in copies:
-        copy.start()
-    return copies
-
-
-def finish_kernel(kept_ref, got_ref, before_ref, out_ref, sems):
-    for copy in placed(kept_ref, got_ref, out_ref, 0, sems):
-        copy.wait()
+def store_kernel(far_ref, near_ref, got_near_ref, out_ref, sems):
+    rows, far, near = out_ref.shape[0], far_ref.shape[0], near_ref.shape[0]
+    pieces = (
+        (far_ref, 0, rows - far),
+        (near_ref, far, rows - far - near),
+        (got_near_ref, rows - far - near, far),
+    )
+    write_rows(pieces, out_ref, sems)
+
+
+def finish_kernel(got_ref, before_ref, out_ref, sems):
+    write_rows(((got_ref, out_ref.shape[0] - got_ref.shape[0], 0),), out_ref, sems)
 
 
 def local(matrix, columns):
@@ -305,16 +326,16 @@
     ]
     beside = [(i, (i + 1) % cols) for i in range(cols)]
     axes = ("row", "col")
-    edge_rows = near * own_slots * size
-    to_same, to_swap, held = pl.pallas_call(
+    edge_rows = own_slots * size
+    edges = pl.pallas_call(
         functools.partial(edge_kernel, near),
         out_shape=(
             jax.ShapeDtypeStruct((edge_rows + TILE, size), dtype),
-            jax.ShapeDtypeStruct((edge_rows, size), dtype),
+            *[jax.ShapeDtypeStruct((edge_rows, size), dtype)] * (2 * near - 1),
             jax.ShapeDtypeStruct(columns.shape, columns.dtype),
         ),
         in_specs=[HBM, HBM],
-        out_specs=(VMEM, VMEM, VMEM),
+        out_specs=(VMEM,) * (2 * near + 1),
         scratch_shapes=[pltpu.VMEM((TILE, size), jnp.float32), pltpu.SemaphoreType.DMA((3,))],
         compiler_params=limit(1),
         cost_estimate=LIGHT,
@@ -323,14 +344,17 @@
         pltpu.with_memory_space_constraint(columns, pltpu.HBM),
         pltpu.with_memory_space_constraint(matrix, pltpu.HBM),
     )
-    near_rows = lax.ppermute(to_same, axes, same)
-    cross_rows = lax.ppermute(to_swap, axes, swap)
+    held = edges[-1]
+    near_rows, cross_rows = [], []
+    for n in range(near):
+        near_rows.append(lax.ppermute(edges[n], axes, same))
+        cross_rows.append(lax.ppermute(edges[near + n], axes, swap))
     other = lax.ppermute(matrix, "col", beside)
 
     panel, first_part = pl.pallas_call(
         functools.partial(base_kernel, far),
         out_shape=(
-            jax.ShapeDtypeStruct((local_rows * size, (width + far + 1) * size), dtype),
+            jax.ShapeDtypeStruct((local_rows * size, (width + 1) * size), dtype),
             jax.ShapeDtypeStruct((reach * size, width * size), jnp.float32),
         ),
         in_specs=[SMEM, VMEM, VMEM],
@@ -347,65 +371,77 @@
         compiler_params=limit(1),
         cost_estimate=LIGHT,
         name="pack",
-    )(panel, cross_rows)
-    far_blocks = lax.ppermute(packed, axes, same)
+    )(panel, held)
+    far_blocks = lax.ppermute(packed, axes, swap)
 
     rows_out = jax.ShapeDtypeStruct((near, own_slots, size, size), dtype)
-    stay_near, leave_near, part, high, cube, lower = pl.pallas_call(
+    stay_near, leave_near, mask, part, high, cube, lower = pl.pallas_call(
         functools.partial(near_kernel, far),
         out_shape=(
             rows_out,
             rows_out,
+            jax.ShapeDtypeStruct((far * low_cols, size), jnp.float32),
             jax.ShapeDtypeStruct((far * size, low_cols * size), jnp.float32),
             jax.ShapeDtypeStruct((far * size, (far_cols - low_cols) * size), dtype),
             jax.ShapeDtypeStruct((far * size, far_cols * size), jnp.float32),
             jax.ShapeDtypeStruct((near * size, (near_cols + 1) * size), dtype),
         ),
-        in_specs=[SMEM] + [VMEM] * 4,
-        out_specs=(VMEM,) * 6,
+        in_specs=[VMEM] * (3 + 2 * near),
+        out_specs=(VMEM,) * 7,
         scratch_shapes=[
             pltpu.VMEM((reach * size, width * size), dtype),
             pltpu.VMEM((near * size, (width + 1) * size), dtype),
             pltpu.SMEM((reach, width + 1), jnp.int32),
+            pltpu.SMEM(columns.shape, columns.dtype),
             pltpu.VMEM((TILE, size), jnp.int32),
             pltpu.SMEM((TILE, size), jnp.int32),
-            pltpu.SemaphoreType.DMA,
+            pltpu.SemaphoreType.DMA((2,)),
         ],
         compiler_params=limit(16),
         cost_estimate=HEAVY,
         name="near",
-    )(held, panel, first_part, near_rows, cross_rows)
+    )(held, panel, first_part, *near_rows, *cross_rows)
     arrived_near = lax.ppermute(leave_near, "col", beside)
 
     far_out = jax.ShapeDtypeStruct((far, own_slots, size, size), dtype)
-    stay_far, leave_far, out = pl.pallas_call(
+    stay_far, leave_far = pl.pallas_call(
         far_kernel,
-        out_shape=(far_out, far_out, jax.ShapeDtypeStruct(matrix.shape, dtype)),
-        in_specs=[SMEM] + [VMEM] * 8,
-        out_specs=(VMEM, VMEM, HBM),
+        out_shape=(far_out, far_out),
+        in_specs=[VMEM] * 8,
+        out_specs=(VMEM, VMEM),
         scratch_shapes=[
             pltpu.VMEM((far * size, low_cols * size), dtype),
             pltpu.VMEM((far * size, low_cols * size), dtype),
             pltpu.VMEM((far * size, (far_cols + 1) * size), dtype),
-            pltpu.SMEM((far, width + 1), jnp.int32),
-            pltpu.SemaphoreType.DMA((2,)),
+            pltpu.SMEM(columns.shape, columns.dtype),
+            pltpu.SemaphoreType.DMA,
         ],
         compiler_params=limit(16),
         cost_estimate=LIGHT,
         name="far",
-    )(held, far_blocks, part, high, cube, lower, panel, stay_near, arrived_near)
+    )(held, mask, part, high, cube, lower, panel, far_blocks)
     arrived_far = lax.ppermute(leave_far, "col", beside)
+    out = pl.pallas_call(
+        store_kernel,
+        out_shape=jax.ShapeDtypeStruct(matrix.shape, dtype),
+        in_specs=[VMEM] * 3,
+        out_specs=HBM,
+        scratch_shapes=[pltpu.SemaphoreType.DMA((far + 2 * near,))],
+        compiler_params=limit(1),
+        cost_estimate=LIGHT,
+        name="store",
+    )(stay_far, stay_near, arrived_near)
     return pl.pallas_call(
         finish_kernel,
         out_shape=jax.ShapeDtypeStruct(matrix.shape, dtype),
-        in_specs=[VMEM, VMEM, HBM],
+        in_specs=[VMEM, HBM],
         out_specs=HBM,
-        input_output_aliases={2: 0},
-        scratch_shapes=[pltpu.SemaphoreType.DMA((2,))],
+        input_output_aliases={1: 0},
+        scratch_shapes=[pltpu.SemaphoreType.DMA((far,))],
         compiler_params=limit(1),
         cost_estimate=LIGHT,
         name="finish",
-    )(stay_far, arrived_far, out)
+    )(arrived_far, out)
 
 
 def solution(mesh):

time: 31.7 us -> 29.3 us (0.924)
  waiting for transfers between devices: 8.14 us -> 2.77 us
  starting transfers between devices: 11.7 us -> 15.8 us
  Pallas kernels: 10.4 us -> 9.22 us
    ppermute x3 -> x5, waiting for transfers between devices: 5.46 us -> 2.53 us  [the longest x1 2.52 us: local(): far_blocks = lax.ppermute(packed, axes, swap)]
    ppermute x1, starting transfers between devices: 0.6 us -> 2.43 us  [local(): arrived_far = lax.ppermute(leave_far, 'col', beside)]
    ppermute x1, waiting for transfers between devices: 1.52 us -> 0.01 us  [local(): arrived_near = lax.ppermute(leave_near, 'col', beside)]
    ppermute x1, starting transfers between devices: 0.07 us -> 1.35 us  [local(): arrived_near = lax.ppermute(leave_near, 'col', beside)]
    ppermute x3 -> x5, starting transfers between devices: 10.5 us -> 11.6 us  [the longest x2 4.44 us: local(): cross_rows.append(lax.ppermute(edges[near + n], axes, swap))]
    ppermute x1, waiting for transfers between devices: 1.16 us -> 0.23 us  [local(): arrived_far = lax.ppermute(leave_far, 'col', beside)]
    pallas_call x1, Pallas kernels: 3.58 us -> 2.76 us  [local(): pl.pallas_call(functools.partial(near_kernel, far), out_shape=(rows_out,...]
    pallas_call x1 -> x2, Pallas kernels: 2.22 us -> 2 us  [the longest x1 1.08 us: local(): pl.pallas_call(far_kernel, out_shape=(far_out, far_out), in_specs=[VMEM]...]
  transfers between devices with their start and end apart: 6 -> 8, of which waited for: 4 -> 2; matrix products, arithmetic and copies ran while one was open for 0% -> 0% of each run, Pallas kernels for 23% -> 29%
where the time goes in v4:
time: 29.3 us; the launch traced here: 29.1 us
  starting transfers between devices  15.8 us (54%)
  Pallas kernels  9.22 us (31%)
  waiting for transfers between devices  2.77 us (9%)
  local copies, waits for them, and re-layouts  1.23 us (4%)
    ppermute x2, starting transfers between devices, local(): cross_rows.append(lax.ppermute(edges[near + n], axes, swap))  4.44 us
    ppermute x2, starting transfers between devices, local(): near_rows.append(lax.ppermute(edges[n], axes, same))  4.09 us
    ppermute x1, starting transfers between devices, local(): far_blocks = lax.ppermute(packed, axes, swap)  3.05 us
    pallas_call x1, Pallas kernels, local(): pl.pallas_call(functools.partial(near_kernel, far), out_shape=(rows_out,...  2.76 us
    pallas_call x1, Pallas kernels, local(): pl.pallas_call(functools.partial(base_kernel, far), out_shape=(jax.ShapeD...  2.65 us
    ppermute x1, waiting for transfers between devices, local(): far_blocks = lax.ppermute(packed, axes, swap)  2.52 us
    ppermute x1, starting transfers between devices, local(): arrived_far = lax.ppermute(leave_far, 'col', beside)  2.43 us
    ppermute x1, starting transfers between devices, local(): arrived_near = lax.ppermute(leave_near, 'col', beside)  1.35 us
  transfers between devices with their start and end apart: 8, of which 2 were waited for; matrix products, arithmetic and copies ran while one was open for 0% of the time, Pallas kernels for 29%

profile of v4, /device:TPU:0, one launch (start us, length us, event | category | flops | bytes accessed | tf_op | source)
XLA Modules:
  0.0 29.1 jit_solution(11420402911456574512)
XLA Ops:
  0.0 0.5 %collective-permute-start = (bf16[8,4,128,128]{3,2,1,0:T(8,128)(2,1)}, bf16[8,4,128,128]{3,2,1,0:T(8,128)(2,1)S(1)}, u32[]{:S(2)}, u32[]{:S(2)}) collective-permute-start(bf16[8,4,128,128]{3,2,1,0:T(8,128)(2,1)} %own_ref.1), channel_id=1, source_target_pairs={{0,1},{1,0},{2,3},{3,2},{4,5},{5,4},{6,7},{7,6},{8,9},{9,8},{10,11... | collective-permute-start | bytes 3145736 | tf_op jit(solution)/shard_map/ppermute | solution.py:352
  0.5 1.0 %edge.1 = (bf16[528,128]{1,0:T(8,128)(2,1)S(1)}, bf16[512,128]{1,0:T(8,128)(2,1)S(1)}, bf16[512,128]{1,0:T(8,128)(2,1)S(1)}, bf16[512,128]{1,0:T(8,128)(2,1)S(1)}, s32[8,8]{1,0:T(8,128)S(1)}) custom-call(s32[8,8]{1,0:T(8,128)} %columns_ref.1, bf16[8,4,128,128]{3,2,1,0:T(8,128)(2,1)} %own_ref.1), custom_call_target="tpu_custom_call" | custom-call | tf_op jit(solution)/shard_map/edge/pallas_call | solution.py:330
  1.5 2.6 %collective-permute-start.1 = (bf16[528,128]{1,0:T(8,128)(2,1)S(1)}, bf16[528,128]{1,0:T(8,128)(2,1)S(1)}, u32[]{:S(2)}, u32[]{:S(2)}) collective-permute-start(bf16[528,128]{1,0:T(8,128)(2,1)S(1)} %get-tuple-element.24), channel_id=1, source_target_pairs={{0,2},{2,4},{4,6},{6,8},{8,10},{10,12},{12,14},{14,0},{1,15},{3,1}... | collective-permute-start | bytes 405512 | tf_op jit(solution)/shard_map/ppermute | solution.py:350
  4.1 1.5 %collective-permute-start.2 = (bf16[512,128]{1,0:T(8,128)(2,1)S(1)}, bf16[512,128]{1,0:T(8,128)(2,1)S(1)}, u32[]{:S(2)}, u32[]{:S(2)}) collective-permute-start(bf16[512,128]{1,0:T(8,128)(2,1)S(1)} %get-tuple-element.25), channel_id=1, source_target_pairs={{0,2},{2,4},{4,6},{6,8},{8,10},{10,12},{12,14},{14,0},{1,15},{3,1}... | collective-permute-start | bytes 393224 | tf_op jit(solution)/shard_map/ppermute | solution.py:350
  5.6 3.0 %collective-permute-start.3 = (bf16[512,128]{1,0:T(8,128)(2,1)S(1)}, bf16[512,128]{1,0:T(8,128)(2,1)S(1)}, u32[]{:S(2)}, u32[]{:S(2)}) collective-permute-start(bf16[512,128]{1,0:T(8,128)(2,1)S(1)} %get-tuple-element.26), channel_id=1, source_target_pairs={{1,2},{3,4},{5,6},{7,8},{9,10},{11,12},{13,14},{15,0},{0,15},{2,1}... | collective-permute-start | bytes 393224 | tf_op jit(solution)/shard_map/ppermute | solution.py:351
  8.6 1.5 %collective-permute-start.4 = (bf16[512,128]{1,0:T(8,128)(2,1)S(1)}, bf16[512,128]{1,0:T(8,128)(2,1)S(1)}, u32[]{:S(2)}, u32[]{:S(2)}) collective-permute-start(bf16[512,128]{1,0:T(8,128)(2,1)S(1)} %get-tuple-element.27), channel_id=1, source_target_pairs={{1,2},{3,4},{5,6},{7,8},{9,10},{11,12},{13,14},{15,0},{0,15},{2,1}... | collective-permute-start | bytes 393224 | tf_op jit(solution)/shard_map/ppermute | solution.py:351
  10.0 0.0 collective-permute-done.other_ref
  10.0 1.2 %copy-done = bf16[8,4,128,128]{3,2,1,0:T(8,128)(2,1)S(1)} copy-done((bf16[8,4,128,128]{3,2,1,0:T(8,128)(2,1)S(1)}, bf16[8,4,128,128]{3,2,1,0:T(8,128)(2,1)}, u32[]{:S(2)}) %copy-start) | copy-done | bytes 1048600
  11.3 2.6 %base.1 = (bf16[1024,1664]{1,0:T(8,128)(2,1)S(1)}, f32[512,1536]{1,0:T(8,128)S(1)}) custom-call(s32[8,8]{1,0:T(8,128)S(1)} %get-tuple-element.21.columns_ref.held_ref.after_ref, bf16[8,4,128,128]{3,2,1,0:T(8,128)(2,1)S(1)} %copy-done, bf16[8,4,128,128]{3,2,1,0:T(8,128)(2,1)S(1)} %collective-permute-done.other_ref), custom_call_target="tpu_custom_call" | custom-call | tf_op jit(solution)/shard_map/base/pallas_call | solution.py:354
  13.9 0.1 pack.1
  14.0 3.0 %collective-permute-start.5 = (bf16[11,128,128]{2,1,0:T(8,128)(2,1)S(1)}, bf16[11,128,128]{2,1,0:T(8,128)(2,1)S(1)}, u32[]{:S(2)}, u32[]{:S(2)}) collective-permute-start(bf16[11,128,128]{2,1,0:T(8,128)(2,1)S(1)} %pack.1), channel_id=1, source_target_pairs={{1,2},{3,4},{5,6},{7,8},{9,10},{11,12},{13,14},{15,0},{0,15},{2,1}... | collective-permute-start | bytes 1081352 | tf_op jit(solution)/shard_map/ppermute | solution.py:375
  17.0 0.0 collective-permute-done.2.refs_1_
  17.0 0.0 collective-permute-done.3.refs_2_
  17.0 0.0 collective-permute-done.4.refs_3_
  17.0 0.0 collective-permute-done.1.refs_0_
  17.0 2.8 %near.1 = (bf16[2,4,128,128]{3,2,1,0:T(8,128)(2,1)S(1)}, bf16[2,4,128,128]{3,2,1,0:T(8,128)(2,1)S(1)}, f32[12,128]{1,0:T(8,128)S(1)}, f32[256,768]{1,0:T(8,128)S...) custom-call(s32[8,8]{1,0:T(8,128)S(1)} %get-tuple-element.21.columns_ref.held_ref.after_re, ...), custom_call_target="tpu_custom_call" | custom-call | flops 20000000000 | tf_op jit(solution)/shard_map/near/pallas_call | solution.py:378
  19.8 1.4 %collective-permute-start.7 = (bf16[2,4,128,128]{3,2,1,0:T(8,128)(2,1)S(1)}, bf16[2,4,128,128]{3,2,1,0:T(8,128)(2,1)S(1)}, u32[]{:S(2)}, u32[]{:S(2)}) collective-permute-start(bf16[2,4,128,128]{3,2,1,0:T(8,128)(2,1)S(1)} %get-tuple-element.36), channel_id=1, source_target_pairs={{0,1},{1,0},{2,3},{3,2},{4,5},{5,4},{6,7},{7,6},{8,9},{9,8},{10,11... | collective-permute-start | bytes 786440 | tf_op jit(solution)/shard_map/ppermute | solution.py:404
  21.2 2.5 %collective-permute-done.5.far_ref = bf16[11,128,128]{2,1,0:T(8,128)(2,1)S(1)} collective-permute-done((bf16[11,128,128]{2,1,0:T(8,128)(2,1)S(1)}, bf16[11,128,128]{2,1,0:T(8,128)(2,1)S(1)}, u32[]{:S(2)}, u32[]{:S(2)}) %collective-permute-start.5) | collective-permute-done | bytes 360480 | tf_op jit(solution)/shard_map/ppermute | solution.py:375
  23.7 1.1 %far.1 = (bf16[2,4,128,128]{3,2,1,0:T(8,128)(2,1)S(1)}, bf16[2,4,128,128]{3,2,1,0:T(8,128)(2,1)S(1)}) custom-call(s32[8,8]{1,0:T(8,128)S(1)} %get-tuple-element.21.columns_ref.held_ref.after_ref, f32[12,128]{1,0:T(8,128)S(1)} %get-tuple-element.28.mask_ref, f32[256,768]{1,0:T(8,128)S(1)} %get-tuple-element.29.part_ref, ...), custom_call_target="tpu_custom_call" | custom-call | tf_op jit(solution)/shard_map/far/pallas_call | solution.py:407
  24.8 2.4 %collective-permute-start.6 = (bf16[2,4,128,128]{3,2,1,0:T(8,128)(2,1)S(1)}, bf16[2,4,128,128]{3,2,1,0:T(8,128)(2,1)S(1)}, u32[]{:S(2)}, u32[]{:S(2)}) collective-permute-start(bf16[2,4,128,128]{3,2,1,0:T(8,128)(2,1)S(1)} %get-tuple-element.33), channel_id=1, source_target_pairs={{0,1},{1,0},{2,3},{3,2},{4,5},{5,4},{6,7},{7,6},{8,9},{9,8},{10,11... | collective-permute-start | bytes 786440 | tf_op jit(solution)/shard_map/ppermute | solution.py:423
  27.2 0.0 collective-permute-done.7.got_near_ref
  27.2 0.9 %store.1.before_ref = bf16[8,4,128,128]{3,2,1,0:T(8,128)(2,1)} custom-call(bf16[2,4,128,128]{3,2,1,0:T(8,128)(2,1)S(1)} %get-tuple-element.34.far_ref, bf16[2,4,128,128]{3,2,1,0:T(8,128)(2,1)S(1)} %get-tuple-element.35.near_ref, bf16[2,4,128,128]{3,2,1,0:T(8,128)(2,1)S(1)} %collective-permute-done.7.got_near_ref), custom_call_target="tpu_custom_call" | custom-call | tf_op jit(solution)/shard_map/store/pallas_call | solution.py:424
  28.1 0.2 collective-permute-done.6.got_ref
  28.4 0.7 %finish.1 = bf16[8,4,128,128]{3,2,1,0:T(8,128)(2,1)} custom-call(bf16[2,4,128,128]{3,2,1,0:T(8,128)(2,1)S(1)} %collective-permute-done.6.got_ref, bf16[8,4,128,128]{3,2,1,0:T(8,128)(2,1)} %store.1.before_ref), custom_call_target="tpu_custom_call", output_to_operand_aliasing={{}: (1, {})} | custom-call | tf_op jit(solution)/shard_map/finish/pallas_call | solution.py:434
  (1 shorter events, 0.0 us)
Async XLA Ops:
  0.0 10.0 %collective-permute-start = (bf16[8,4,128,128]{3,2,1,0:T(8,128)(2,1)}, bf16[8,4,128,128]{3,2,1,0:T(8,128)(2,1)S(1)}, u32[]{:S(2)}, u32[]{:S(2)}) collective-permute-start(bf16[8,4,128,128]{3,2,1,0:T(8,128)(2,1)} %own_ref.1), channel_id=1, source_target_pairs={{0,1},{1,0},{2,3},{3,2},{4,5},{5,4},{6,7},{7,6},{8,9},{9,8},{10,11... | collective-permute-start | bytes 3145736 | tf_op jit(solution)/shard_map/ppermute | solution.py:352
  1.5 15.5 %collective-permute-start.1 = (bf16[528,128]{1,0:T(8,128)(2,1)S(1)}, bf16[528,128]{1,0:T(8,128)(2,1)S(1)}, u32[]{:S(2)}, u32[]{:S(2)}) collective-permute-start(bf16[528,128]{1,0:T(8,128)(2,1)S(1)} %get-tuple-element.24), channel_id=1, source_target_pairs={{0,2},{2,4},{4,6},{6,8},{8,10},{10,12},{12,14},{14,0},{1,15},{3,1}... | collective-permute-start | bytes 405512 | tf_op jit(solution)/shard_map/ppermute | solution.py:350
  4.1 13.0 %collective-permute-start.2 = (bf16[512,128]{1,0:T(8,128)(2,1)S(1)}, bf16[512,128]{1,0:T(8,128)(2,1)S(1)}, u32[]{:S(2)}, u32[]{:S(2)}) collective-permute-start(bf16[512,128]{1,0:T(8,128)(2,1)S(1)} %get-tuple-element.25), channel_id=1, source_target_pairs={{0,2},{2,4},{4,6},{6,8},{8,10},{10,12},{12,14},{14,0},{1,15},{3,1}... | collective-permute-start | bytes 393224 | tf_op jit(solution)/shard_map/ppermute | solution.py:350
  5.6 11.4 %collective-permute-start.3 = (bf16[512,128]{1,0:T(8,128)(2,1)S(1)}, bf16[512,128]{1,0:T(8,128)(2,1)S(1)}, u32[]{:S(2)}, u32[]{:S(2)}) collective-permute-start(bf16[512,128]{1,0:T(8,128)(2,1)S(1)} %get-tuple-element.26), channel_id=1, source_target_pairs={{1,2},{3,4},{5,6},{7,8},{9,10},{11,12},{13,14},{15,0},{0,15},{2,1}... | collective-permute-start | bytes 393224 | tf_op jit(solution)/shard_map/ppermute | solution.py:351
  8.6 8.5 %collective-permute-start.4 = (bf16[512,128]{1,0:T(8,128)(2,1)S(1)}, bf16[512,128]{1,0:T(8,128)(2,1)S(1)}, u32[]{:S(2)}, u32[]{:S(2)}) collective-permute-start(bf16[512,128]{1,0:T(8,128)(2,1)S(1)} %get-tuple-element.27), channel_id=1, source_target_pairs={{1,2},{3,4},{5,6},{7,8},{9,10},{11,12},{13,14},{15,0},{0,15},{2,1}... | collective-permute-start | bytes 393224 | tf_op jit(solution)/shard_map/ppermute | solution.py:351
  10.0 1.2 %copy-start = (bf16[8,4,128,128]{3,2,1,0:T(8,128)(2,1)S(1)}, bf16[8,4,128,128]{3,2,1,0:T(8,128)(2,1)}, u32[]{:S(2)}) copy-start(bf16[8,4,128,128]{3,2,1,0:T(8,128)(2,1)} %own_ref.1) | copy-start | bytes 3145732
  14.0 9.7 %collective-permute-start.5 = (bf16[11,128,128]{2,1,0:T(8,128)(2,1)S(1)}, bf16[11,128,128]{2,1,0:T(8,128)(2,1)S(1)}, u32[]{:S(2)}, u32[]{:S(2)}) collective-permute-start(bf16[11,128,128]{2,1,0:T(8,128)(2,1)S(1)} %pack.1), channel_id=1, source_target_pairs={{1,2},{3,4},{5,6},{7,8},{9,10},{11,12},{13,14},{15,0},{0,15},{2,1}... | collective-permute-start | bytes 1081352 | tf_op jit(solution)/shard_map/ppermute | solution.py:375
  19.8 7.4 %collective-permute-start.7 = (bf16[2,4,128,128]{3,2,1,0:T(8,128)(2,1)S(1)}, bf16[2,4,128,128]{3,2,1,0:T(8,128)(2,1)S(1)}, u32[]{:S(2)}, u32[]{:S(2)}) collective-permute-start(bf16[2,4,128,128]{3,2,1,0:T(8,128)(2,1)S(1)} %get-tuple-element.36), channel_id=1, source_target_pairs={{0,1},{1,0},{2,3},{3,2},{4,5},{5,4},{6,7},{7,6},{8,9},{9,8},{10,11... | collective-permute-start | bytes 786440 | tf_op jit(solution)/shard_map/ppermute | solution.py:404
  24.8 3.6 %collective-permute-start.6 = (bf16[2,4,128,128]{3,2,1,0:T(8,128)(2,1)S(1)}, bf16[2,4,128,128]{3,2,1,0:T(8,128)(2,1)S(1)}, u32[]{:S(2)}, u32[]{:S(2)}) collective-permute-start(bf16[2,4,128,128]{3,2,1,0:T(8,128)(2,1)S(1)} %get-tuple-element.33), channel_id=1, source_target_pairs={{0,1},{1,0},{2,3},{3,2},{4,5},{5,4},{6,7},{7,6},{8,9},{9,8},{10,11... | collective-permute-start | bytes 786440 | tf_op jit(solution)/shard_map/ppermute | solution.py:423

commit v5 on v4

v5 whole, which is shorter than its diff:
```python
import functools

import jax
import jax.numpy as jnp
from jax import lax
from jax.experimental import pallas as pl
from jax.experimental.pallas import tpu as pltpu
from jax.sharding import PartitionSpec as P

REACH = 4
HEAD = 1
MIB = 1024 * 1024
ABSENT = 64
TILE = 16

HEAVY = pl.CostEstimate(flops=20_000_000_000, bytes_accessed=0, transcendentals=0)
LIGHT = pl.CostEstimate(flops=0, bytes_accessed=0, transcendentals=0)

SMEM = pl.BlockSpec(memory_space=pltpu.SMEM)
VMEM = pl.BlockSpec(memory_space=pltpu.VMEM)
ANY = pl.BlockSpec(memory_space=pl.ANY)
HBM = pl.BlockSpec(memory_space=pltpu.HBM)


def limit(mib):
    return pltpu.CompilerParams(vmem_limit_bytes=mib * MIB)


def blocks(first, last, size):
    return slice(first * size, last * size)


def own_place(columns_ref, q, s, limit):
    rows, slots = columns_ref.shape
    flip = lax.axis_index("col")
    row = jnp.where(flip == 0, q - REACH, rows + REACH - 1 - q)
    slot = lax.rem(s + flip * (slots // 2), slots)
    total = rows * lax.axis_size("row")
    column = columns_ref[row, slot]
    step = column - lax.axis_index("row") * rows - row
    step = jnp.where(step > REACH, step - total, step)
    step = jnp.where(step < -REACH, step + total, step)
    place = jnp.where(flip == 0, q + step, q - step)
    inside = (column >= 0) & (place >= 0) & (place < limit)
    return jnp.where(inside, place, limit)


def halo_place(steps_ref, rows, slots, q, s, limit):
    flip = lax.axis_index("col")
    row = jnp.where(flip == 0, rows - REACH + q, REACH - 1 - q)
    slot = lax.rem(s + flip * (slots // 2), slots)
    step = steps_ref[row, slot]
    place = jnp.where(flip == 0, q + step, q - step)
    inside = (step <= REACH) & (place >= 0) & (place < limit)
    return jnp.where(inside, place, limit)


def edge_kernel(near, columns_ref, matrix_ref, *refs):
    rows, half, size = matrix_ref.shape[:3]
    same_refs, swap_refs = refs[:near], refs[near : 2 * near]
    copied_ref, steps, sems = refs[2 * near :]
    straight = lax.axis_index("col") == 0
    copies = []
    for n in range(near):
        up, down = rows - 1 - n, n
        for s in range(half):
            at = blocks(s, s + 1, size)
            source = matrix_ref.at[jnp.where(straight, up, down), s]
            copies.append(pltpu.make_async_copy(source, same_refs[n].at[at], sems.at[0]))
            source = matrix_ref.at[jnp.where(straight, down, up), s]
            copies.append(pltpu.make_async_copy(source, swap_refs[n].at[at], sems.at[1]))
    held = pltpu.make_async_copy(columns_ref, copied_ref, sems.at[2])
    held.start()
    for copy in copies:
        copy.start()
    held.wait()
    column = copied_ref[...]
    row = lax.broadcasted_iota(jnp.int32, column.shape, 0) + lax.axis_index("row") * rows
    total = rows * lax.axis_size("row")
    step = column - row
    step = jnp.where(step > REACH, step - total, step)
    step = jnp.where(step < -REACH, step + total, step)
    step = jnp.where(column >= 0, step, ABSENT)
    steps[...] = jnp.zeros_like(steps)
    steps[:rows, : column.shape[1]] = step.astype(jnp.float32)
    same_refs[0][half * size :, :] = steps[...].astype(same_refs[0].dtype)
    for copy in copies:
        copy.wait()


def pack_kernel(far, held_ref, matrix_ref, other_ref, mid_ref, last_ref, own, columns_ref, sems):
    rows, half = other_ref.shape[:2]
    lead = own.shape[0]
    straight = lax.axis_index("col") == 0
    start = jnp.where(straight, REACH - lead, rows - REACH)
    copies = [
        pltpu.make_async_copy(held_ref, columns_ref, sems.at[0]),
        pltpu.make_async_copy(matrix_ref.at[pl.ds(start, lead)], own, sems.at[1]),
    ]
    for copy in copies:
        copy.start()
    mid_ref[...] = jnp.zeros_like(mid_ref)
    last_ref[...] = jnp.zeros_like(last_ref)
    for copy in copies:
        copy.wait()
    base = 0
    for f in range(lead):
        if f == far:
            base = 0
        out_ref = last_ref if f < far else mid_ref
        q = 2 * REACH - 1 - f
        index = jnp.where(straight, lead - 1 - f, f)
        count = REACH + 1 + f
        for s in range(2 * half):
            place = 2 * REACH - 1 - own_place(columns_ref, q, s, 2 * REACH + 1)

            @pl.when((place >= 0) & (place < count))
            def _(place=place, index=index, s=s, base=base, out_ref=out_ref):
                if s < half:
                    out_ref[base + place] = own[index, s]
                else:
                    out_ref[base + place] = other_ref[start + index, s - half]
        base += count


def base_kernel(
    held_ref, matrix_ref, other_ref, same_ref, swap_ref, panel_ref, first_ref, mask_ref,
    own_ref, columns_ref, keep_ref, steps, halo_ref, sems
):
    rows, half, size = own_ref.shape[0], own_ref.shape[1], own_ref.shape[2]
    reach = REACH
    width = rows + reach
    lead = reach - HEAD
    steps[...] = same_ref[half * size :, :].astype(jnp.float32).astype(jnp.int32)
    copies = [
        pltpu.make_async_copy(held_ref, columns_ref, sems.at[0]),
        pltpu.make_async_copy(steps, halo_ref, sems.at[1]),
        pltpu.make_async_copy(matrix_ref, own_ref, sems.at[2]),
    ]
    for copy in copies:
        copy.start()
    panel_ref[...] = jnp.zeros_like(panel_ref)
    for copy in copies:
        copy.wait()
    for s in range(2 * half):
        place = halo_place(halo_ref, rows, 2 * half, lead, s, width)
        place = pl.multiple_of(place * size, size)
        source = same_ref if s < half else swap_ref
        panel_ref[blocks(lead, lead + 1, size), pl.ds(place, size)] = source[
            blocks(s % half, s % half + 1, size), :
        ]
    for q in range(reach, width):
        index = jnp.where(lax.axis_index("col") == 0, q - reach, width - 1 - q)
        for s in range(2 * half):
            place = pl.multiple_of(own_place(columns_ref, q, s, width) * size, size)
            source = own_ref if s < half else other_ref
            panel_ref[blocks(q, q + 1, size), pl.ds(place, size)] = source[index, s % half]
    for i in range(reach):
        for k in range(width + 1):
            keep_ref[i, k] = 0
        for s in range(2 * half):
            keep_ref[i, own_place(columns_ref, i + reach, s, width)] = 1
        for k in range(width):
            at = i * width + k
            mask_ref[at : at + 1, :] = jnp.full((1, size), keep_ref[i, k], jnp.float32)
    for p in range(width // 2):
        low = max(lead, 2 * p - reach)
        high = min(width, 2 * p + 2 + reach)
        cols = blocks(2 * p, 2 * p + 2, size)
        first_ref[:, cols] = jnp.dot(
            panel_ref[blocks(reach, 2 * reach, size), blocks(low, high, size)],
            panel_ref[blocks(low, high, size), cols],
            preferred_element_type=jnp.float32,
        )


def keep_block(mask_ref, i, k, width, block, dtype):
    if abs(i + REACH - k) > REACH:
        return jnp.zeros(block.shape, dtype)
    return jnp.where(mask_ref[i * width + k : i * width + k + 1, :] > 0, block, 0.0).astype(dtype)


def near_kernel(
    far, held_ref, mask_ref, first_ref, mid_ref, before_ref,
    panel_ref, stay_ref, leave_ref, part_ref, high_ref, cube_ref, square, result, columns_ref, sem
):
    reach = REACH
    lead = reach - HEAD
    scalars = pltpu.make_async_copy(held_ref, columns_ref, sem)
    scalars.start()
    half, size = stay_ref.shape[1], stay_ref.shape[2]
    width = panel_ref.shape[0] // size
    near = reach - far
    low_cols = reach + far
    far_cols = 2 * reach + far
    near_cols = 2 * reach
    at = 0
    for q in range(far, lead):
        for k in range(reach + 1 + q):
            panel_ref[blocks(q, q + 1, size), blocks(k, k + 1, size)] = mid_ref[at]
            at += 1
    result[:, blocks(width, width + 1, size)] = jnp.zeros((near * size, size), result.dtype)
    left = panel_ref[blocks(reach, 2 * reach, size), blocks(far, lead, size)]
    for p in range(width // 2):
        cols = blocks(2 * p, 2 * p + 2, size)
        value = first_ref[:, cols]
        if 2 * p < near_cols:
            value = value + jnp.dot(
                left, panel_ref[blocks(far, lead, size), cols], preferred_element_type=jnp.float32
            )
        for i in range(reach):
            for k in (2 * p, 2 * p + 1):
                block = value[blocks(i, i + 1, size), blocks(k - 2 * p, k - 2 * p + 1, size)]
                here = (blocks(i, i + 1, size), blocks(k, k + 1, size))
                if i < far and k < low_cols:
                    part_ref[here] = block
                    square[here] = jnp.zeros((size, size), square.dtype)
                else:
                    square[here] = keep_block(mask_ref, i, k, width, block, square.dtype)
    rest = slice(far * size, reach * size)
    for p in range(width // 2):
        cols = blocks(2 * p, 2 * p + 2, size)
        low = max(far, 2 * p - reach)
        high = min(width, 2 * p + 2 + reach)
        value = jnp.dot(
            square[rest, blocks(low, high, size)],
            panel_ref[blocks(low, high, size), cols],
            preferred_element_type=jnp.float32,
        )
        result[:, cols] = (3.0 * square[rest, cols].astype(jnp.float32) - 2.0 * value).astype(result.dtype)
        low = max(low_cols, 2 * p - reach)
        high = min(far_cols, 2 * p + 2 + reach)
        if 2 * p < far_cols:
            if low < high:
                cube_ref[:, cols] = jnp.dot(
                    square[: far * size, blocks(low, high, size)],
                    panel_ref[blocks(low, high, size), cols],
                    preferred_element_type=jnp.float32,
                )
            else:
                cube_ref[:, cols] = jnp.zeros((far * size, 2 * size), jnp.float32)
    high_ref[...] = square[: far * size, blocks(low_cols, far_cols, size)]
    scalars.wait()
    for i in range(near):
        index = jnp.where(lax.axis_index("col") == 0, i, near - 1 - i)
        for s in range(2 * half):
            place = pl.multiple_of(own_place(columns_ref, i + reach + far, s, width) * size, size)
            target = stay_ref if s < half else leave_ref
            target[index, s % half] = result[blocks(i, i + 1, size), pl.ds(place, size)]


def far_kernel(
    held_ref, mask_ref, part_ref, high_ref, cube_ref, far_ref, before_ref,
    panel_ref, stay_ref, leave_ref, square, result, columns_ref, sem
):
    reach, far = REACH, stay_ref.shape[0]
    scalars = pltpu.make_async_copy(held_ref, columns_ref, sem)
    scalars.start()
    half, size = stay_ref.shape[1], stay_ref.shape[2]
    width = panel_ref.shape[0] // size
    low_cols = reach + far
    far_cols = 2 * reach + far
    at = 0
    for f in range(far):
        for k in range(reach + 1 + f):
            panel_ref[blocks(f, f + 1, size), blocks(k, k + 1, size)] = far_ref[at]
            at += 1
    result[:, blocks(far_cols, far_cols + 1, size)] = jnp.zeros((far * size, size), result.dtype)
    left = panel_ref[blocks(reach, reach + far, size), blocks(0, far, size)]
    for p in range(low_cols // 2):
        cols = blocks(2 * p, 2 * p + 2, size)
        value = part_ref[:, cols] + jnp.dot(
            left, panel_ref[blocks(0, far, size), cols], preferred_element_type=jnp.float32
        )
        for i in range(far):
            for k in (2 * p, 2 * p + 1):
                block = value[blocks(i, i + 1, size), blocks(k - 2 * p, k - 2 * p + 1, size)]
                here = (blocks(i, i + 1, size), blocks(k, k + 1, size))
                square[here] = keep_block(mask_ref, i, k, width, block, square.dtype)
    for p in range(far_cols // 2):
        cols = blocks(2 * p, 2 * p + 2, size)
        low = max(0, 2 * p - reach)
        value = cube_ref[:, cols] + jnp.dot(
            square[:, blocks(low, low_cols, size)],
            panel_ref[blocks(low, low_cols, size), cols],
            preferred_element_type=jnp.float32,
        )
        if 2 * p < low_cols:
            kept = square[:, cols]
        else:
            kept = high_ref[:, blocks(2 * p - low_cols, 2 * p + 2 - low_cols, size)]
        result[:, cols] = (3.0 * kept.astype(jnp.float32) - 2.0 * value).astype(result.dtype)
    scalars.wait()
    for i in range(far):
        index = jnp.where(lax.axis_index("col") == 0, i, far - 1 - i)
        for s in range(2 * half):
            place = pl.multiple_of(own_place(columns_ref, i + reach, s, far_cols) * size, size)
            target = stay_ref if s < half else leave_ref
            target[index, s % half] = result[blocks(i, i + 1, size), pl.ds(place, size)]


def write_rows(pieces, out_ref, sems):
    straight = lax.axis_index("col") == 0
    copies = []
    for rows_ref, here, there in pieces:
        for n in range(rows_ref.shape[0]):
            to = out_ref.at[jnp.where(straight, here, there) + n]
            copies.append(pltpu.make_async_copy(rows_ref.at[n], to, sems.at[len(copies)]))
    for copy in copies:
        copy.start()
    for copy in copies:
        copy.wait()


def store_kernel(far_ref, near_ref, got_near_ref, out_ref, sems):
    rows, far, near = out_ref.shape[0], far_ref.shape[0], near_ref.shape[0]
    pieces = (
        (far_ref, 0, rows - far),
        (near_ref, far, rows - far - near),
        (got_near_ref, rows - far - near, far),
    )
    write_rows(pieces, out_ref, sems)


def finish_kernel(got_ref, before_ref, out_ref, sems):
    write_rows(((got_ref, out_ref.shape[0] - got_ref.shape[0], 0),), out_ref, sems)


def local(matrix, columns):
    local_rows, own_slots, size = matrix.shape[:3]
    dtype = matrix.dtype
    reach = REACH
    far = reach // 2
    near = reach - far
    cols = lax.axis_size("col")
    ring = lax.axis_size("row")
    width = local_rows + reach
    low_cols = reach + far
    far_cols = 2 * reach + far
    same = [(r * cols, (r + 1) % ring * cols) for r in range(ring)] + [
        (r * cols + 1, (r - 1) % ring * cols + 1) for r in range(ring)
    ]
    swap = [(r * cols + 1, (r + 1) % ring * cols) for r in range(ring)] + [
        (r * cols, (r - 1) % ring * cols + 1) for r in range(ring)
    ]
    beside = [(i, (i + 1) % cols) for i in range(cols)]
    axes = ("row", "col")
    edge_rows = own_slots * size
    in_place = pltpu.with_memory_space_constraint(matrix, pltpu.HBM)
    same_edge, swap_edge, held = pl.pallas_call(
        functools.partial(edge_kernel, HEAD),
        out_shape=(
            jax.ShapeDtypeStruct((edge_rows + TILE, size), dtype),
            jax.ShapeDtypeStruct((edge_rows, size), dtype),
            jax.ShapeDtypeStruct(columns.shape, columns.dtype),
        ),
        in_specs=[HBM, HBM],
        out_specs=(VMEM,) * 3,
        scratch_shapes=[pltpu.VMEM((TILE, size), jnp.float32), pltpu.SemaphoreType.DMA((3,))],
        compiler_params=limit(1),
        cost_estimate=LIGHT,
        name="edge",
    )(pltpu.with_memory_space_constraint(columns, pltpu.HBM), in_place)
    same_rows = lax.ppermute(same_edge, axes, same)
    swap_rows = lax.ppermute(swap_edge, axes, swap)
    other = lax.ppermute(matrix, "col", beside)

    lead = reach - HEAD
    scalars = pltpu.SMEM(columns.shape, columns.dtype)
    packed_mid, packed_last = pl.pallas_call(
        functools.partial(pack_kernel, far),
        out_shape=tuple(
            jax.ShapeDtypeStruct((sum(reach + 1 + f for f in part), size, size), dtype)
            for part in (range(far, lead), range(far))
        ),
        in_specs=[VMEM, HBM, VMEM],
        out_specs=(VMEM, VMEM),
        scratch_shapes=[
            pltpu.VMEM((lead,) + matrix.shape[1:], dtype),
            scalars,
            pltpu.SemaphoreType.DMA((2,)),
        ],
        compiler_params=limit(2),
        cost_estimate=LIGHT,
        name="pack",
    )(held, in_place, other)
    mid_blocks = lax.ppermute(packed_mid, axes, swap)
    far_blocks = lax.ppermute(packed_last, axes, swap)

    panel_shape = jax.ShapeDtypeStruct((width * size, (width + 1) * size), dtype)
    panel, first_part, mask = pl.pallas_call(
        base_kernel,
        out_shape=(
            panel_shape,
            jax.ShapeDtypeStruct((reach * size, width * size), jnp.float32),
            jax.ShapeDtypeStruct((reach * width, size), jnp.float32),
        ),
        in_specs=[VMEM, HBM, VMEM, VMEM, VMEM],
        out_specs=(VMEM,) * 3,
        scratch_shapes=[
            pltpu.VMEM(matrix.shape, dtype),
            scalars,
            pltpu.SMEM((reach, width + 1), jnp.int32),
            pltpu.VMEM((TILE, size), jnp.int32),
            pltpu.SMEM((TILE, size), jnp.int32),
            pltpu.SemaphoreType.DMA((3,)),
        ],
        compiler_params=limit(12),
        cost_estimate=HEAVY,
        name="base",
    )(held, in_place, other, same_rows, swap_rows)

    rows_out = jax.ShapeDtypeStruct((near, own_slots, size, size), dtype)
    panel, stay_near, leave_near, part, high, cube = pl.pallas_call(
        functools.partial(near_kernel, far),
        out_shape=(
            panel_shape,
            rows_out,
            rows_out,
            jax.ShapeDtypeStruct((far * size, low_cols * size), jnp.float32),
            jax.ShapeDtypeStruct((far * size, (far_cols - low_cols) * size), dtype),
            jax.ShapeDtypeStruct((far * size, far_cols * size), jnp.float32),
        ),
        in_specs=[VMEM] * 5,
        out_specs=(VMEM,) * 6,
        input_output_aliases={4: 0},
        scratch_shapes=[
            pltpu.VMEM((reach * size, width * size), dtype),
            pltpu.VMEM((near * size, (width + 1) * size), dtype),
            scalars,
            pltpu.SemaphoreType.DMA,
        ],
        compiler_params=limit(16),
        cost_estimate=HEAVY,
        name="near",
    )(held, mask, first_part, mid_blocks, panel)
    arrived_near = lax.ppermute(leave_near, "col", beside)

    far_out = jax.ShapeDtypeStruct((far, own_slots, size, size), dtype)
    panel, stay_far, leave_far = pl.pallas_call(
        far_kernel,
        out_shape=(panel_shape, far_out, far_out),
        in_specs=[VMEM] * 7,
        out_specs=(VMEM,) * 3,
        input_output_aliases={6: 0},
        scratch_shapes=[
            pltpu.VMEM((far * size, low_cols * size), dtype),
            pltpu.VMEM((far * size, (far_cols + 1) * size), dtype),
            scalars,
            pltpu.SemaphoreType.DMA,
        ],
        compiler_params=limit(16),
        cost_estimate=LIGHT,
        name="far",
    )(held, mask, part, high, cube, far_blocks, panel)
    arrived_far = lax.ppermute(leave_far, "col", beside)
    out = pl.pallas_call(
        store_kernel,
        out_shape=jax.ShapeDtypeStruct(matrix.shape, dtype),
        in_specs=[VMEM] * 3,
        out_specs=HBM,
        scratch_shapes=[pltpu.SemaphoreType.DMA((far + 2 * near,))],
        compiler_params=limit(1),
        cost_estimate=LIGHT,
        name="store",
    )(stay_far, stay_near, arrived_near)
    return pl.pallas_call(
        finish_kernel,
        out_shape=jax.ShapeDtypeStruct(matrix.shape, dtype),
        in_specs=[VMEM, HBM],
        out_specs=HBM,
        input_output_aliases={1: 0},
        scratch_shapes=[pltpu.SemaphoreType.DMA((far,))],
        compiler_params=limit(1),
        cost_estimate=LIGHT,
        name="finish",
    )(arrived_far, out)


def solution(mesh):
    placed = (P(("geom", "row"), "col", None, None), P("row", None))
    return jax.shard_map(
        local,
        mesh=mesh,
        in_specs=placed,
        out_specs=P(("geom", "row"), "col", None, None),
        check_vma=False,
    )
```

time: 29.3 us -> 28.5 us (0.973)
  waiting for transfers between devices: 2.77 us -> 0.26 us
  Pallas kernels: 9.22 us -> 10.8 us
  starting transfers between devices: 15.8 us -> 17.2 us
  local copies, waits for them, and re-layouts: 1.23 us -> 0 us
    ppermute x1, starting transfers between devices: 1.35 us -> 4.37 us  [local(): arrived_near = lax.ppermute(leave_near, 'col', beside)]
    ppermute x5 -> x4, waiting for transfers between devices: 2.53 us -> 0.03 us  [the longest x1 0.02 us: local(): mid_blocks = lax.ppermute(packed_mid, axes, swap)]
    pallas_call x5, Pallas kernels: 7.58 us -> 9.16 us  [the longest x1 3.77 us: local(): pl.pallas_call(base_kernel, out_shape=(panel_shape, jax.ShapeDtypeStruct(...]
    unnamed x2 -> x0, local copies, waits for them, and re-layouts: 1.23 us -> none
    ppermute x5 -> x4, starting transfers between devices: 11.6 us -> 10.5 us  [the longest x1 3.38 us: local(): swap_rows = lax.ppermute(swap_edge, axes, swap)]
    ppermute x1, starting transfers between devices: 2.43 us -> 1.88 us  [local(): arrived_far = lax.ppermute(leave_far, 'col', beside)]
  transfers between devices with their start and end apart: 8 -> 7, of which waited for: 2 -> 1; matrix products, arithmetic and copies ran while one was open for 0% -> 0% of each run, Pallas kernels for 29% -> 36%
where the time goes in v5:
time: 28.5 us; the launch traced here: 28.3 us
  starting transfers between devices  17.2 us (60%)
  Pallas kernels  10.8 us (38%)
    ppermute x1, starting transfers between devices, local(): arrived_near = lax.ppermute(leave_near, 'col', beside)  4.37 us
    pallas_call x1, Pallas kernels, local(): pl.pallas_call(base_kernel, out_shape=(panel_shape, jax.ShapeDtypeStruct(...  3.77 us
    ppermute x1, starting transfers between devices, local(): swap_rows = lax.ppermute(swap_edge, axes, swap)  3.38 us
    ppermute x1, starting transfers between devices, local(): far_blocks = lax.ppermute(packed_last, axes, swap)  3.36 us
    ppermute x1, starting transfers between devices, local(): same_rows = lax.ppermute(same_edge, axes, same)  2.57 us
    pallas_call x1, Pallas kernels, local(): pl.pallas_call(functools.partial(near_kernel, far), out_shape=(panel_shap...  1.97 us
    ppermute x1, starting transfers between devices, local(): arrived_far = lax.ppermute(leave_far, 'col', beside)  1.88 us
    pallas_call x1, Pallas kernels, local(): pl.pallas_call(functools.partial(pack_kernel, far), out_shape=tuple((jax....  1.44 us
  transfers between devices with their start and end apart: 7, of which 1 were waited for; matrix products, arithmetic and copies ran while one was open for 0% of the time, Pallas kernels for 36%

profile of v5, /device:TPU:0, one launch (start us, length us, event | category | flops | bytes accessed | tf_op | source)
XLA Modules:
  0.0 28.3 jit_solution(5797043460994556095)
XLA Ops:
  0.0 0.5 %collective-permute-start = (bf16[8,4,128,128]{3,2,1,0:T(8,128)(2,1)}, bf16[8,4,128,128]{3,2,1,0:T(8,128)(2,1)S(1)}, u32[]{:S(2)}, u32[]{:S(2)}) collective-permute-start(bf16[8,4,128,128]{3,2,1,0:T(8,128)(2,1)} %matrix_ref.5), channel_id=1, source_target_pairs={{0,1},{1,0},{2,3},{3,2},{4,5},{5,4},{6,7},{7,6},{8,9},{9,8},{10,11... | collective-permute-start | bytes 3145736 | tf_op jit(solution)/shard_map/ppermute | solution.py:366
  0.5 0.9 %edge.1 = (bf16[528,128]{1,0:T(8,128)(2,1)S(1)}, bf16[512,128]{1,0:T(8,128)(2,1)S(1)}, s32[8,8]{1,0:T(8,128)S(1)}) custom-call(s32[8,8]{1,0:T(8,128)} %columns_ref.1, bf16[8,4,128,128]{3,2,1,0:T(8,128)(2,1)} %matrix_ref.5), custom_call_target="tpu_custom_call" | custom-call | tf_op jit(solution)/shard_map/edge/pallas_call | solution.py:350
  1.4 2.6 %collective-permute-start.1 = (bf16[528,128]{1,0:T(8,128)(2,1)S(1)}, bf16[528,128]{1,0:T(8,128)(2,1)S(1)}, u32[]{:S(2)}, u32[]{:S(2)}) collective-permute-start(bf16[528,128]{1,0:T(8,128)(2,1)S(1)} %get-tuple-element.22), channel_id=1, source_target_pairs={{0,2},{2,4},{4,6},{6,8},{8,10},{10,12},{12,14},{14,0},{1,15},{3,1}... | collective-permute-start | bytes 405512 | tf_op jit(solution)/shard_map/ppermute | solution.py:364
  3.9 3.4 %collective-permute-start.2 = (bf16[512,128]{1,0:T(8,128)(2,1)S(1)}, bf16[512,128]{1,0:T(8,128)(2,1)S(1)}, u32[]{:S(2)}, u32[]{:S(2)}) collective-permute-start(bf16[512,128]{1,0:T(8,128)(2,1)S(1)} %get-tuple-element.23), channel_id=1, source_target_pairs={{1,2},{3,4},{5,6},{7,8},{9,10},{11,12},{13,14},{15,0},{0,15},{2,1}... | collective-permute-start | bytes 393224 | tf_op jit(solution)/shard_map/ppermute | solution.py:365
  7.3 0.0 collective-permute-done.other_ref
  7.3 1.4 %pack.1 = (bf16[7,128,128]{2,1,0:T(8,128)(2,1)S(1)}, bf16[11,128,128]{2,1,0:T(8,128)(2,1)S(1)}) custom-call(s32[8,8]{1,0:T(8,128)S(1)} %get-tuple-element.21.held_ref, bf16[8,4,128,128]{3,2,1,0:T(8,128)(2,1)} %matrix_ref.5, bf16[8,4,128,128]{3,2,1,0:T(8,128)(2,1)S(1)} %collective-permute-done.other_ref), custom_call_target="tpu_custom_call" | custom-call | tf_op jit(solution)/shard_map/pack/pallas_call | solution.py:370
  8.8 1.1 %collective-permute-start.3 = (bf16[7,128,128]{2,1,0:T(8,128)(2,1)S(1)}, bf16[7,128,128]{2,1,0:T(8,128)(2,1)S(1)}, u32[]{:S(2)}, u32[]{:S(2)}) collective-permute-start(bf16[7,128,128]{2,1,0:T(8,128)(2,1)S(1)} %get-tuple-element.26), channel_id=1, source_target_pairs={{1,2},{3,4},{5,6},{7,8},{9,10},{11,12},{13,14},{15,0},{0,15},{2,1}... | collective-permute-start | bytes 688136 | tf_op jit(solution)/shard_map/ppermute | solution.py:387
  9.9 3.4 %collective-permute-start.4 = (bf16[11,128,128]{2,1,0:T(8,128)(2,1)S(1)}, bf16[11,128,128]{2,1,0:T(8,128)(2,1)S(1)}, u32[]{:S(2)}, u32[]{:S(2)}) collective-permute-start(bf16[11,128,128]{2,1,0:T(8,128)(2,1)S(1)} %get-tuple-element.31), channel_id=1, source_target_pairs={{1,2},{3,4},{5,6},{7,8},{9,10},{11,12},{13,14},{15,0},{0,15},{2,1}... | collective-permute-start | bytes 1081352 | tf_op jit(solution)/shard_map/ppermute | solution.py:388
  13.3 0.0 collective-permute-done.2.swap_ref
  13.3 0.0 collective-permute-done.1.same_ref
  13.3 3.8 %base.1 = (bf16[1536,1664]{1,0:T(8,128)(2,1)S(1)}, f32[512,1536]{1,0:T(8,128)S(1)}, f32[48,128]{1,0:T(8,128)S(1)}) custom-call(s32[8,8]{1,0:T(8,128)S(1)} %get-tuple-element.21.held_ref, bf16[8,4,128,128]{3,2,1,0:T(8,128)(2,1)} %matrix_ref.5, bf16[8,4,128,128]{3,2,1,0:T(8,128)(2,1)S(1)} %collective-permute-done.other_ref, ...), custom_call_target="tpu_custom_call" | custom-call | flops 20000000000 | tf_op jit(solution)/shard_map/base/pallas_call | solution.py:391
  17.1 0.0 collective-permute-done.3.mid_ref
  17.1 2.0 %near.1 = (bf16[1536,1664]{1,0:T(8,128)(2,1)S(1)}, bf16[2,4,128,128]{3,2,1,0:T(8,128)(2,1)S(1)}, bf16[2,4,128,128]{3,2,1,0:T(8,128)(2,1)S(1)}, f32[256,768]{1,0:...) custom-call(s32[8,8]{1,0:T(8,128)S(1)} %get-tuple-element.21.held_ref, ...), custom_call_target="tpu_custom_call", output_to_operand_aliasing={{0}: (4, {})} | custom-call | flops 20000000000 | tf_op jit(solution)/shard_map/near/pallas_call | solution.py:414
  19.0 4.4 %collective-permute-start.6 = (bf16[2,4,128,128]{3,2,1,0:T(8,128)(2,1)S(1)}, bf16[2,4,128,128]{3,2,1,0:T(8,128)(2,1)S(1)}, u32[]{:S(2)}, u32[]{:S(2)}) collective-permute-start(bf16[2,4,128,128]{3,2,1,0:T(8,128)(2,1)S(1)} %get-tuple-element.36), channel_id=1, source_target_pairs={{0,1},{1,0},{2,3},{3,2},{4,5},{5,4},{6,7},{7,6},{8,9},{9,8},{10,11... | collective-permute-start | bytes 786440 | tf_op jit(solution)/shard_map/ppermute | solution.py:437
  23.4 0.0 collective-permute-done.4.far_ref
  23.4 1.1 %far.1 = (bf16[1536,1664]{1,0:T(8,128)(2,1)S(1)}, bf16[2,4,128,128]{3,2,1,0:T(8,128)(2,1)S(1)}, bf16[2,4,128,128]{3,2,1,0:T(8,128)(2,1)S(1)}) custom-call(s32[8,8]{1,0:T(8,128)S(1)} %get-tuple-element.21.held_ref, f32[48,128]{1,0:T(8,128)S(1)} %get-tuple-element.24.mask_ref, ...), custom_call_target="tpu_custom_call", output_to_operand_aliasing={{0}: (6, {})} | custom-call | tf_op jit(solution)/shard_map/far/pallas_call | solution.py:440
  24.5 1.9 %collective-permute-start.5 = (bf16[2,4,128,128]{3,2,1,0:T(8,128)(2,1)S(1)}, bf16[2,4,128,128]{3,2,1,0:T(8,128)(2,1)S(1)}, u32[]{:S(2)}, u32[]{:S(2)}) collective-permute-start(bf16[2,4,128,128]{3,2,1,0:T(8,128)(2,1)S(1)} %get-tuple-element.33), channel_id=1, source_target_pairs={{0,1},{1,0},{2,3},{3,2},{4,5},{5,4},{6,7},{7,6},{8,9},{9,8},{10,11... | collective-permute-start | bytes 786440 | tf_op jit(solution)/shard_map/ppermute | solution.py:456
  26.4 0.0 collective-permute-done.6.got_near_ref
  26.4 0.9 %store.1.before_ref = bf16[8,4,128,128]{3,2,1,0:T(8,128)(2,1)} custom-call(bf16[2,4,128,128]{3,2,1,0:T(8,128)(2,1)S(1)} %get-tuple-element.34.far_ref, bf16[2,4,128,128]{3,2,1,0:T(8,128)(2,1)S(1)} %get-tuple-element.35.near_ref, bf16[2,4,128,128]{3,2,1,0:T(8,128)(2,1)S(1)} %collective-permute-done.6.got_near_ref), custom_call_target="tpu_custom_call" | custom-call | tf_op jit(solution)/shard_map/store/pallas_call | solution.py:457
  27.3 0.2 collective-permute-done.5.got_ref
  27.6 0.7 %finish.1 = bf16[8,4,128,128]{3,2,1,0:T(8,128)(2,1)} custom-call(bf16[2,4,128,128]{3,2,1,0:T(8,128)(2,1)S(1)} %collective-permute-done.5.got_ref, bf16[8,4,128,128]{3,2,1,0:T(8,128)(2,1)} %store.1.before_ref), custom_call_target="tpu_custom_call", output_to_operand_aliasing={{}: (1, {})} | custom-call | tf_op jit(solution)/shard_map/finish/pallas_call | solution.py:467
Async XLA Ops:
  0.0 7.3 %collective-permute-start = (bf16[8,4,128,128]{3,2,1,0:T(8,128)(2,1)}, bf16[8,4,128,128]{3,2,1,0:T(8,128)(2,1)S(1)}, u32[]{:S(2)}, u32[]{:S(2)}) collective-permute-start(bf16[8,4,128,128]{3,2,1,0:T(8,128)(2,1)} %matrix_ref.5), channel_id=1, source_target_pairs={{0,1},{1,0},{2,3},{3,2},{4,5},{5,4},{6,7},{7,6},{8,9},{9,8},{10,11... | collective-permute-start | bytes 3145736 | tf_op jit(solution)/shard_map/ppermute | solution.py:366
  1.4 11.9 %collective-permute-start.1 = (bf16[528,128]{1,0:T(8,128)(2,1)S(1)}, bf16[528,128]{1,0:T(8,128)(2,1)S(1)}, u32[]{:S(2)}, u32[]{:S(2)}) collective-permute-start(bf16[528,128]{1,0:T(8,128)(2,1)S(1)} %get-tuple-element.22), channel_id=1, source_target_pairs={{0,2},{2,4},{4,6},{6,8},{8,10},{10,12},{12,14},{14,0},{1,15},{3,1}... | collective-permute-start | bytes 405512 | tf_op jit(solution)/shard_map/ppermute | solution.py:364
  3.9 9.3 %collective-permute-start.2 = (bf16[512,128]{1,0:T(8,128)(2,1)S(1)}, bf16[512,128]{1,0:T(8,128)(2,1)S(1)}, u32[]{:S(2)}, u32[]{:S(2)}) collective-permute-start(bf16[512,128]{1,0:T(8,128)(2,1)S(1)} %get-tuple-element.23), channel_id=1, source_target_pairs={{1,2},{3,4},{5,6},{7,8},{9,10},{11,12},{13,14},{15,0},{0,15},{2,1}... | collective-permute-start | bytes 393224 | tf_op jit(solution)/shard_map/ppermute | solution.py:365
  8.8 8.3 %collective-permute-start.3 = (bf16[7,128,128]{2,1,0:T(8,128)(2,1)S(1)}, bf16[7,128,128]{2,1,0:T(8,128)(2,1)S(1)}, u32[]{:S(2)}, u32[]{:S(2)}) collective-permute-start(bf16[7,128,128]{2,1,0:T(8,128)(2,1)S(1)} %get-tuple-element.26), channel_id=1, source_target_pairs={{1,2},{3,4},{5,6},{7,8},{9,10},{11,12},{13,14},{15,0},{0,15},{2,1}... | collective-permute-start | bytes 688136 | tf_op jit(solution)/shard_map/ppermute | solution.py:387
  9.9 13.5 %collective-permute-start.4 = (bf16[11,128,128]{2,1,0:T(8,128)(2,1)S(1)}, bf16[11,128,128]{2,1,0:T(8,128)(2,1)S(1)}, u32[]{:S(2)}, u32[]{:S(2)}) collective-permute-start(bf16[11,128,128]{2,1,0:T(8,128)(2,1)S(1)} %get-tuple-element.31), channel_id=1, source_target_pairs={{1,2},{3,4},{5,6},{7,8},{9,10},{11,12},{13,14},{15,0},{0,15},{2,1}... | collective-permute-start | bytes 1081352 | tf_op jit(solution)/shard_map/ppermute | solution.py:388
  19.0 7.3 %collective-permute-start.6 = (bf16[2,4,128,128]{3,2,1,0:T(8,128)(2,1)S(1)}, bf16[2,4,128,128]{3,2,1,0:T(8,128)(2,1)S(1)}, u32[]{:S(2)}, u32[]{:S(2)}) collective-permute-start(bf16[2,4,128,128]{3,2,1,0:T(8,128)(2,1)S(1)} %get-tuple-element.36), channel_id=1, source_target_pairs={{0,1},{1,0},{2,3},{3,2},{4,5},{5,4},{6,7},{7,6},{8,9},{9,8},{10,11... | collective-permute-start | bytes 786440 | tf_op jit(solution)/shard_map/ppermute | solution.py:437
  24.5 3.0 %collective-permute-start.5 = (bf16[2,4,128,128]{3,2,1,0:T(8,128)(2,1)S(1)}, bf16[2,4,128,128]{3,2,1,0:T(8,128)(2,1)S(1)}, u32[]{:S(2)}, u32[]{:S(2)}) collective-permute-start(bf16[2,4,128,128]{3,2,1,0:T(8,128)(2,1)S(1)} %get-tuple-element.33), channel_id=1, source_target_pairs={{0,1},{1,0},{2,3},{3,2},{4,5},{5,4},{6,7},{7,6},{8,9},{9,8},{10,11... | collective-permute-start | bytes 786440 | tf_op jit(solution)/shard_map/ppermute | solution.py:456

commit v6 on v5

--- a/solution.py
+++ b/solution.py
@@ -15,6 +15,8 @@
 
 HEAVY = pl.CostEstimate(flops=20_000_000_000, bytes_accessed=0, transcendentals=0)
 LIGHT = pl.CostEstimate(flops=0, bytes_accessed=0, transcendentals=0)
+SHORT = pl.CostEstimate(flops=500_000_000, bytes_accessed=0, transcendentals=0)
+MEDIUM = pl.CostEstimate(flops=1_200_000_000, bytes_accessed=0, transcendentals=0)
 
 SMEM = pl.BlockSpec(memory_space=pltpu.SMEM)
 VMEM = pl.BlockSpec(memory_space=pltpu.VMEM)
@@ -88,7 +90,8 @@
         copy.wait()
 
 
-def pack_kernel(far, held_ref, matrix_ref, other_ref, mid_ref, last_ref, own, columns_ref, sems):
+def pack_kernel(held_ref, matrix_ref, other_ref, after_ref, *refs):
+    out_refs, (own, columns_ref, sems) = refs[:-3], refs[-3:]
     rows, half = other_ref.shape[:2]
     lead = own.shape[0]
     straight = lax.axis_index("col") == 0
@@ -99,15 +102,11 @@
     ]
     for copy in copies:
         copy.start()
-    mid_ref[...] = jnp.zeros_like(mid_ref)
-    last_ref[...] = jnp.zeros_like(last_ref)
+    for out_ref in out_refs:
+        out_ref[...] = jnp.zeros_like(out_ref)
     for copy in copies:
         copy.wait()
-    base = 0
-    for f in range(lead):
-        if f == far:
-            base = 0
-        out_ref = last_ref if f < far else mid_ref
+    for f, out_ref in enumerate(out_refs):
         q = 2 * REACH - 1 - f
         index = jnp.where(straight, lead - 1 - f, f)
         count = REACH + 1 + f
@@ -115,62 +114,78 @@
             place = 2 * REACH - 1 - own_place(columns_ref, q, s, 2 * REACH + 1)
 
             @pl.when((place >= 0) & (place < count))
-            def _(place=place, index=index, s=s, base=base, out_ref=out_ref):
+            def _(place=place, index=index, s=s, out_ref=out_ref):
                 if s < half:
-                    out_ref[base + place] = own[index, s]
+                    out_ref[place] = own[index, s]
                 else:
-                    out_ref[base + place] = other_ref[start + index, s - half]
-        base += count
-
-
-def base_kernel(
-    held_ref, matrix_ref, other_ref, same_ref, swap_ref, panel_ref, first_ref, mask_ref,
-    own_ref, columns_ref, keep_ref, steps, halo_ref, sems
-):
+                    out_ref[place] = other_ref[start + index, s - half]
+
+
+def base_kernel(turn, held_ref, matrix_ref, other_ref, *refs):
+    panel_ref, first_ref, mask_ref, own_ref, columns_ref, keep_ref, sems = refs[-7:]
     rows, half, size = own_ref.shape[0], own_ref.shape[1], own_ref.shape[2]
     reach = REACH
     width = rows + reach
+
+    @pl.when(lax.rem(lax.axis_index("row") + lax.axis_index("col"), 2) == turn)
+    def _():
+        copies = [
+            pltpu.make_async_copy(held_ref, columns_ref, sems.at[0]),
+            pltpu.make_async_copy(matrix_ref, own_ref, sems.at[1]),
+        ]
+        for copy in copies:
+            copy.start()
+        panel_ref[...] = jnp.zeros_like(panel_ref)
+        for copy in copies:
+            copy.wait()
+        for q in range(reach, width):
+            index = jnp.where(lax.axis_index("col") == 0, q - reach, width - 1 - q)
+            for s in range(2 * half):
+                place = pl.multiple_of(own_place(columns_ref, q, s, width) * size, size)
+                source = own_ref if s < half else other_ref
+                panel_ref[blocks(q, q + 1, size), pl.ds(place, size)] = source[index, s % half]
+        for i in range(reach):
+            for k in range(width + 1):
+                keep_ref[i, k] = 0
+            for s in range(2 * half):
+                keep_ref[i, own_place(columns_ref, i + reach, s, width)] = 1
+            for k in range(width):
+                at = i * width + k
+                mask_ref[at : at + 1, :] = jnp.full((1, size), keep_ref[i, k], jnp.float32)
+        for p in range(width // 2):
+            low = max(reach, 2 * p - reach)
+            high = min(width, 2 * p + 2 + reach)
+            cols = blocks(2 * p, 2 * p + 2, size)
+            first_ref[:, cols] = jnp.dot(
+                panel_ref[blocks(reach, 2 * reach, size), blocks(low, high, size)],
+                panel_ref[blocks(low, high, size), cols],
+                preferred_element_type=jnp.float32,
+            )
+
+
+def lead_kernel(
+    half, same_ref, swap_ref, before_panel, before_first, panel_ref, first_ref, steps, halo_ref, sem
+):
+    size = same_ref.shape[1]
+    reach = REACH
+    width = panel_ref.shape[0] // size
     lead = reach - HEAD
     steps[...] = same_ref[half * size :, :].astype(jnp.float32).astype(jnp.int32)
-    copies = [
-        pltpu.make_async_copy(held_ref, columns_ref, sems.at[0]),
-        pltpu.make_async_copy(steps, halo_ref, sems.at[1]),
-        pltpu.make_async_copy(matrix_ref, own_ref, sems.at[2]),
-    ]
-    for copy in copies:
-        copy.start()
-    panel_ref[...] = jnp.zeros_like(panel_ref)
-    for copy in copies:
-        copy.wait()
+    copy = pltpu.make_async_copy(steps, halo_ref, sem)
+    copy.start()
+    copy.wait()
     for s in range(2 * half):
-        place = halo_place(halo_ref, rows, 2 * half, lead, s, width)
+        place = halo_place(halo_ref, width - reach, 2 * half, lead, s, width)
         place = pl.multiple_of(place * size, size)
         source = same_ref if s < half else swap_ref
         panel_ref[blocks(lead, lead + 1, size), pl.ds(place, size)] = source[
             blocks(s % half, s % half + 1, size), :
         ]
-    for q in range(reach, width):
-        index = jnp.where(lax.axis_index("col") == 0, q - reach, width - 1 - q)
-        for s in range(2 * half):
-            place = pl.multiple_of(own_place(columns_ref, q, s, width) * size, size)
-            source = own_ref if s < half else other_ref
-            panel_ref[blocks(q, q + 1, size), pl.ds(place, size)] = source[index, s % half]
-    for i in range(reach):
-        for k in range(width + 1):
-            keep_ref[i, k] = 0
-        for s in range(2 * half):
-            keep_ref[i, own_place(columns_ref, i + reach, s, width)] = 1
-        for k in range(width):
-            at = i * width + k
-            mask_ref[at : at + 1, :] = jnp.full((1, size), keep_ref[i, k], jnp.float32)
-    for p in range(width // 2):
-        low = max(lead, 2 * p - reach)
-        high = min(width, 2 * p + 2 + reach)
+    left = panel_ref[blocks(reach, 2 * reach, size), blocks(lead, reach, size)]
+    for p in range(reach):
         cols = blocks(2 * p, 2 * p + 2, size)
-        first_ref[:, cols] = jnp.dot(
-            panel_ref[blocks(reach, 2 * reach, size), blocks(low, high, size)],
-            panel_ref[blocks(low, high, size), cols],
-            preferred_element_type=jnp.float32,
+        first_ref[:, cols] += jnp.dot(
+            left, panel_ref[blocks(lead, reach, size), cols], preferred_element_type=jnp.float32
         )
 
 
@@ -181,9 +196,12 @@
 
 
 def near_kernel(
-    far, held_ref, mask_ref, first_ref, mid_ref, before_ref,
-    panel_ref, stay_ref, leave_ref, part_ref, high_ref, cube_ref, square, result, columns_ref, sem
+    far, held_ref, mask_ref, first_ref, before_ref, *refs
 ):
+    mid_refs = refs[: REACH - HEAD - far]
+    (
+        panel_ref, stay_ref, leave_ref, part_ref, high_ref, cube_ref, square, result, columns_ref, sem,
+    ) = refs[REACH - HEAD - far :]
     reach = REACH
     lead = reach - HEAD
     scalars = pltpu.make_async_copy(held_ref, columns_ref, sem)
@@ -194,11 +212,9 @@
     low_cols = reach + far
     far_cols = 2 * reach + far
     near_cols = 2 * reach
-    at = 0
-    for q in range(far, lead):
+    for q, mid_ref in zip(range(far, lead), mid_refs):
         for k in range(reach + 1 + q):
-            panel_ref[blocks(q, q + 1, size), blocks(k, k + 1, size)] = mid_ref[at]
-            at += 1
+            panel_ref[blocks(q, q + 1, size), blocks(k, k + 1, size)] = mid_ref[k]
     result[:, blocks(width, width + 1, size)] = jnp.zeros((near * size, size), result.dtype)
     left = panel_ref[blocks(reach, 2 * reach, size), blocks(far, lead, size)]
     for p in range(width // 2):
@@ -250,37 +266,33 @@
 
 
 def far_kernel(
-    held_ref, mask_ref, part_ref, high_ref, cube_ref, far_ref, before_ref,
+    far, i, held_ref, mask_ref, part_ref, high_ref, cube_ref, row_ref, before_ref,
     panel_ref, stay_ref, leave_ref, square, result, columns_ref, sem
 ):
-    reach, far = REACH, stay_ref.shape[0]
+    reach = REACH
     scalars = pltpu.make_async_copy(held_ref, columns_ref, sem)
     scalars.start()
     half, size = stay_ref.shape[1], stay_ref.shape[2]
     width = panel_ref.shape[0] // size
     low_cols = reach + far
     far_cols = 2 * reach + far
-    at = 0
-    for f in range(far):
-        for k in range(reach + 1 + f):
-            panel_ref[blocks(f, f + 1, size), blocks(k, k + 1, size)] = far_ref[at]
-            at += 1
-    result[:, blocks(far_cols, far_cols + 1, size)] = jnp.zeros((far * size, size), result.dtype)
-    left = panel_ref[blocks(reach, reach + far, size), blocks(0, far, size)]
+    mine = blocks(i, i + 1, size)
+    for k in range(reach + 1 + i):
+        panel_ref[mine, blocks(k, k + 1, size)] = row_ref[k]
+    result[:, blocks(far_cols, far_cols + 1, size)] = jnp.zeros((size, size), result.dtype)
+    left = panel_ref[blocks(reach + i, reach + i + 1, size), blocks(0, far, size)]
     for p in range(low_cols // 2):
         cols = blocks(2 * p, 2 * p + 2, size)
-        value = part_ref[:, cols] + jnp.dot(
+        value = part_ref[mine, cols] + jnp.dot(
             left, panel_ref[blocks(0, far, size), cols], preferred_element_type=jnp.float32
         )
-        for i in range(far):
-            for k in (2 * p, 2 * p + 1):
-                block = value[blocks(i, i + 1, size), blocks(k - 2 * p, k - 2 * p + 1, size)]
-                here = (blocks(i, i + 1, size), blocks(k, k + 1, size))
-                square[here] = keep_block(mask_ref, i, k, width, block, square.dtype)
+        for k in (2 * p, 2 * p + 1):
+            block = value[:, blocks(k - 2 * p, k - 2 * p + 1, size)]
+            square[:, blocks(k, k + 1, size)] = keep_block(mask_ref, i, k, width, block, square.dtype)
     for p in range(far_cols // 2):
         cols = blocks(2 * p, 2 * p + 2, size)
         low = max(0, 2 * p - reach)
-        value = cube_ref[:, cols] + jnp.dot(
+        value = cube_ref[mine, cols] + jnp.dot(
             square[:, blocks(low, low_cols, size)],
             panel_ref[blocks(low, low_cols, size), cols],
             preferred_element_type=jnp.float32,
@@ -288,15 +300,13 @@
         if 2 * p < low_cols:
             kept = square[:, cols]
         else:
-            kept = high_ref[:, blocks(2 * p - low_cols, 2 * p + 2 - low_cols, size)]
+            kept = high_ref[mine, blocks(2 * p - low_cols, 2 * p + 2 - low_cols, size)]
         result[:, cols] = (3.0 * kept.astype(jnp.float32) - 2.0 * value).astype(result.dtype)
     scalars.wait()
-    for i in range(far):
-        index = jnp.where(lax.axis_index("col") == 0, i, far - 1 - i)
-        for s in range(2 * half):
-            place = pl.multiple_of(own_place(columns_ref, i + reach, s, far_cols) * size, size)
-            target = stay_ref if s < half else leave_ref
-            target[index, s % half] = result[blocks(i, i + 1, size), pl.ds(place, size)]
+    for s in range(2 * half):
+        place = pl.multiple_of(own_place(columns_ref, i + reach, s, far_cols) * size, size)
+        target = stay_ref if s < half else leave_ref
+        target[0, s % half] = result[:, pl.ds(place, size)]
 
 
 def write_rows(pieces, out_ref, sems):
@@ -312,13 +322,16 @@
         copy.wait()
 
 
-def store_kernel(far_ref, near_ref, got_near_ref, out_ref, sems):
-    rows, far, near = out_ref.shape[0], far_ref.shape[0], near_ref.shape[0]
-    pieces = (
-        (far_ref, 0, rows - far),
-        (near_ref, far, rows - far - near),
-        (got_near_ref, rows - far - near, far),
-    )
+def store_kernel(*refs):
+    *row_refs, out_ref, sems = refs
+    rows = out_ref.shape[0]
+    far = sum(ref.shape[0] == 1 for ref in row_refs) // 2 + 1
+    kept, near_ref, got_near_ref, got = row_refs[:far], row_refs[far], row_refs[far + 1], row_refs[far + 2 :]
+    near = near_ref.shape[0]
+    pieces = [(ref, i, rows - 1 - i) for i, ref in enumerate(kept)]
+    pieces.append((near_ref, far, rows - far - near))
+    pieces.append((got_near_ref, rows - far - near, far))
+    pieces += [(ref, rows - 2 - i, 1 + i) for i, ref in enumerate(got)]
     write_rows(pieces, out_ref, sems)
 
 
@@ -363,18 +376,41 @@
     )(pltpu.with_memory_space_constraint(columns, pltpu.HBM), in_place)
     same_rows = lax.ppermute(same_edge, axes, same)
     swap_rows = lax.ppermute(swap_edge, axes, swap)
-    other = lax.ppermute(matrix, "col", beside)
+    sent, held = lax.optimization_barrier((matrix, held))
+    other = lax.ppermute(sent, "col", beside)
 
     lead = reach - HEAD
     scalars = pltpu.SMEM(columns.shape, columns.dtype)
-    packed_mid, packed_last = pl.pallas_call(
-        functools.partial(pack_kernel, far),
+    panel_shape = jax.ShapeDtypeStruct((width * size, (width + 1) * size), dtype)
+    first_shape = jax.ShapeDtypeStruct((reach * size, width * size), jnp.float32)
+    base_shapes = (panel_shape, first_shape, jax.ShapeDtypeStruct((reach * width, size), jnp.float32))
+
+    def base(turn, *before):
+        return pl.pallas_call(
+            functools.partial(base_kernel, turn),
+            out_shape=base_shapes,
+            in_specs=[VMEM, HBM, VMEM] + [VMEM] * len(before),
+            out_specs=(VMEM,) * 3,
+            input_output_aliases={3 + n: n for n in range(len(before))},
+            scratch_shapes=[
+                pltpu.VMEM(matrix.shape, dtype),
+                scalars,
+                pltpu.SMEM((reach, width + 1), jnp.int32),
+                pltpu.SemaphoreType.DMA((2,)),
+            ],
+            compiler_params=limit(12),
+            cost_estimate=LIGHT,
+            name="base",
+        )(held, in_place, other, *before)
+
+    early = base(0)
+    packed = pl.pallas_call(
+        pack_kernel,
         out_shape=tuple(
-            jax.ShapeDtypeStruct((sum(reach + 1 + f for f in part), size, size), dtype)
-            for part in (range(far, lead), range(far))
+            jax.ShapeDtypeStruct((reach + 1 + f, size, size), dtype) for f in range(lead)
         ),
-        in_specs=[VMEM, HBM, VMEM],
-        out_specs=(VMEM, VMEM),
+        in_specs=[VMEM, HBM, VMEM, ANY],
+        out_specs=(VMEM,) * lead,
         scratch_shapes=[
             pltpu.VMEM((lead,) + matrix.shape[1:], dtype),
             scalars,
@@ -383,32 +419,25 @@
         compiler_params=limit(2),
         cost_estimate=LIGHT,
         name="pack",
-    )(held, in_place, other)
-    mid_blocks = lax.ppermute(packed_mid, axes, swap)
-    far_blocks = lax.ppermute(packed_last, axes, swap)
-
-    panel_shape = jax.ShapeDtypeStruct((width * size, (width + 1) * size), dtype)
-    panel, first_part, mask = pl.pallas_call(
-        base_kernel,
-        out_shape=(
-            panel_shape,
-            jax.ShapeDtypeStruct((reach * size, width * size), jnp.float32),
-            jax.ShapeDtypeStruct((reach * width, size), jnp.float32),
-        ),
-        in_specs=[VMEM, HBM, VMEM, VMEM, VMEM],
-        out_specs=(VMEM,) * 3,
+    )(held, in_place, other, early[2])
+    arrived = {f: lax.ppermute(packed[f], axes, swap) for f in reversed(range(lead))}
+
+    panel, first_part, mask = base(1, *early)
+    panel, first_part = pl.pallas_call(
+        functools.partial(lead_kernel, own_slots),
+        out_shape=(panel_shape, first_shape),
+        in_specs=[VMEM] * 4,
+        out_specs=(VMEM,) * 2,
+        input_output_aliases={2: 0, 3: 1},
         scratch_shapes=[
-            pltpu.VMEM(matrix.shape, dtype),
-            scalars,
-            pltpu.SMEM((reach, width + 1), jnp.int32),
             pltpu.VMEM((TILE, size), jnp.int32),
             pltpu.SMEM((TILE, size), jnp.int32),
-            pltpu.SemaphoreType.DMA((3,)),
+            pltpu.SemaphoreType.DMA,
         ],
         compiler_params=limit(12),
-        cost_estimate=HEAVY,
-        name="base",
-    )(held, in_place, other, same_rows, swap_rows)
+        cost_estimate=MEDIUM,
+        name="lead",
+    )(same_rows, swap_rows, panel, first_part)
 
     rows_out = jax.ShapeDtypeStruct((near, own_slots, size, size), dtype)
     panel, stay_near, leave_near, part, high, cube = pl.pallas_call(
@@ -421,9 +450,9 @@
             jax.ShapeDtypeStruct((far * size, (far_cols - low_cols) * size), dtype),
             jax.ShapeDtypeStruct((far * size, far_cols * size), jnp.float32),
         ),
-        in_specs=[VMEM] * 5,
+        in_specs=[VMEM] * (4 + lead - far),
         out_specs=(VMEM,) * 6,
-        input_output_aliases={4: 0},
+        input_output_aliases={3: 0},
         scratch_shapes=[
             pltpu.VMEM((reach * size, width * size), dtype),
             pltpu.VMEM((near * size, (width + 1) * size), dtype),
@@ -431,50 +460,53 @@
             pltpu.SemaphoreType.DMA,
         ],
         compiler_params=limit(16),
-        cost_estimate=HEAVY,
+        cost_estimate=SHORT,
         name="near",
-    )(held, mask, first_part, mid_blocks, panel)
+    )(held, mask, first_part, panel, *[arrived[f] for f in range(far, lead)])
     arrived_near = lax.ppermute(leave_near, "col", beside)
 
-    far_out = jax.ShapeDtypeStruct((far, own_slots, size, size), dtype)
-    panel, stay_far, leave_far = pl.pallas_call(
-        far_kernel,
-        out_shape=(panel_shape, far_out, far_out),
-        in_specs=[VMEM] * 7,
-        out_specs=(VMEM,) * 3,
-        input_output_aliases={6: 0},
-        scratch_shapes=[
-            pltpu.VMEM((far * size, low_cols * size), dtype),
-            pltpu.VMEM((far * size, (far_cols + 1) * size), dtype),
-            scalars,
-            pltpu.SemaphoreType.DMA,
-        ],
-        compiler_params=limit(16),
-        cost_estimate=LIGHT,
-        name="far",
-    )(held, mask, part, high, cube, far_blocks, panel)
-    arrived_far = lax.ppermute(leave_far, "col", beside)
+    row_out = jax.ShapeDtypeStruct((1, own_slots, size, size), dtype)
+    stay, got = {}, {}
+    for i in reversed(range(far)):
+        panel, stay[i], leave = pl.pallas_call(
+            functools.partial(far_kernel, far, i),
+            out_shape=(panel_shape, row_out, row_out),
+            in_specs=[VMEM] * 7,
+            out_specs=(VMEM,) * 3,
+            input_output_aliases={6: 0},
+            scratch_shapes=[
+                pltpu.VMEM((size, low_cols * size), dtype),
+                pltpu.VMEM((size, (far_cols + 1) * size), dtype),
+                scalars,
+                pltpu.SemaphoreType.DMA,
+            ],
+            compiler_params=limit(16),
+            cost_estimate=HEAVY if i else LIGHT,
+            name="far",
+        )(held, mask, part, high, cube, arrived[i], panel)
+        got[i] = lax.ppermute(leave, "col", beside)
+    pieces = [*[stay[i] for i in range(far)], stay_near, arrived_near, *[got[i] for i in range(1, far)]]
     out = pl.pallas_call(
         store_kernel,
         out_shape=jax.ShapeDtypeStruct(matrix.shape, dtype),
-        in_specs=[VMEM] * 3,
+        in_specs=[VMEM] * len(pieces),
         out_specs=HBM,
-        scratch_shapes=[pltpu.SemaphoreType.DMA((far + 2 * near,))],
+        scratch_shapes=[pltpu.SemaphoreType.DMA((local_rows - 1,))],
         compiler_params=limit(1),
         cost_estimate=LIGHT,
         name="store",
-    )(stay_far, stay_near, arrived_near)
+    )(*pieces)
     return pl.pallas_call(
         finish_kernel,
         out_shape=jax.ShapeDtypeStruct(matrix.shape, dtype),
         in_specs=[VMEM, HBM],
         out_specs=HBM,
         input_output_aliases={1: 0},
-        scratch_shapes=[pltpu.SemaphoreType.DMA((far,))],
+        scratch_shapes=[pltpu.SemaphoreType.DMA((1,))],
         compiler_params=limit(1),
         cost_estimate=LIGHT,
         name="finish",
-    )(arrived_far, out)
+    )(got[0], out)
 
 
 def solution(mesh):

time: 28.5 us -> 28.4 us (level)
  starting transfers between devices: 17.2 us -> 15.1 us
  Pallas kernels: 10.8 us -> 12 us
  waiting for transfers between devices: 0.26 us -> 0.88 us
    ppermute x1, starting transfers between devices: 4.37 us -> 0.07 us  [local(): arrived_near = lax.ppermute(leave_near, 'col', beside)]
    ppermute x4 -> x6, starting transfers between devices: 6.84 us -> 9.11 us  [the longest x3 6.73 us: local(): lax.ppermute(packed[f], axes, swap)]
    pallas_call x3 -> x6, Pallas kernels: 6.28 us -> 7.51 us  [the longest x2 3.1 us: base(): pl.pallas_call(functools.partial(base_kernel, turn), out_shape=base_shape...]
    ppermute x4 -> x6, waiting for transfers between devices: 0.25 us -> 0.87 us  [the longest x3 0.86 us: local(): lax.ppermute(packed[f], axes, swap)]
  transfers between devices with their start and end apart: 7 -> 9, of which waited for: 1 -> 3; matrix products, arithmetic and copies ran while one was open for 0% -> 0% of each run, Pallas kernels for 36% -> 37%
where the time goes in v6:
time: 28.4 us; the launch traced here: 28.1 us
  starting transfers between devices  15.1 us (53%)
  Pallas kernels  12 us (42%)
  waiting for transfers between devices  0.88 us (3%)
    ppermute x3, starting transfers between devices, local(): lax.ppermute(packed[f], axes, swap)  6.73 us
    ppermute x1, starting transfers between devices, local(): swap_rows = lax.ppermute(swap_edge, axes, swap)  3.31 us
    pallas_call x2, Pallas kernels, base(): pl.pallas_call(functools.partial(base_kernel, turn), out_shape=base_shape...  3.1 us
    ppermute x1, starting transfers between devices, local(): same_rows = lax.ppermute(same_edge, axes, same)  2.58 us
    pallas_call x1, Pallas kernels, local(): pl.pallas_call(functools.partial(near_kernel, far), out_shape=(panel_shap...  1.96 us
    ppermute x2, starting transfers between devices, local(): got[i] = lax.ppermute(leave, 'col', beside)  1.86 us
    pallas_call x2, Pallas kernels, local(): pl.pallas_call(functools.partial(far_kernel, far, i), out_shape=(panel_sh...  1.83 us
    pallas_call x1, Pallas kernels, local(): pl.pallas_call(pack_kernel, out_shape=tuple((jax.ShapeDtypeStruct((reach...  1.42 us
  transfers between devices with their start and end apart: 9, of which 3 were waited for; matrix products, arithmetic and copies ran while one was open for 0% of the time, Pallas kernels for 37%

profile of v6, /device:TPU:0, one launch (start us, length us, event | category | flops | bytes accessed | tf_op | source)
XLA Modules:
  0.0 28.1 jit_solution(12762468037864102347)
XLA Ops:
  0.0 0.9 %edge.1 = (bf16[528,128]{1,0:T(8,128)(2,1)S(1)}, bf16[512,128]{1,0:T(8,128)(2,1)S(1)}, s32[8,8]{1,0:T(8,128)S(1)}) custom-call(s32[8,8]{1,0:T(8,128)} %columns_ref.1, bf16[8,4,128,128]{3,2,1,0:T(8,128)(2,1)} %matrix_ref.7), custom_call_target="tpu_custom_call" | custom-call | tf_op jit(solution)/shard_map/edge/pallas_call | solution.py:363
  0.9 0.5 %collective-permute-start = (bf16[8,4,128,128]{3,2,1,0:T(8,128)(2,1)}, bf16[8,4,128,128]{3,2,1,0:T(8,128)(2,1)S(1)}, u32[]{:S(2)}, u32[]{:S(2)}) collective-permute-start(bf16[8,4,128,128]{3,2,1,0:T(8,128)(2,1)} %matrix_ref.7), channel_id=1, source_target_pairs={{0,1},{1,0},{2,3},{3,2},{4,5},{5,4},{6,7},{7,6},{8,9},{9,8},{10,11... | collective-permute-start | bytes 3145736 | tf_op jit(solution)/shard_map/ppermute | solution.py:380
  1.4 2.6 %collective-permute-start.1 = (bf16[528,128]{1,0:T(8,128)(2,1)S(1)}, bf16[528,128]{1,0:T(8,128)(2,1)S(1)}, u32[]{:S(2)}, u32[]{:S(2)}) collective-permute-start(bf16[528,128]{1,0:T(8,128)(2,1)S(1)} %get-tuple-element.39), channel_id=1, source_target_pairs={{0,2},{2,4},{4,6},{6,8},{8,10},{10,12},{12,14},{14,0},{1,15},{3,1}... | collective-permute-start | bytes 405512 | tf_op jit(solution)/shard_map/ppermute | solution.py:377
  4.0 3.3 %collective-permute-start.2 = (bf16[512,128]{1,0:T(8,128)(2,1)S(1)}, bf16[512,128]{1,0:T(8,128)(2,1)S(1)}, u32[]{:S(2)}, u32[]{:S(2)}) collective-permute-start(bf16[512,128]{1,0:T(8,128)(2,1)S(1)} %get-tuple-element.40), channel_id=1, source_target_pairs={{1,2},{3,4},{5,6},{7,8},{9,10},{11,12},{13,14},{15,0},{0,15},{2,1}... | collective-permute-start | bytes 393224 | tf_op jit(solution)/shard_map/ppermute | solution.py:378
  7.3 0.0 collective-permute-done.other_ref
  7.3 3.1 %base.2 = (bf16[1536,1664]{1,0:T(8,128)(2,1)S(1)}, f32[512,1536]{1,0:T(8,128)S(1)}, f32[48,128]{1,0:T(8,128)S(1)}) custom-call(s32[8,8]{1,0:T(8,128)S(1)} %get-tuple-element.33.held_ref, bf16[8,4,128,128]{3,2,1,0:T(8,128)(2,1)} %matrix_ref.7, bf16[8,4,128,128]{3,2,1,0:T(8,128)(2,1)S(1)} %collective-permute-done.other_ref), custom_call_target="tpu_custom_call" | custom-call | tf_op jit(solution)/shard_map/base/pallas_call | solution.py:389
  10.4 1.4 %pack.1 = (bf16[5,128,128]{2,1,0:T(8,128)(2,1)S(1)}, bf16[6,128,128]{2,1,0:T(8,128)(2,1)S(1)}, bf16[7,128,128]{2,1,0:T(8,128)(2,1)S(1)}) custom-call(s32[8,8]{1,0:T(8,128)S(1)} %get-tuple-element.33.held_ref, bf16[8,4,128,128]{3,2,1,0:T(8,128)(2,1)} %matrix_ref.7, bf16[8,4,128,128]{3,2,1,0:T(8,128)(2,1)S(1)} %collective-permute-done.other_ref, ...), custom_call_target="tpu_custom_call" | custom-call | tf_op jit(solution)/shard_map/pack/pallas_call | solution.py:407
  11.8 2.3 %collective-permute-start.3 = (bf16[7,128,128]{2,1,0:T(8,128)(2,1)S(1)}, bf16[7,128,128]{2,1,0:T(8,128)(2,1)S(1)}, u32[]{:S(2)}, u32[]{:S(2)}) collective-permute-start(bf16[7,128,128]{2,1,0:T(8,128)(2,1)S(1)} %get-tuple-element.45), channel_id=1, source_target_pairs={{1,2},{3,4},{5,6},{7,8},{9,10},{11,12},{13,14},{15,0},{0,15},{2,1}... | collective-permute-start | bytes 688136 | tf_op jit(solution)/shard_map/ppermute | solution.py:423
  14.1 2.2 %collective-permute-start.5 = (bf16[6,128,128]{2,1,0:T(8,128)(2,1)S(1)}, bf16[6,128,128]{2,1,0:T(8,128)(2,1)S(1)}, u32[]{:S(2)}, u32[]{:S(2)}) collective-permute-start(bf16[6,128,128]{2,1,0:T(8,128)(2,1)S(1)} %get-tuple-element.50), channel_id=1, source_target_pairs={{1,2},{3,4},{5,6},{7,8},{9,10},{11,12},{13,14},{15,0},{0,15},{2,1}... | collective-permute-start | bytes 589832 | tf_op jit(solution)/shard_map/ppermute | solution.py:423
  16.4 2.2 %collective-permute-start.4 = (bf16[5,128,128]{2,1,0:T(8,128)(2,1)S(1)}, bf16[5,128,128]{2,1,0:T(8,128)(2,1)S(1)}, u32[]{:S(2)}, u32[]{:S(2)}) collective-permute-start(bf16[5,128,128]{2,1,0:T(8,128)(2,1)S(1)} %get-tuple-element.49), channel_id=1, source_target_pairs={{1,2},{3,4},{5,6},{7,8},{9,10},{11,12},{13,14},{15,0},{0,15},{2,1}... | collective-permute-start | bytes 491528 | tf_op jit(solution)/shard_map/ppermute | solution.py:423
  18.6 0.0 collective-permute-done.1.same_ref
  18.6 1.2 %lead.1 = (bf16[1536,1664]{1,0:T(8,128)(2,1)S(1)}, f32[512,1536]{1,0:T(8,128)S(1)}) custom-call(bf16[528,128]{1,0:T(8,128)(2,1)S(1)} %collective-permute-done.1.same_ref, bf16[512,128]{1,0:T(8,128)(2,1)S(1)} %collective-permute-done.2.swap_ref, bf16[1536,1664]{1,0:T(8,128)(2,1)S(1)} %get-tuple-element.41.before_panel, ...), custom_call_target="tpu_custom_call", output_to_operand_aliasing={{0}: (2, {}), {1}: (3, {})} | custom-call | flops 1200000000 | tf_op jit(solution)/shard_map/lead/pallas_call | solution.py:426
  19.8 0.4 %collective-permute-done.3.refs_0_ = bf16[7,128,128]{2,1,0:T(8,128)(2,1)S(1)} collective-permute-done((bf16[7,128,128]{2,1,0:T(8,128)(2,1)S(1)}, bf16[7,128,128]{2,1,0:T(8,128)(2,1)S(1)}, u32[]{:S(2)}, u32[]{:S(2)}) %collective-permute-start.3) | collective-permute-done | bytes 229408 | tf_op jit(solution)/shard_map/ppermute | solution.py:423
  20.2 2.0 %near.1 = (bf16[1536,1664]{1,0:T(8,128)(2,1)S(1)}, bf16[2,4,128,128]{3,2,1,0:T(8,128)(2,1)S(1)}, bf16[2,4,128,128]{3,2,1,0:T(8,128)(2,1)S(1)}, f32[256,768]{1,0:...) custom-call(s32[8,8]{1,0:T(8,128)S(1)} %get-tuple-element.33.held_ref, ...), custom_call_target="tpu_custom_call", output_to_operand_aliasing={{0}: (3, {})} | custom-call | flops 500000000 | tf_op jit(solution)/shard_map/near/pallas_call | solution.py:443
  22.1 0.1 collective-permute-start.7
  22.2 0.1 collective-permute-done.5.row_ref
  22.3 0.8 %far.2 = (bf16[1536,1664]{1,0:T(8,128)(2,1)S(1)}, bf16[1,4,128,128]{3,2,1,0:T(8,128)(2,1)S(1)}, bf16[1,4,128,128]{3,2,1,0:T(8,128)(2,1)S(1)}) custom-call(s32[8,8]{1,0:T(8,128)S(1)} %get-tuple-element.33.held_ref, f32[48,128]{1,0:T(8,128)S(1)} %get-tuple-element.38.mask_ref, ...), custom_call_target="tpu_custom_call", output_to_operand_aliasing={{0}: (6, {})} | custom-call | flops 20000000000 | tf_op jit(solution)/shard_map/far/pallas_call | solution.py:471
  23.1 0.5 %collective-permute-start.8 = (bf16[1,4,128,128]{3,2,1,0:T(8,128)(2,1)S(1)}, bf16[1,4,128,128]{3,2,1,0:T(8,128)(2,1)S(1)}, u32[]{:S(2)}, u32[]{:S(2)}) collective-permute-start(bf16[1,4,128,128]{3,2,1,0:T(8,128)(2,1)S(1)} %get-tuple-element.58), channel_id=1, source_target_pairs={{0,1},{1,0},{2,3},{3,2},{4,5},{5,4},{6,7},{7,6},{8,9},{9,8},{10,11... | collective-permute-start | bytes 393224 | tf_op jit(solution)/shard_map/ppermute | solution.py:487
  23.6 0.4 %collective-permute-done.4.row_ref = bf16[5,128,128]{2,1,0:T(8,128)(2,1)S(1)} collective-permute-done((bf16[5,128,128]{2,1,0:T(8,128)(2,1)S(1)}, bf16[5,128,128]{2,1,0:T(8,128)(2,1)S(1)}, u32[]{:S(2)}, u32[]{:S(2)}) %collective-permute-start.4) | collective-permute-done | bytes 163872 | tf_op jit(solution)/shard_map/ppermute | solution.py:423
  24.0 1.0 %far.3 = (bf16[1536,1664]{1,0:T(8,128)(2,1)S(1)}, bf16[1,4,128,128]{3,2,1,0:T(8,128)(2,1)S(1)}, bf16[1,4,128,128]{3,2,1,0:T(8,128)(2,1)S(1)}) custom-call(s32[8,8]{1,0:T(8,128)S(1)} %get-tuple-element.33.held_ref, f32[48,128]{1,0:T(8,128)S(1)} %get-tuple-element.38.mask_ref, ...), custom_call_target="tpu_custom_call", output_to_operand_aliasing={{0}: (6, {})} | custom-call | tf_op jit(solution)/shard_map/far/pallas_call | solution.py:471
  25.1 1.4 %collective-permute-start.6 = (bf16[1,4,128,128]{3,2,1,0:T(8,128)(2,1)S(1)}, bf16[1,4,128,128]{3,2,1,0:T(8,128)(2,1)S(1)}, u32[]{:S(2)}, u32[]{:S(2)}) collective-permute-start(bf16[1,4,128,128]{3,2,1,0:T(8,128)(2,1)S(1)} %get-tuple-element.53), channel_id=1, source_target_pairs={{0,1},{1,0},{2,3},{3,2},{4,5},{5,4},{6,7},{7,6},{8,9},{9,8},{10,11... | collective-permute-start | bytes 393224 | tf_op jit(solution)/shard_map/ppermute | solution.py:487
  26.4 0.0 collective-permute-done.8.refs_4_
  26.4 1.0 %store.1.before_ref = bf16[8,4,128,128]{3,2,1,0:T(8,128)(2,1)} custom-call(bf16[1,4,128,128]{3,2,1,0:T(8,128)(2,1)S(1)} %get-tuple-element.54.refs_0_, bf16[1,4,128,128]{3,2,1,0:T(8,128)(2,1)S(1)} %get-tuple-element.55.refs_1_, bf16[2,4,128,128]{3,2,1,0:T(8,128)(2,1)S(1)} %get-tuple-element.56.refs_2_, ...), custom_call_target="tpu_custom_call" | custom-call | tf_op jit(solution)/shard_map/store/pallas_call | solution.py:489
  27.4 0.7 %finish.1 = bf16[8,4,128,128]{3,2,1,0:T(8,128)(2,1)} custom-call(bf16[1,4,128,128]{3,2,1,0:T(8,128)(2,1)S(1)} %collective-permute-done.6.got_ref, bf16[8,4,128,128]{3,2,1,0:T(8,128)(2,1)} %store.1.before_ref), custom_call_target="tpu_custom_call", output_to_operand_aliasing={{}: (1, {})} | custom-call | tf_op jit(solution)/shard_map/finish/pallas_call | solution.py:499
  (4 shorter events, 0.0 us)
Async XLA Ops:
  0.9 6.4 %collective-permute-start = (bf16[8,4,128,128]{3,2,1,0:T(8,128)(2,1)}, bf16[8,4,128,128]{3,2,1,0:T(8,128)(2,1)S(1)}, u32[]{:S(2)}, u32[]{:S(2)}) collective-permute-start(bf16[8,4,128,128]{3,2,1,0:T(8,128)(2,1)} %matrix_ref.7), channel_id=1, source_target_pairs={{0,1},{1,0},{2,3},{3,2},{4,5},{5,4},{6,7},{7,6},{8,9},{9,8},{10,11... | collective-permute-start | bytes 3145736 | tf_op jit(solution)/shard_map/ppermute | solution.py:380
  1.4 17.2 %collective-permute-start.1 = (bf16[528,128]{1,0:T(8,128)(2,1)S(1)}, bf16[528,128]{1,0:T(8,128)(2,1)S(1)}, u32[]{:S(2)}, u32[]{:S(2)}) collective-permute-start(bf16[528,128]{1,0:T(8,128)(2,1)S(1)} %get-tuple-element.39), channel_id=1, source_target_pairs={{0,2},{2,4},{4,6},{6,8},{8,10},{10,12},{12,14},{14,0},{1,15},{3,1}... | collective-permute-start | bytes 405512 | tf_op jit(solution)/shard_map/ppermute | solution.py:377
  4.0 14.6 %collective-permute-start.2 = (bf16[512,128]{1,0:T(8,128)(2,1)S(1)}, bf16[512,128]{1,0:T(8,128)(2,1)S(1)}, u32[]{:S(2)}, u32[]{:S(2)}) collective-permute-start(bf16[512,128]{1,0:T(8,128)(2,1)S(1)} %get-tuple-element.40), channel_id=1, source_target_pairs={{1,2},{3,4},{5,6},{7,8},{9,10},{11,12},{13,14},{15,0},{0,15},{2,1}... | collective-permute-start | bytes 393224 | tf_op jit(solution)/shard_map/ppermute | solution.py:378
  11.8 8.3 %collective-permute-start.3 = (bf16[7,128,128]{2,1,0:T(8,128)(2,1)S(1)}, bf16[7,128,128]{2,1,0:T(8,128)(2,1)S(1)}, u32[]{:S(2)}, u32[]{:S(2)}) collective-permute-start(bf16[7,128,128]{2,1,0:T(8,128)(2,1)S(1)} %get-tuple-element.45), channel_id=1, source_target_pairs={{1,2},{3,4},{5,6},{7,8},{9,10},{11,12},{13,14},{15,0},{0,15},{2,1}... | collective-permute-start | bytes 688136 | tf_op jit(solution)/shard_map/ppermute | solution.py:423
  14.1 8.1 %collective-permute-start.5 = (bf16[6,128,128]{2,1,0:T(8,128)(2,1)S(1)}, bf16[6,128,128]{2,1,0:T(8,128)(2,1)S(1)}, u32[]{:S(2)}, u32[]{:S(2)}) collective-permute-start(bf16[6,128,128]{2,1,0:T(8,128)(2,1)S(1)} %get-tuple-element.50), channel_id=1, source_target_pairs={{1,2},{3,4},{5,6},{7,8},{9,10},{11,12},{13,14},{15,0},{0,15},{2,1}... | collective-permute-start | bytes 589832 | tf_op jit(solution)/shard_map/ppermute | solution.py:423
  16.4 7.7 %collective-permute-start.4 = (bf16[5,128,128]{2,1,0:T(8,128)(2,1)S(1)}, bf16[5,128,128]{2,1,0:T(8,128)(2,1)S(1)}, u32[]{:S(2)}, u32[]{:S(2)}) collective-permute-start(bf16[5,128,128]{2,1,0:T(8,128)(2,1)S(1)} %get-tuple-element.49), channel_id=1, source_target_pairs={{1,2},{3,4},{5,6},{7,8},{9,10},{11,12},{13,14},{15,0},{0,15},{2,1}... | collective-permute-start | bytes 491528 | tf_op jit(solution)/shard_map/ppermute | solution.py:423
  22.1 4.3 %collective-permute-start.7 = (bf16[2,4,128,128]{3,2,1,0:T(8,128)(2,1)S(1)}, bf16[2,4,128,128]{3,2,1,0:T(8,128)(2,1)S(1)}, u32[]{:S(2)}, u32[]{:S(2)}) collective-permute-start(bf16[2,4,128,128]{3,2,1,0:T(8,128)(2,1)S(1)} %get-tuple-element.57), channel_id=1, source_target_pairs={{0,1},{1,0},{2,3},{3,2},{4,5},{5,4},{6,7},{7,6},{8,9},{9,8},{10,11... | collective-permute-start | bytes 786440 | tf_op jit(solution)/shard_map/ppermute | solution.py:466
  23.1 3.3 %collective-permute-start.8 = (bf16[1,4,128,128]{3,2,1,0:T(8,128)(2,1)S(1)}, bf16[1,4,128,128]{3,2,1,0:T(8,128)(2,1)S(1)}, u32[]{:S(2)}, u32[]{:S(2)}) collective-permute-start(bf16[1,4,128,128]{3,2,1,0:T(8,128)(2,1)S(1)} %get-tuple-element.58), channel_id=1, source_target_pairs={{0,1},{1,0},{2,3},{3,2},{4,5},{5,4},{6,7},{7,6},{8,9},{9,8},{10,11... | collective-permute-start | bytes 393224 | tf_op jit(solution)/shard_map/ppermute | solution.py:487
  25.1 2.3 %collective-permute-start.6 = (bf16[1,4,128,128]{3,2,1,0:T(8,128)(2,1)S(1)}, bf16[1,4,128,128]{3,2,1,0:T(8,128)(2,1)S(1)}, u32[]{:S(2)}, u32[]{:S(2)}) collective-permute-start(bf16[1,4,128,128]{3,2,1,0:T(8,128)(2,1)S(1)} %get-tuple-element.53), channel_id=1, source_target_pairs={{0,1},{1,0},{2,3},{3,2},{4,5},{5,4},{6,7},{7,6},{8,9},{9,8},{10,11... | collective-permute-start | bytes 393224 | tf_op jit(solution)/shard_map/ppermute | solution.py:487

commit v7 on v6

--- a/solution.py
+++ b/solution.py
@@ -122,7 +122,7 @@
 
 
 def base_kernel(turn, held_ref, matrix_ref, other_ref, *refs):
-    panel_ref, first_ref, mask_ref, own_ref, columns_ref, keep_ref, sems = refs[-7:]
+    panel_ref, first_ref, mask_ref, spot_ref, own_ref, columns_ref, keep_ref, sems = refs[-8:]
     rows, half, size = own_ref.shape[0], own_ref.shape[1], own_ref.shape[2]
     reach = REACH
     width = rows + reach
@@ -152,6 +152,14 @@
             for k in range(width):
                 at = i * width + k
                 mask_ref[at : at + 1, :] = jnp.full((1, size), keep_ref[i, k], jnp.float32)
+        window = 2 * reach + 1
+        for i in range(spot_ref.shape[0] // (2 * half * window)):
+            for s in range(2 * half):
+                place = own_place(columns_ref, i + reach, s, width)
+                for d in range(window):
+                    at = (i * 2 * half + s) * window + d
+                    taken = jnp.where(place == i + d, 1, 0)
+                    spot_ref[at : at + 1, :] = jnp.full((1, size), taken, jnp.float32)
         for p in range(width // 2):
             low = max(reach, 2 * p - reach)
             high = min(width, 2 * p + 2 + reach)
@@ -266,12 +274,10 @@
 
 
 def far_kernel(
-    far, i, held_ref, mask_ref, part_ref, high_ref, cube_ref, row_ref, before_ref,
-    panel_ref, stay_ref, leave_ref, square, result, columns_ref, sem
+    far, i, mask_ref, spot_ref, part_ref, high_ref, cube_ref, row_ref, before_ref,
+    panel_ref, stay_ref, leave_ref, square, result
 ):
     reach = REACH
-    scalars = pltpu.make_async_copy(held_ref, columns_ref, sem)
-    scalars.start()
     half, size = stay_ref.shape[1], stay_ref.shape[2]
     width = panel_ref.shape[0] // size
     low_cols = reach + far
@@ -279,7 +285,6 @@
     mine = blocks(i, i + 1, size)
     for k in range(reach + 1 + i):
         panel_ref[mine, blocks(k, k + 1, size)] = row_ref[k]
-    result[:, blocks(far_cols, far_cols + 1, size)] = jnp.zeros((size, size), result.dtype)
     left = panel_ref[blocks(reach + i, reach + i + 1, size), blocks(0, far, size)]
     for p in range(low_cols // 2):
         cols = blocks(2 * p, 2 * p + 2, size)
@@ -302,11 +307,14 @@
         else:
             kept = high_ref[mine, blocks(2 * p - low_cols, 2 * p + 2 - low_cols, size)]
         result[:, cols] = (3.0 * kept.astype(jnp.float32) - 2.0 * value).astype(result.dtype)
-    scalars.wait()
+    window = 2 * reach + 1
     for s in range(2 * half):
-        place = pl.multiple_of(own_place(columns_ref, i + reach, s, far_cols) * size, size)
+        block = jnp.zeros((size, size), result.dtype)
+        for d in range(window):
+            at = (i * 2 * half + s) * window + d
+            block = jnp.where(spot_ref[at : at + 1, :] > 0, result[:, blocks(i + d, i + d + 1, size)], block)
         target = stay_ref if s < half else leave_ref
-        target[0, s % half] = result[:, pl.ds(place, size)]
+        target[0, s % half] = block
 
 
 def write_rows(pieces, out_ref, sems):
@@ -383,14 +391,19 @@
     scalars = pltpu.SMEM(columns.shape, columns.dtype)
     panel_shape = jax.ShapeDtypeStruct((width * size, (width + 1) * size), dtype)
     first_shape = jax.ShapeDtypeStruct((reach * size, width * size), jnp.float32)
-    base_shapes = (panel_shape, first_shape, jax.ShapeDtypeStruct((reach * width, size), jnp.float32))
+    base_shapes = (
+        panel_shape,
+        first_shape,
+        jax.ShapeDtypeStruct((reach * width, size), jnp.float32),
+        jax.ShapeDtypeStruct((far * 2 * own_slots * (2 * reach + 1), size), jnp.float32),
+    )
 
     def base(turn, *before):
         return pl.pallas_call(
             functools.partial(base_kernel, turn),
             out_shape=base_shapes,
             in_specs=[VMEM, HBM, VMEM] + [VMEM] * len(before),
-            out_specs=(VMEM,) * 3,
+            out_specs=(VMEM,) * 4,
             input_output_aliases={3 + n: n for n in range(len(before))},
             scratch_shapes=[
                 pltpu.VMEM(matrix.shape, dtype),
@@ -422,7 +435,7 @@
     )(held, in_place, other, early[2])
     arrived = {f: lax.ppermute(packed[f], axes, swap) for f in reversed(range(lead))}
 
-    panel, first_part, mask = base(1, *early)
+    panel, first_part, mask, spot = base(1, *early)
     panel, first_part = pl.pallas_call(
         functools.partial(lead_kernel, own_slots),
         out_shape=(panel_shape, first_shape),
@@ -476,14 +489,12 @@
             input_output_aliases={6: 0},
             scratch_shapes=[
                 pltpu.VMEM((size, low_cols * size), dtype),
-                pltpu.VMEM((size, (far_cols + 1) * size), dtype),
-                scalars,
-                pltpu.SemaphoreType.DMA,
+                pltpu.VMEM((size, far_cols * size), dtype),
             ],
             compiler_params=limit(16),
             cost_estimate=HEAVY if i else LIGHT,
             name="far",
-        )(held, mask, part, high, cube, arrived[i], panel)
+        )(mask, spot, part, high, cube, arrived[i], panel)
         got[i] = lax.ppermute(leave, "col", beside)
     pieces = [*[stay[i] for i in range(far)], stay_near, arrived_near, *[got[i] for i in range(1, far)]]
     out = pl.pallas_call(

time: 28.4 us -> 28.2 us (level)
  no operation moved by 1% of the time
where the time goes in v7:
time: 28.2 us; the launch traced here: 27.9 us
  starting transfers between devices  15 us (53%)
  Pallas kernels  11.9 us (42%)
  waiting for transfers between devices  0.95 us (3%)
    ppermute x3, starting transfers between devices, local(): lax.ppermute(packed[f], axes, swap)  6.63 us
    ppermute x1, starting transfers between devices, local(): swap_rows = lax.ppermute(swap_edge, axes, swap)  3.31 us
    pallas_call x2, Pallas kernels, base(): pl.pallas_call(functools.partial(base_kernel, turn), out_shape=base_shape...  3.11 us
    ppermute x1, starting transfers between devices, local(): same_rows = lax.ppermute(same_edge, axes, same)  2.58 us
    pallas_call x1, Pallas kernels, local(): pl.pallas_call(functools.partial(near_kernel, far), out_shape=(panel_shap...  1.96 us
    ppermute x2, starting transfers between devices, local(): got[i] = lax.ppermute(leave, 'col', beside)  1.87 us
    pallas_call x2, Pallas kernels, local(): pl.pallas_call(functools.partial(far_kernel, far, i), out_shape=(panel_sh...  1.68 us
    pallas_call x1, Pallas kernels, local(): pl.pallas_call(pack_kernel, out_shape=tuple((jax.ShapeDtypeStruct((reach...  1.4 us
  transfers between devices with their start and end apart: 9, of which 3 were waited for; matrix products, arithmetic and copies ran while one was open for 0% of the time, Pallas kernels for 37%

profile of v7, /device:TPU:0, one launch (start us, length us, event | category | flops | bytes accessed | tf_op | source)
XLA Modules:
  0.0 27.9 jit_solution(966151942005855176)
XLA Ops:
  0.0 0.9 %edge.1 = (bf16[528,128]{1,0:T(8,128)(2,1)S(1)}, bf16[512,128]{1,0:T(8,128)(2,1)S(1)}, s32[8,8]{1,0:T(8,128)S(1)}) custom-call(s32[8,8]{1,0:T(8,128)} %columns_ref.1, bf16[8,4,128,128]{3,2,1,0:T(8,128)(2,1)} %matrix_ref.7), custom_call_target="tpu_custom_call" | custom-call | tf_op jit(solution)/shard_map/edge/pallas_call | solution.py:371
  0.9 0.5 %collective-permute-start = (bf16[8,4,128,128]{3,2,1,0:T(8,128)(2,1)}, bf16[8,4,128,128]{3,2,1,0:T(8,128)(2,1)S(1)}, u32[]{:S(2)}, u32[]{:S(2)}) collective-permute-start(bf16[8,4,128,128]{3,2,1,0:T(8,128)(2,1)} %matrix_ref.7), channel_id=1, source_target_pairs={{0,1},{1,0},{2,3},{3,2},{4,5},{5,4},{6,7},{7,6},{8,9},{9,8},{10,11... | collective-permute-start | bytes 3145736 | tf_op jit(solution)/shard_map/ppermute | solution.py:388
  1.4 2.6 %collective-permute-start.1 = (bf16[528,128]{1,0:T(8,128)(2,1)S(1)}, bf16[528,128]{1,0:T(8,128)(2,1)S(1)}, u32[]{:S(2)}, u32[]{:S(2)}) collective-permute-start(bf16[528,128]{1,0:T(8,128)(2,1)S(1)} %get-tuple-element.43), channel_id=1, source_target_pairs={{0,2},{2,4},{4,6},{6,8},{8,10},{10,12},{12,14},{14,0},{1,15},{3,1}... | collective-permute-start | bytes 405512 | tf_op jit(solution)/shard_map/ppermute | solution.py:385
  4.0 3.3 %collective-permute-start.2 = (bf16[512,128]{1,0:T(8,128)(2,1)S(1)}, bf16[512,128]{1,0:T(8,128)(2,1)S(1)}, u32[]{:S(2)}, u32[]{:S(2)}) collective-permute-start(bf16[512,128]{1,0:T(8,128)(2,1)S(1)} %get-tuple-element.44), channel_id=1, source_target_pairs={{1,2},{3,4},{5,6},{7,8},{9,10},{11,12},{13,14},{15,0},{0,15},{2,1}... | collective-permute-start | bytes 393224 | tf_op jit(solution)/shard_map/ppermute | solution.py:386
  7.3 0.0 collective-permute-done.other_ref
  7.3 3.1 %base.2 = (bf16[1536,1664]{1,0:T(8,128)(2,1)S(1)}, f32[512,1536]{1,0:T(8,128)S(1)}, f32[48,128]{1,0:T(8,128)S(1)}, f32[144,128]{1,0:T(8,128)S(1)}) custom-call(s32[8,8]{1,0:T(8,128)S(1)} %get-tuple-element.35.held_ref, bf16[8,4,128,128]{3,2,1,0:T(8,128)(2,1)} %matrix_ref.7, bf16[8,4,128,128]{3,2,1,0:T(8,128)(2,1)S(1)} %collective-permute-done.other_ref), custom_call_target="tpu_custom_call" | custom-call | tf_op jit(solution)/shard_map/base/pallas_call | solution.py:402
  10.4 1.4 %pack.1 = (bf16[5,128,128]{2,1,0:T(8,128)(2,1)S(1)}, bf16[6,128,128]{2,1,0:T(8,128)(2,1)S(1)}, bf16[7,128,128]{2,1,0:T(8,128)(2,1)S(1)}) custom-call(s32[8,8]{1,0:T(8,128)S(1)} %get-tuple-element.35.held_ref, bf16[8,4,128,128]{3,2,1,0:T(8,128)(2,1)} %matrix_ref.7, bf16[8,4,128,128]{3,2,1,0:T(8,128)(2,1)S(1)} %collective-permute-done.other_ref, ...), custom_call_target="tpu_custom_call" | custom-call | tf_op jit(solution)/shard_map/pack/pallas_call | solution.py:420
  11.8 2.2 %collective-permute-start.3 = (bf16[7,128,128]{2,1,0:T(8,128)(2,1)S(1)}, bf16[7,128,128]{2,1,0:T(8,128)(2,1)S(1)}, u32[]{:S(2)}, u32[]{:S(2)}) collective-permute-start(bf16[7,128,128]{2,1,0:T(8,128)(2,1)S(1)} %get-tuple-element.49), channel_id=1, source_target_pairs={{1,2},{3,4},{5,6},{7,8},{9,10},{11,12},{13,14},{15,0},{0,15},{2,1}... | collective-permute-start | bytes 688136 | tf_op jit(solution)/shard_map/ppermute | solution.py:436
  14.0 2.3 %collective-permute-start.5 = (bf16[6,128,128]{2,1,0:T(8,128)(2,1)S(1)}, bf16[6,128,128]{2,1,0:T(8,128)(2,1)S(1)}, u32[]{:S(2)}, u32[]{:S(2)}) collective-permute-start(bf16[6,128,128]{2,1,0:T(8,128)(2,1)S(1)} %get-tuple-element.54), channel_id=1, source_target_pairs={{1,2},{3,4},{5,6},{7,8},{9,10},{11,12},{13,14},{15,0},{0,15},{2,1}... | collective-permute-start | bytes 589832 | tf_op jit(solution)/shard_map/ppermute | solution.py:436
  16.3 2.1 %collective-permute-start.4 = (bf16[5,128,128]{2,1,0:T(8,128)(2,1)S(1)}, bf16[5,128,128]{2,1,0:T(8,128)(2,1)S(1)}, u32[]{:S(2)}, u32[]{:S(2)}) collective-permute-start(bf16[5,128,128]{2,1,0:T(8,128)(2,1)S(1)} %get-tuple-element.53), channel_id=1, source_target_pairs={{1,2},{3,4},{5,6},{7,8},{9,10},{11,12},{13,14},{15,0},{0,15},{2,1}... | collective-permute-start | bytes 491528 | tf_op jit(solution)/shard_map/ppermute | solution.py:436
  18.5 0.0 collective-permute-done.2.swap_ref
  18.5 0.0 collective-permute-done.1.same_ref
  18.5 1.2 %lead.1 = (bf16[1536,1664]{1,0:T(8,128)(2,1)S(1)}, f32[512,1536]{1,0:T(8,128)S(1)}) custom-call(bf16[528,128]{1,0:T(8,128)(2,1)S(1)} %collective-permute-done.1.same_ref, bf16[512,128]{1,0:T(8,128)(2,1)S(1)} %collective-permute-done.2.swap_ref, bf16[1536,1664]{1,0:T(8,128)(2,1)S(1)} %get-tuple-element.45.before_panel, ...), custom_call_target="tpu_custom_call", output_to_operand_aliasing={{0}: (2, {}), {1}: (3, {})} | custom-call | flops 1200000000 | tf_op jit(solution)/shard_map/lead/pallas_call | solution.py:439
  19.7 0.5 %collective-permute-done.3.refs_0_ = bf16[7,128,128]{2,1,0:T(8,128)(2,1)S(1)} collective-permute-done((bf16[7,128,128]{2,1,0:T(8,128)(2,1)S(1)}, bf16[7,128,128]{2,1,0:T(8,128)(2,1)S(1)}, u32[]{:S(2)}, u32[]{:S(2)}) %collective-permute-start.3) | collective-permute-done | bytes 229408 | tf_op jit(solution)/shard_map/ppermute | solution.py:436
  20.1 2.0 %near.1 = (bf16[1536,1664]{1,0:T(8,128)(2,1)S(1)}, bf16[2,4,128,128]{3,2,1,0:T(8,128)(2,1)S(1)}, bf16[2,4,128,128]{3,2,1,0:T(8,128)(2,1)S(1)}, f32[256,768]{1,0:...) custom-call(s32[8,8]{1,0:T(8,128)S(1)} %get-tuple-element.35.held_ref, ...), custom_call_target="tpu_custom_call", output_to_operand_aliasing={{0}: (3, {})} | custom-call | flops 500000000 | tf_op jit(solution)/shard_map/near/pallas_call | solution.py:456
  22.1 0.1 collective-permute-start.7
  22.2 0.1 collective-permute-done.5.row_ref
  22.3 0.8 %far.2 = (bf16[1536,1664]{1,0:T(8,128)(2,1)S(1)}, bf16[1,4,128,128]{3,2,1,0:T(8,128)(2,1)S(1)}, bf16[1,4,128,128]{3,2,1,0:T(8,128)(2,1)S(1)}) custom-call(f32[48,128]{1,0:T(8,128)S(1)} %get-tuple-element.41.mask_ref, f32[144,128]{1,0:T(8,128)S(1)} %get-tuple-element.42.spot_ref, ...), custom_call_target="tpu_custom_call", output_to_operand_aliasing={{0}: (6, {})} | custom-call | flops 20000000000 | tf_op jit(solution)/shard_map/far/pallas_call | solution.py:484
  23.1 0.5 %collective-permute-start.8 = (bf16[1,4,128,128]{3,2,1,0:T(8,128)(2,1)S(1)}, bf16[1,4,128,128]{3,2,1,0:T(8,128)(2,1)S(1)}, u32[]{:S(2)}, u32[]{:S(2)}) collective-permute-start(bf16[1,4,128,128]{3,2,1,0:T(8,128)(2,1)S(1)} %get-tuple-element.62), channel_id=1, source_target_pairs={{0,1},{1,0},{2,3},{3,2},{4,5},{5,4},{6,7},{7,6},{8,9},{9,8},{10,11... | collective-permute-start | bytes 393224 | tf_op jit(solution)/shard_map/ppermute | solution.py:498
  23.6 0.4 %collective-permute-done.4.row_ref = bf16[5,128,128]{2,1,0:T(8,128)(2,1)S(1)} collective-permute-done((bf16[5,128,128]{2,1,0:T(8,128)(2,1)S(1)}, bf16[5,128,128]{2,1,0:T(8,128)(2,1)S(1)}, u32[]{:S(2)}, u32[]{:S(2)}) %collective-permute-start.4) | collective-permute-done | bytes 163872 | tf_op jit(solution)/shard_map/ppermute | solution.py:436
  24.0 0.9 %far.3 = (bf16[1536,1664]{1,0:T(8,128)(2,1)S(1)}, bf16[1,4,128,128]{3,2,1,0:T(8,128)(2,1)S(1)}, bf16[1,4,128,128]{3,2,1,0:T(8,128)(2,1)S(1)}) custom-call(f32[48,128]{1,0:T(8,128)S(1)} %get-tuple-element.41.mask_ref, f32[144,128]{1,0:T(8,128)S(1)} %get-tuple-element.42.spot_ref, ...), custom_call_target="tpu_custom_call", output_to_operand_aliasing={{0}: (6, {})} | custom-call | tf_op jit(solution)/shard_map/far/pallas_call | solution.py:484
  24.9 1.4 %collective-permute-start.6 = (bf16[1,4,128,128]{3,2,1,0:T(8,128)(2,1)S(1)}, bf16[1,4,128,128]{3,2,1,0:T(8,128)(2,1)S(1)}, u32[]{:S(2)}, u32[]{:S(2)}) collective-permute-start(bf16[1,4,128,128]{3,2,1,0:T(8,128)(2,1)S(1)} %get-tuple-element.57), channel_id=1, source_target_pairs={{0,1},{1,0},{2,3},{3,2},{4,5},{5,4},{6,7},{7,6},{8,9},{9,8},{10,11... | collective-permute-start | bytes 393224 | tf_op jit(solution)/shard_map/ppermute | solution.py:498
  26.3 1.0 %store.1.before_ref = bf16[8,4,128,128]{3,2,1,0:T(8,128)(2,1)} custom-call(bf16[1,4,128,128]{3,2,1,0:T(8,128)(2,1)S(1)} %get-tuple-element.58.refs_0_, bf16[1,4,128,128]{3,2,1,0:T(8,128)(2,1)S(1)} %get-tuple-element.59.refs_1_, bf16[2,4,128,128]{3,2,1,0:T(8,128)(2,1)S(1)} %get-tuple-element.60.refs_2_, ...), custom_call_target="tpu_custom_call" | custom-call | tf_op jit(solution)/shard_map/store/pallas_call | solution.py:500
  27.2 0.7 %finish.1 = bf16[8,4,128,128]{3,2,1,0:T(8,128)(2,1)} custom-call(bf16[1,4,128,128]{3,2,1,0:T(8,128)(2,1)S(1)} %collective-permute-done.6.got_ref, bf16[8,4,128,128]{3,2,1,0:T(8,128)(2,1)} %store.1.before_ref), custom_call_target="tpu_custom_call", output_to_operand_aliasing={{}: (1, {})} | custom-call | tf_op jit(solution)/shard_map/finish/pallas_call | solution.py:510
  (4 shorter events, 0.0 us)
Async XLA Ops:
  0.9 6.4 %collective-permute-start = (bf16[8,4,128,128]{3,2,1,0:T(8,128)(2,1)}, bf16[8,4,128,128]{3,2,1,0:T(8,128)(2,1)S(1)}, u32[]{:S(2)}, u32[]{:S(2)}) collective-permute-start(bf16[8,4,128,128]{3,2,1,0:T(8,128)(2,1)} %matrix_ref.7), channel_id=1, source_target_pairs={{0,1},{1,0},{2,3},{3,2},{4,5},{5,4},{6,7},{7,6},{8,9},{9,8},{10,11... | collective-permute-start | bytes 3145736 | tf_op jit(solution)/shard_map/ppermute | solution.py:388
  1.4 17.1 %collective-permute-start.1 = (bf16[528,128]{1,0:T(8,128)(2,1)S(1)}, bf16[528,128]{1,0:T(8,128)(2,1)S(1)}, u32[]{:S(2)}, u32[]{:S(2)}) collective-permute-start(bf16[528,128]{1,0:T(8,128)(2,1)S(1)} %get-tuple-element.43), channel_id=1, source_target_pairs={{0,2},{2,4},{4,6},{6,8},{8,10},{10,12},{12,14},{14,0},{1,15},{3,1}... | collective-permute-start | bytes 405512 | tf_op jit(solution)/shard_map/ppermute | solution.py:385
  4.0 14.5 %collective-permute-start.2 = (bf16[512,128]{1,0:T(8,128)(2,1)S(1)}, bf16[512,128]{1,0:T(8,128)(2,1)S(1)}, u32[]{:S(2)}, u32[]{:S(2)}) collective-permute-start(bf16[512,128]{1,0:T(8,128)(2,1)S(1)} %get-tuple-element.44), channel_id=1, source_target_pairs={{1,2},{3,4},{5,6},{7,8},{9,10},{11,12},{13,14},{15,0},{0,15},{2,1}... | collective-permute-start | bytes 393224 | tf_op jit(solution)/shard_map/ppermute | solution.py:386
  11.8 8.3 %collective-permute-start.3 = (bf16[7,128,128]{2,1,0:T(8,128)(2,1)S(1)}, bf16[7,128,128]{2,1,0:T(8,128)(2,1)S(1)}, u32[]{:S(2)}, u32[]{:S(2)}) collective-permute-start(bf16[7,128,128]{2,1,0:T(8,128)(2,1)S(1)} %get-tuple-element.49), channel_id=1, source_target_pairs={{1,2},{3,4},{5,6},{7,8},{9,10},{11,12},{13,14},{15,0},{0,15},{2,1}... | collective-permute-start | bytes 688136 | tf_op jit(solution)/shard_map/ppermute | solution.py:436
  14.0 8.2 %collective-permute-start.5 = (bf16[6,128,128]{2,1,0:T(8,128)(2,1)S(1)}, bf16[6,128,128]{2,1,0:T(8,128)(2,1)S(1)}, u32[]{:S(2)}, u32[]{:S(2)}) collective-permute-start(bf16[6,128,128]{2,1,0:T(8,128)(2,1)S(1)} %get-tuple-element.54), channel_id=1, source_target_pairs={{1,2},{3,4},{5,6},{7,8},{9,10},{11,12},{13,14},{15,0},{0,15},{2,1}... | collective-permute-start | bytes 589832 | tf_op jit(solution)/shard_map/ppermute | solution.py:436
  16.3 7.7 %collective-permute-start.4 = (bf16[5,128,128]{2,1,0:T(8,128)(2,1)S(1)}, bf16[5,128,128]{2,1,0:T(8,128)(2,1)S(1)}, u32[]{:S(2)}, u32[]{:S(2)}) collective-permute-start(bf16[5,128,128]{2,1,0:T(8,128)(2,1)S(1)} %get-tuple-element.53), channel_id=1, source_target_pairs={{1,2},{3,4},{5,6},{7,8},{9,10},{11,12},{13,14},{15,0},{0,15},{2,1}... | collective-permute-start | bytes 491528 | tf_op jit(solution)/shard_map/ppermute | solution.py:436
  22.1 4.1 %collective-permute-start.7 = (bf16[2,4,128,128]{3,2,1,0:T(8,128)(2,1)S(1)}, bf16[2,4,128,128]{3,2,1,0:T(8,128)(2,1)S(1)}, u32[]{:S(2)}, u32[]{:S(2)}) collective-permute-start(bf16[2,4,128,128]{3,2,1,0:T(8,128)(2,1)S(1)} %get-tuple-element.61), channel_id=1, source_target_pairs={{0,1},{1,0},{2,3},{3,2},{4,5},{5,4},{6,7},{7,6},{8,9},{9,8},{10,11... | collective-permute-start | bytes 786440 | tf_op jit(solution)/shard_map/ppermute | solution.py:479
  23.1 3.2 %collective-permute-start.8 = (bf16[1,4,128,128]{3,2,1,0:T(8,128)(2,1)S(1)}, bf16[1,4,128,128]{3,2,1,0:T(8,128)(2,1)S(1)}, u32[]{:S(2)}, u32[]{:S(2)}) collective-permute-start(bf16[1,4,128,128]{3,2,1,0:T(8,128)(2,1)S(1)} %get-tuple-element.62), channel_id=1, source_target_pairs={{0,1},{1,0},{2,3},{3,2},{4,5},{5,4},{6,7},{7,6},{8,9},{9,8},{10,11... | collective-permute-start | bytes 393224 | tf_op jit(solution)/shard_map/ppermute | solution.py:498
  24.9 2.4 %collective-permute-start.6 = (bf16[1,4,128,128]{3,2,1,0:T(8,128)(2,1)S(1)}, bf16[1,4,128,128]{3,2,1,0:T(8,128)(2,1)S(1)}, u32[]{:S(2)}, u32[]{:S(2)}) collective-permute-start(bf16[1,4,128,128]{3,2,1,0:T(8,128)(2,1)S(1)} %get-tuple-element.57), channel_id=1, source_target_pairs={{0,1},{1,0},{2,3},{3,2},{4,5},{5,4},{6,7},{7,6},{8,9},{9,8},{10,11... | collective-permute-start | bytes 393224 | tf_op jit(solution)/shard_map/ppermute | solution.py:498

commit v8 on v7

--- a/solution.py
+++ b/solution.py
@@ -90,7 +90,7 @@
         copy.wait()
 
 
-def pack_kernel(held_ref, matrix_ref, other_ref, after_ref, *refs):
+def pack_kernel(held_ref, matrix_ref, other_ref, *refs):
     out_refs, (own, columns_ref, sems) = refs[:-3], refs[-3:]
     rows, half = other_ref.shape[:2]
     lead = own.shape[0]
@@ -121,54 +121,54 @@
                     out_ref[place] = other_ref[start + index, s - half]
 
 
-def base_kernel(turn, held_ref, matrix_ref, other_ref, *refs):
-    panel_ref, first_ref, mask_ref, spot_ref, own_ref, columns_ref, keep_ref, sems = refs[-8:]
+def base_kernel(
+    held_ref, matrix_ref, other_ref,
+    panel_ref, first_ref, mask_ref, spot_ref, own_ref, columns_ref, keep_ref, sems
+):
     rows, half, size = own_ref.shape[0], own_ref.shape[1], own_ref.shape[2]
     reach = REACH
     width = rows + reach
 
-    @pl.when(lax.rem(lax.axis_index("row") + lax.axis_index("col"), 2) == turn)
-    def _():
-        copies = [
-            pltpu.make_async_copy(held_ref, columns_ref, sems.at[0]),
-            pltpu.make_async_copy(matrix_ref, own_ref, sems.at[1]),
-        ]
-        for copy in copies:
-            copy.start()
-        panel_ref[...] = jnp.zeros_like(panel_ref)
-        for copy in copies:
-            copy.wait()
-        for q in range(reach, width):
-            index = jnp.where(lax.axis_index("col") == 0, q - reach, width - 1 - q)
-            for s in range(2 * half):
-                place = pl.multiple_of(own_place(columns_ref, q, s, width) * size, size)
-                source = own_ref if s < half else other_ref
-                panel_ref[blocks(q, q + 1, size), pl.ds(place, size)] = source[index, s % half]
-        for i in range(reach):
-            for k in range(width + 1):
-                keep_ref[i, k] = 0
-            for s in range(2 * half):
-                keep_ref[i, own_place(columns_ref, i + reach, s, width)] = 1
-            for k in range(width):
-                at = i * width + k
-                mask_ref[at : at + 1, :] = jnp.full((1, size), keep_ref[i, k], jnp.float32)
-        window = 2 * reach + 1
-        for i in range(spot_ref.shape[0] // (2 * half * window)):
-            for s in range(2 * half):
-                place = own_place(columns_ref, i + reach, s, width)
-                for d in range(window):
-                    at = (i * 2 * half + s) * window + d
-                    taken = jnp.where(place == i + d, 1, 0)
-                    spot_ref[at : at + 1, :] = jnp.full((1, size), taken, jnp.float32)
-        for p in range(width // 2):
-            low = max(reach, 2 * p - reach)
-            high = min(width, 2 * p + 2 + reach)
-            cols = blocks(2 * p, 2 * p + 2, size)
-            first_ref[:, cols] = jnp.dot(
-                panel_ref[blocks(reach, 2 * reach, size), blocks(low, high, size)],
-                panel_ref[blocks(low, high, size), cols],
-                preferred_element_type=jnp.float32,
-            )
+    copies = [
+        pltpu.make_async_copy(held_ref, columns_ref, sems.at[0]),
+        pltpu.make_async_copy(matrix_ref, own_ref, sems.at[1]),
+    ]
+    for copy in copies:
+        copy.start()
+    panel_ref[...] = jnp.zeros_like(panel_ref)
+    for copy in copies:
+        copy.wait()
+    for q in range(reach, width):
+        index = jnp.where(lax.axis_index("col") == 0, q - reach, width - 1 - q)
+        for s in range(2 * half):
+            place = pl.multiple_of(own_place(columns_ref, q, s, width) * size, size)
+            source = own_ref if s < half else other_ref
+            panel_ref[blocks(q, q + 1, size), pl.ds(place, size)] = source[index, s % half]
+    for i in range(reach):
+        for k in range(width + 1):
+            keep_ref[i, k] = 0
+        for s in range(2 * half):
+            keep_ref[i, own_place(columns_ref, i + reach, s, width)] = 1
+        for k in range(width):
+            at = i * width + k
+            mask_ref[at : at + 1, :] = jnp.full((1, size), keep_ref[i, k], jnp.float32)
+    window = 2 * reach + 1
+    for i in range(spot_ref.shape[0] // (2 * half * window)):
+        for s in range(2 * half):
+            place = own_place(columns_ref, i + reach, s, width)
+            for d in range(window):
+                at = (i * 2 * half + s) * window + d
+                taken = jnp.where(place == i + d, 1, 0)
+                spot_ref[at : at + 1, :] = jnp.full((1, size), taken, jnp.float32)
+    for p in range(width // 2):
+        low = max(reach, 2 * p - reach)
+        high = min(width, 2 * p + 2 + reach)
+        cols = blocks(2 * p, 2 * p + 2, size)
+        first_ref[:, cols] = jnp.dot(
+            panel_ref[blocks(reach, 2 * reach, size), blocks(low, high, size)],
+            panel_ref[blocks(low, high, size), cols],
+            preferred_element_type=jnp.float32,
+        )
 
 
 def lead_kernel(
@@ -398,31 +398,12 @@
         jax.ShapeDtypeStruct((far * 2 * own_slots * (2 * reach + 1), size), jnp.float32),
     )
 
-    def base(turn, *before):
-        return pl.pallas_call(
-            functools.partial(base_kernel, turn),
-            out_shape=base_shapes,
-            in_specs=[VMEM, HBM, VMEM] + [VMEM] * len(before),
-            out_specs=(VMEM,) * 4,
-            input_output_aliases={3 + n: n for n in range(len(before))},
-            scratch_shapes=[
-                pltpu.VMEM(matrix.shape, dtype),
-                scalars,
-                pltpu.SMEM((reach, width + 1), jnp.int32),
-                pltpu.SemaphoreType.DMA((2,)),
-            ],
-            compiler_params=limit(12),
-            cost_estimate=LIGHT,
-            name="base",
-        )(held, in_place, other, *before)
-
-    early = base(0)
     packed = pl.pallas_call(
         pack_kernel,
         out_shape=tuple(
             jax.ShapeDtypeStruct((reach + 1 + f, size, size), dtype) for f in range(lead)
         ),
-        in_specs=[VMEM, HBM, VMEM, ANY],
+        in_specs=[VMEM, HBM, VMEM],
         out_specs=(VMEM,) * lead,
         scratch_shapes=[
             pltpu.VMEM((lead,) + matrix.shape[1:], dtype),
@@ -432,10 +413,24 @@
         compiler_params=limit(2),
         cost_estimate=LIGHT,
         name="pack",
-    )(held, in_place, other, early[2])
+    )(held, in_place, other)
     arrived = {f: lax.ppermute(packed[f], axes, swap) for f in reversed(range(lead))}
 
-    panel, first_part, mask, spot = base(1, *early)
+    panel, first_part, mask, spot = pl.pallas_call(
+        base_kernel,
+        out_shape=base_shapes,
+        in_specs=[VMEM, HBM, VMEM],
+        out_specs=(VMEM,) * 4,
+        scratch_shapes=[
+            pltpu.VMEM(matrix.shape, dtype),
+            scalars,
+            pltpu.SMEM((reach, width + 1), jnp.int32),
+            pltpu.SemaphoreType.DMA((2,)),
+        ],
+        compiler_params=limit(12),
+        cost_estimate=LIGHT,
+        name="base",
+    )(held, in_place, other)
     panel, first_part = pl.pallas_call(
         functools.partial(lead_kernel, own_slots),
         out_shape=(panel_shape, first_shape),

time: 28.2 us -> 28.2 us (level)
  waiting for transfers between devices: 0.95 us -> 0.02 us
  starting transfers between devices: 15 us -> 15.9 us
    ppermute x1, starting transfers between devices: 0.07 us -> 1.84 us  [local(): arrived_near = lax.ppermute(leave_near, 'col', beside)]
    ppermute x3, waiting for transfers between devices: 0.94 us -> 0.01 us  [local(): lax.ppermute(packed[f], axes, swap)]
    ppermute x2, starting transfers between devices: 1.87 us -> 1.03 us  [local(): got[i] = lax.ppermute(leave, 'col', beside)]
    pallas_call x2 -> x1, Pallas kernels: 3.11 us -> 3.1 us  [local(): pl.pallas_call(base_kernel, out_shape=base_shapes, in_specs=[VMEM, HBM, V...]
  transfers between devices with their start and end apart: 9 -> 9, of which waited for: 3 -> 0; matrix products, arithmetic and copies ran while one was open for 0% -> 0% of each run, Pallas kernels for 37% -> 37%
where the time goes in v8:
time: 28.2 us; the launch traced here: 27.9 us
  starting transfers between devices  15.9 us (56%)
  Pallas kernels  11.9 us (42%)
    ppermute x3, starting transfers between devices, local(): lax.ppermute(packed[f], axes, swap)  6.62 us
    ppermute x1, starting transfers between devices, local(): swap_rows = lax.ppermute(swap_edge, axes, swap)  3.31 us
    pallas_call x1, Pallas kernels, local(): pl.pallas_call(base_kernel, out_shape=base_shapes, in_specs=[VMEM, HBM, V...  3.1 us
    ppermute x1, starting transfers between devices, local(): same_rows = lax.ppermute(same_edge, axes, same)  2.58 us
    pallas_call x1, Pallas kernels, local(): pl.pallas_call(functools.partial(near_kernel, far), out_shape=(panel_shap...  1.98 us
    ppermute x1, starting transfers between devices, local(): arrived_near = lax.ppermute(leave_near, 'col', beside)  1.84 us
    pallas_call x2, Pallas kernels, local(): pl.pallas_call(functools.partial(far_kernel, far, i), out_shape=(panel_sh...  1.68 us
    pallas_call x1, Pallas kernels, local(): pl.pallas_call(pack_kernel, out_shape=tuple((jax.ShapeDtypeStruct((reach...  1.39 us
  transfers between devices with their start and end apart: 9, of which 0 were waited for; matrix products, arithmetic and copies ran while one was open for 0% of the time, Pallas kernels for 37%

profile of v8, /device:TPU:0, one launch (start us, length us, event | category | flops | bytes accessed | tf_op | source)
XLA Modules:
  0.0 27.9 jit_solution(12902748783181285755)
XLA Ops:
  0.0 0.9 %edge.1 = (bf16[528,128]{1,0:T(8,128)(2,1)S(1)}, bf16[512,128]{1,0:T(8,128)(2,1)S(1)}, s32[8,8]{1,0:T(8,128)S(1)}) custom-call(s32[8,8]{1,0:T(8,128)} %columns_ref.1, bf16[8,4,128,128]{3,2,1,0:T(8,128)(2,1)} %matrix_ref.5), custom_call_target="tpu_custom_call" | custom-call | tf_op jit(solution)/shard_map/edge/pallas_call | solution.py:371
  0.9 0.5 %collective-permute-start = (bf16[8,4,128,128]{3,2,1,0:T(8,128)(2,1)}, bf16[8,4,128,128]{3,2,1,0:T(8,128)(2,1)S(1)}, u32[]{:S(2)}, u32[]{:S(2)}) collective-permute-start(bf16[8,4,128,128]{3,2,1,0:T(8,128)(2,1)} %matrix_ref.5), channel_id=1, source_target_pairs={{0,1},{1,0},{2,3},{3,2},{4,5},{5,4},{6,7},{7,6},{8,9},{9,8},{10,11... | collective-permute-start | bytes 3145736 | tf_op jit(solution)/shard_map/ppermute | solution.py:388
  1.4 2.6 %collective-permute-start.1 = (bf16[528,128]{1,0:T(8,128)(2,1)S(1)}, bf16[528,128]{1,0:T(8,128)(2,1)S(1)}, u32[]{:S(2)}, u32[]{:S(2)}) collective-permute-start(bf16[528,128]{1,0:T(8,128)(2,1)S(1)} %get-tuple-element.35), channel_id=1, source_target_pairs={{0,2},{2,4},{4,6},{6,8},{8,10},{10,12},{12,14},{14,0},{1,15},{3,1}... | collective-permute-start | bytes 405512 | tf_op jit(solution)/shard_map/ppermute | solution.py:385
  4.0 3.3 %collective-permute-start.2 = (bf16[512,128]{1,0:T(8,128)(2,1)S(1)}, bf16[512,128]{1,0:T(8,128)(2,1)S(1)}, u32[]{:S(2)}, u32[]{:S(2)}) collective-permute-start(bf16[512,128]{1,0:T(8,128)(2,1)S(1)} %get-tuple-element.36), channel_id=1, source_target_pairs={{1,2},{3,4},{5,6},{7,8},{9,10},{11,12},{13,14},{15,0},{0,15},{2,1}... | collective-permute-start | bytes 393224 | tf_op jit(solution)/shard_map/ppermute | solution.py:386
  7.3 0.0 collective-permute-done.other_ref
  7.3 1.4 %pack.1 = (bf16[5,128,128]{2,1,0:T(8,128)(2,1)S(1)}, bf16[6,128,128]{2,1,0:T(8,128)(2,1)S(1)}, bf16[7,128,128]{2,1,0:T(8,128)(2,1)S(1)}) custom-call(s32[8,8]{1,0:T(8,128)S(1)} %get-tuple-element.31.held_ref, bf16[8,4,128,128]{3,2,1,0:T(8,128)(2,1)} %matrix_ref.5, bf16[8,4,128,128]{3,2,1,0:T(8,128)(2,1)S(1)} %collective-permute-done.other_ref), custom_call_target="tpu_custom_call" | custom-call | tf_op jit(solution)/shard_map/pack/pallas_call | solution.py:401
  8.7 2.2 %collective-permute-start.3 = (bf16[7,128,128]{2,1,0:T(8,128)(2,1)S(1)}, bf16[7,128,128]{2,1,0:T(8,128)(2,1)S(1)}, u32[]{:S(2)}, u32[]{:S(2)}) collective-permute-start(bf16[7,128,128]{2,1,0:T(8,128)(2,1)S(1)} %get-tuple-element.41), channel_id=1, source_target_pairs={{1,2},{3,4},{5,6},{7,8},{9,10},{11,12},{13,14},{15,0},{0,15},{2,1}... | collective-permute-start | bytes 688136 | tf_op jit(solution)/shard_map/ppermute | solution.py:417
  10.9 2.3 %collective-permute-start.5 = (bf16[6,128,128]{2,1,0:T(8,128)(2,1)S(1)}, bf16[6,128,128]{2,1,0:T(8,128)(2,1)S(1)}, u32[]{:S(2)}, u32[]{:S(2)}) collective-permute-start(bf16[6,128,128]{2,1,0:T(8,128)(2,1)S(1)} %get-tuple-element.46), channel_id=1, source_target_pairs={{1,2},{3,4},{5,6},{7,8},{9,10},{11,12},{13,14},{15,0},{0,15},{2,1}... | collective-permute-start | bytes 589832 | tf_op jit(solution)/shard_map/ppermute | solution.py:417
  13.2 2.1 %collective-permute-start.4 = (bf16[5,128,128]{2,1,0:T(8,128)(2,1)S(1)}, bf16[5,128,128]{2,1,0:T(8,128)(2,1)S(1)}, u32[]{:S(2)}, u32[]{:S(2)}) collective-permute-start(bf16[5,128,128]{2,1,0:T(8,128)(2,1)S(1)} %get-tuple-element.45), channel_id=1, source_target_pairs={{1,2},{3,4},{5,6},{7,8},{9,10},{11,12},{13,14},{15,0},{0,15},{2,1}... | collective-permute-start | bytes 491528 | tf_op jit(solution)/shard_map/ppermute | solution.py:417
  15.4 3.1 %base.1 = (bf16[1536,1664]{1,0:T(8,128)(2,1)S(1)}, f32[512,1536]{1,0:T(8,128)S(1)}, f32[48,128]{1,0:T(8,128)S(1)}, f32[144,128]{1,0:T(8,128)S(1)}) custom-call(s32[8,8]{1,0:T(8,128)S(1)} %get-tuple-element.31.held_ref, bf16[8,4,128,128]{3,2,1,0:T(8,128)(2,1)} %matrix_ref.5, bf16[8,4,128,128]{3,2,1,0:T(8,128)(2,1)S(1)} %collective-permute-done.other_ref), custom_call_target="tpu_custom_call" | custom-call | tf_op jit(solution)/shard_map/base/pallas_call | solution.py:419
  18.5 0.0 collective-permute-done.2.swap_ref
  18.5 0.0 collective-permute-done.1.same_ref
  18.5 1.2 %lead.1 = (bf16[1536,1664]{1,0:T(8,128)(2,1)S(1)}, f32[512,1536]{1,0:T(8,128)S(1)}) custom-call(bf16[528,128]{1,0:T(8,128)(2,1)S(1)} %collective-permute-done.1.same_ref, bf16[512,128]{1,0:T(8,128)(2,1)S(1)} %collective-permute-done.2.swap_ref, bf16[1536,1664]{1,0:T(8,128)(2,1)S(1)} %get-tuple-element.37.before_panel, ...), custom_call_target="tpu_custom_call", output_to_operand_aliasing={{0}: (2, {}), {1}: (3, {})} | custom-call | flops 1200000000 | tf_op jit(solution)/shard_map/lead/pallas_call | solution.py:434
  19.7 2.0 %near.1 = (bf16[1536,1664]{1,0:T(8,128)(2,1)S(1)}, bf16[2,4,128,128]{3,2,1,0:T(8,128)(2,1)S(1)}, bf16[2,4,128,128]{3,2,1,0:T(8,128)(2,1)S(1)}, f32[256,768]{1,0:...) custom-call(s32[8,8]{1,0:T(8,128)S(1)} %get-tuple-element.31.held_ref, ...), custom_call_target="tpu_custom_call", output_to_operand_aliasing={{0}: (3, {})} | custom-call | flops 500000000 | tf_op jit(solution)/shard_map/near/pallas_call | solution.py:451
  21.7 1.8 %collective-permute-start.7 = (bf16[2,4,128,128]{3,2,1,0:T(8,128)(2,1)S(1)}, bf16[2,4,128,128]{3,2,1,0:T(8,128)(2,1)S(1)}, u32[]{:S(2)}, u32[]{:S(2)}) collective-permute-start(bf16[2,4,128,128]{3,2,1,0:T(8,128)(2,1)S(1)} %get-tuple-element.53), channel_id=1, source_target_pairs={{0,1},{1,0},{2,3},{3,2},{4,5},{5,4},{6,7},{7,6},{8,9},{9,8},{10,11... | collective-permute-start | bytes 786440 | tf_op jit(solution)/shard_map/ppermute | solution.py:474
  23.5 0.0 collective-permute-done.5.row_ref
  23.5 0.8 %far.2 = (bf16[1536,1664]{1,0:T(8,128)(2,1)S(1)}, bf16[1,4,128,128]{3,2,1,0:T(8,128)(2,1)S(1)}, bf16[1,4,128,128]{3,2,1,0:T(8,128)(2,1)S(1)}) custom-call(f32[48,128]{1,0:T(8,128)S(1)} %get-tuple-element.33.mask_ref, f32[144,128]{1,0:T(8,128)S(1)} %get-tuple-element.34.spot_ref, ...), custom_call_target="tpu_custom_call", output_to_operand_aliasing={{0}: (6, {})} | custom-call | flops 20000000000 | tf_op jit(solution)/shard_map/far/pallas_call | solution.py:479
  24.3 0.1 collective-permute-start.8
  24.5 0.0 collective-permute-done.4.row_ref
  24.5 0.9 %far.3 = (bf16[1536,1664]{1,0:T(8,128)(2,1)S(1)}, bf16[1,4,128,128]{3,2,1,0:T(8,128)(2,1)S(1)}, bf16[1,4,128,128]{3,2,1,0:T(8,128)(2,1)S(1)}) custom-call(f32[48,128]{1,0:T(8,128)S(1)} %get-tuple-element.33.mask_ref, f32[144,128]{1,0:T(8,128)S(1)} %get-tuple-element.34.spot_ref, ...), custom_call_target="tpu_custom_call", output_to_operand_aliasing={{0}: (6, {})} | custom-call | tf_op jit(solution)/shard_map/far/pallas_call | solution.py:479
  25.3 0.9 %collective-permute-start.6 = (bf16[1,4,128,128]{3,2,1,0:T(8,128)(2,1)S(1)}, bf16[1,4,128,128]{3,2,1,0:T(8,128)(2,1)S(1)}, u32[]{:S(2)}, u32[]{:S(2)}) collective-permute-start(bf16[1,4,128,128]{3,2,1,0:T(8,128)(2,1)S(1)} %get-tuple-element.49), channel_id=1, source_target_pairs={{0,1},{1,0},{2,3},{3,2},{4,5},{5,4},{6,7},{7,6},{8,9},{9,8},{10,11... | collective-permute-start | bytes 393224 | tf_op jit(solution)/shard_map/ppermute | solution.py:493
  26.2 0.0 collective-permute-done.8.refs_4_
  26.2 1.0 %store.1.before_ref = bf16[8,4,128,128]{3,2,1,0:T(8,128)(2,1)} custom-call(bf16[1,4,128,128]{3,2,1,0:T(8,128)(2,1)S(1)} %get-tuple-element.50.refs_0_, bf16[1,4,128,128]{3,2,1,0:T(8,128)(2,1)S(1)} %get-tuple-element.51.refs_1_, bf16[2,4,128,128]{3,2,1,0:T(8,128)(2,1)S(1)} %get-tuple-element.52.refs_2_, ...), custom_call_target="tpu_custom_call" | custom-call | tf_op jit(solution)/shard_map/store/pallas_call | solution.py:495
  27.2 0.7 %finish.1 = bf16[8,4,128,128]{3,2,1,0:T(8,128)(2,1)} custom-call(bf16[1,4,128,128]{3,2,1,0:T(8,128)(2,1)S(1)} %collective-permute-done.6.got_ref, bf16[8,4,128,128]{3,2,1,0:T(8,128)(2,1)} %store.1.before_ref), custom_call_target="tpu_custom_call", output_to_operand_aliasing={{}: (1, {})} | custom-call | tf_op jit(solution)/shard_map/finish/pallas_call | solution.py:505
  (3 shorter events, 0.0 us)
Async XLA Ops:
  0.9 6.4 %collective-permute-start = (bf16[8,4,128,128]{3,2,1,0:T(8,128)(2,1)}, bf16[8,4,128,128]{3,2,1,0:T(8,128)(2,1)S(1)}, u32[]{:S(2)}, u32[]{:S(2)}) collective-permute-start(bf16[8,4,128,128]{3,2,1,0:T(8,128)(2,1)} %matrix_ref.5), channel_id=1, source_target_pairs={{0,1},{1,0},{2,3},{3,2},{4,5},{5,4},{6,7},{7,6},{8,9},{9,8},{10,11... | collective-permute-start | bytes 3145736 | tf_op jit(solution)/shard_map/ppermute | solution.py:388
  1.4 17.0 %collective-permute-start.1 = (bf16[528,128]{1,0:T(8,128)(2,1)S(1)}, bf16[528,128]{1,0:T(8,128)(2,1)S(1)}, u32[]{:S(2)}, u32[]{:S(2)}) collective-permute-start(bf16[528,128]{1,0:T(8,128)(2,1)S(1)} %get-tuple-element.35), channel_id=1, source_target_pairs={{0,2},{2,4},{4,6},{6,8},{8,10},{10,12},{12,14},{14,0},{1,15},{3,1}... | collective-permute-start | bytes 405512 | tf_op jit(solution)/shard_map/ppermute | solution.py:385
  4.0 14.5 %collective-permute-start.2 = (bf16[512,128]{1,0:T(8,128)(2,1)S(1)}, bf16[512,128]{1,0:T(8,128)(2,1)S(1)}, u32[]{:S(2)}, u32[]{:S(2)}) collective-permute-start(bf16[512,128]{1,0:T(8,128)(2,1)S(1)} %get-tuple-element.36), channel_id=1, source_target_pairs={{1,2},{3,4},{5,6},{7,8},{9,10},{11,12},{13,14},{15,0},{0,15},{2,1}... | collective-permute-start | bytes 393224 | tf_op jit(solution)/shard_map/ppermute | solution.py:386
  8.7 10.9 %collective-permute-start.3 = (bf16[7,128,128]{2,1,0:T(8,128)(2,1)S(1)}, bf16[7,128,128]{2,1,0:T(8,128)(2,1)S(1)}, u32[]{:S(2)}, u32[]{:S(2)}) collective-permute-start(bf16[7,128,128]{2,1,0:T(8,128)(2,1)S(1)} %get-tuple-element.41), channel_id=1, source_target_pairs={{1,2},{3,4},{5,6},{7,8},{9,10},{11,12},{13,14},{15,0},{0,15},{2,1}... | collective-permute-start | bytes 688136 | tf_op jit(solution)/shard_map/ppermute | solution.py:417
  10.9 12.6 %collective-permute-start.5 = (bf16[6,128,128]{2,1,0:T(8,128)(2,1)S(1)}, bf16[6,128,128]{2,1,0:T(8,128)(2,1)S(1)}, u32[]{:S(2)}, u32[]{:S(2)}) collective-permute-start(bf16[6,128,128]{2,1,0:T(8,128)(2,1)S(1)} %get-tuple-element.46), channel_id=1, source_target_pairs={{1,2},{3,4},{5,6},{7,8},{9,10},{11,12},{13,14},{15,0},{0,15},{2,1}... | collective-permute-start | bytes 589832 | tf_op jit(solution)/shard_map/ppermute | solution.py:417
  13.2 11.2 %collective-permute-start.4 = (bf16[5,128,128]{2,1,0:T(8,128)(2,1)S(1)}, bf16[5,128,128]{2,1,0:T(8,128)(2,1)S(1)}, u32[]{:S(2)}, u32[]{:S(2)}) collective-permute-start(bf16[5,128,128]{2,1,0:T(8,128)(2,1)S(1)} %get-tuple-element.45), channel_id=1, source_target_pairs={{1,2},{3,4},{5,6},{7,8},{9,10},{11,12},{13,14},{15,0},{0,15},{2,1}... | collective-permute-start | bytes 491528 | tf_op jit(solution)/shard_map/ppermute | solution.py:417
  21.7 4.6 %collective-permute-start.7 = (bf16[2,4,128,128]{3,2,1,0:T(8,128)(2,1)S(1)}, bf16[2,4,128,128]{3,2,1,0:T(8,128)(2,1)S(1)}, u32[]{:S(2)}, u32[]{:S(2)}) collective-permute-start(bf16[2,4,128,128]{3,2,1,0:T(8,128)(2,1)S(1)} %get-tuple-element.53), channel_id=1, source_target_pairs={{0,1},{1,0},{2,3},{3,2},{4,5},{5,4},{6,7},{7,6},{8,9},{9,8},{10,11... | collective-permute-start | bytes 786440 | tf_op jit(solution)/shard_map/ppermute | solution.py:474
  24.3 1.9 %collective-permute-start.8 = (bf16[1,4,128,128]{3,2,1,0:T(8,128)(2,1)S(1)}, bf16[1,4,128,128]{3,2,1,0:T(8,128)(2,1)S(1)}, u32[]{:S(2)}, u32[]{:S(2)}) collective-permute-start(bf16[1,4,128,128]{3,2,1,0:T(8,128)(2,1)S(1)} %get-tuple-element.54), channel_id=1, source_target_pairs={{0,1},{1,0},{2,3},{3,2},{4,5},{5,4},{6,7},{7,6},{8,9},{9,8},{10,11... | collective-permute-start | bytes 393224 | tf_op jit(solution)/shard_map/ppermute | solution.py:493
  25.3 1.9 %collective-permute-start.6 = (bf16[1,4,128,128]{3,2,1,0:T(8,128)(2,1)S(1)}, bf16[1,4,128,128]{3,2,1,0:T(8,128)(2,1)S(1)}, u32[]{:S(2)}, u32[]{:S(2)}) collective-permute-start(bf16[1,4,128,128]{3,2,1,0:T(8,128)(2,1)S(1)} %get-tuple-element.49), channel_id=1, source_target_pairs={{0,1},{1,0},{2,3},{3,2},{4,5},{5,4},{6,7},{7,6},{8,9},{9,8},{10,11... | collective-permute-start | bytes 393224 | tf_op jit(solution)/shard_map/ppermute | solution.py:493

commit v9 on v7

--- a/solution.py
+++ b/solution.py
@@ -274,11 +274,12 @@
 
 
 def far_kernel(
-    far, i, mask_ref, spot_ref, part_ref, high_ref, cube_ref, row_ref, before_ref,
-    panel_ref, stay_ref, leave_ref, square, result
+    far, i, mask_ref, spot_ref, part_ref, high_ref, cube_ref, row_ref, after_ref, before_ref,
+    panel_ref, stay_ref, leave_ref, square, scratch
 ):
     reach = REACH
-    half, size = stay_ref.shape[1], stay_ref.shape[2]
+    result = scratch if i else stay_ref
+    half, size = leave_ref.shape[1], leave_ref.shape[2]
     width = panel_ref.shape[0] // size
     low_cols = reach + far
     far_cols = 2 * reach + far
@@ -307,40 +308,57 @@
         else:
             kept = high_ref[mine, blocks(2 * p - low_cols, 2 * p + 2 - low_cols, size)]
         result[:, cols] = (3.0 * kept.astype(jnp.float32) - 2.0 * value).astype(result.dtype)
-    window = 2 * reach + 1
-    for s in range(2 * half):
-        block = jnp.zeros((size, size), result.dtype)
-        for d in range(window):
-            at = (i * 2 * half + s) * window + d
-            block = jnp.where(spot_ref[at : at + 1, :] > 0, result[:, blocks(i + d, i + d + 1, size)], block)
+    for s in range(0 if i else half, 2 * half):
         target = stay_ref if s < half else leave_ref
-        target[0, s % half] = block
-
-
-def write_rows(pieces, out_ref, sems):
+        target[0, s % half] = chosen(result, spot_ref, i, s, 2 * half)
+
+
+def chosen(result, spot_ref, i, s, slots):
+    size = result.shape[0]
+    window = 2 * REACH + 1
+    block = jnp.zeros((size, size), result.dtype)
+    for d in range(window):
+        at = (i * slots + s) * window + d
+        block = jnp.where(spot_ref[at : at + 1, :] > 0, result[:, blocks(i + d, i + d + 1, size)], block)
+    return block
+
+
+def start_rows(pieces, out_ref, sems, first=0):
     straight = lax.axis_index("col") == 0
     copies = []
     for rows_ref, here, there in pieces:
         for n in range(rows_ref.shape[0]):
             to = out_ref.at[jnp.where(straight, here, there) + n]
-            copies.append(pltpu.make_async_copy(rows_ref.at[n], to, sems.at[len(copies)]))
+            copies.append(pltpu.make_async_copy(rows_ref.at[n], to, sems.at[first + len(copies)]))
     for copy in copies:
         copy.start()
+    return copies
+
+
+def write_rows(pieces, out_ref, sems):
+    for copy in start_rows(pieces, out_ref, sems):
+        copy.wait()
+
+
+def store_near_kernel(near_ref, out_ref, mark_ref, sems):
+    rows, near = out_ref.shape[0], near_ref.shape[0]
+    write_rows(((near_ref, rows // 2 - near, rows // 2),), out_ref, sems)
+    mark_ref[...] = jnp.zeros_like(mark_ref)
+
+
+def store_kernel(result_ref, spot_ref, got_near_ref, *refs):
+    *row_refs, before_ref, out_ref, stay, sems = refs
+    rows, near, half = out_ref.shape[0], got_near_ref.shape[0], out_ref.shape[1]
+    count = len(row_refs) // 2
+    pieces = [(got_near_ref, rows - 1 - count - near, 1 + count)]
+    pieces += [(ref, 1 + i, rows - 2 - i) for i, ref in enumerate(row_refs[:count])]
+    pieces += [(ref, rows - 2 - i, 1 + i) for i, ref in enumerate(row_refs[count:])]
+    copies = start_rows(pieces, out_ref, sems)
+    for s in range(half):
+        stay[0, s] = chosen(result_ref, spot_ref, 0, s, 2 * half)
+    copies += start_rows(((stay, 0, rows - 1),), out_ref, sems, len(copies))
     for copy in copies:
         copy.wait()
-
-
-def store_kernel(*refs):
-    *row_refs, out_ref, sems = refs
-    rows = out_ref.shape[0]
-    far = sum(ref.shape[0] == 1 for ref in row_refs) // 2 + 1
-    kept, near_ref, got_near_ref, got = row_refs[:far], row_refs[far], row_refs[far + 1], row_refs[far + 2 :]
-    near = near_ref.shape[0]
-    pieces = [(ref, i, rows - 1 - i) for i, ref in enumerate(kept)]
-    pieces.append((near_ref, far, rows - far - near))
-    pieces.append((got_near_ref, rows - far - near, far))
-    pieces += [(ref, rows - 2 - i, 1 + i) for i, ref in enumerate(got)]
-    write_rows(pieces, out_ref, sems)
 
 
 def finish_kernel(got_ref, before_ref, out_ref, sems):
@@ -478,15 +496,26 @@
     )(held, mask, first_part, panel, *[arrived[f] for f in range(far, lead)])
     arrived_near = lax.ppermute(leave_near, "col", beside)
 
+    out, mark = pl.pallas_call(
+        store_near_kernel,
+        out_shape=(jax.ShapeDtypeStruct(matrix.shape, dtype), jax.ShapeDtypeStruct((8, size), jnp.float32)),
+        in_specs=[VMEM],
+        out_specs=(HBM, VMEM),
+        scratch_shapes=[pltpu.SemaphoreType.DMA((near,))],
+        compiler_params=limit(1),
+        cost_estimate=LIGHT,
+        name="store_near",
+    )(stay_near)
     row_out = jax.ShapeDtypeStruct((1, own_slots, size, size), dtype)
+    result_out = jax.ShapeDtypeStruct((size, far_cols * size), dtype)
     stay, got = {}, {}
     for i in reversed(range(far)):
         panel, stay[i], leave = pl.pallas_call(
             functools.partial(far_kernel, far, i),
-            out_shape=(panel_shape, row_out, row_out),
-            in_specs=[VMEM] * 7,
+            out_shape=(panel_shape, row_out if i else result_out, row_out),
+            in_specs=[VMEM] * 8,
             out_specs=(VMEM,) * 3,
-            input_output_aliases={6: 0},
+            input_output_aliases={7: 0},
             scratch_shapes=[
                 pltpu.VMEM((size, low_cols * size), dtype),
                 pltpu.VMEM((size, far_cols * size), dtype),
@@ -494,19 +523,24 @@
             compiler_params=limit(16),
             cost_estimate=HEAVY if i else LIGHT,
             name="far",
-        )(mask, spot, part, high, cube, arrived[i], panel)
+        )(mask, spot, part, high, cube, arrived[i], mark, panel)
         got[i] = lax.ppermute(leave, "col", beside)
-    pieces = [*[stay[i] for i in range(far)], stay_near, arrived_near, *[got[i] for i in range(1, far)]]
+    rest = range(1, far)
+    pieces = [stay[0], spot, arrived_near, *[stay[i] for i in rest], *[got[i] for i in rest]]
     out = pl.pallas_call(
         store_kernel,
         out_shape=jax.ShapeDtypeStruct(matrix.shape, dtype),
-        in_specs=[VMEM] * len(pieces),
+        in_specs=[VMEM] * len(pieces) + [HBM],
         out_specs=HBM,
-        scratch_shapes=[pltpu.SemaphoreType.DMA((local_rows - 1,))],
-        compiler_params=limit(1),
+        input_output_aliases={len(pieces): 0},
+        scratch_shapes=[
+            pltpu.VMEM((1,) + matrix.shape[1:], dtype),
+            pltpu.SemaphoreType.DMA((local_rows - near - 1,)),
+        ],
+        compiler_params=limit(2),
         cost_estimate=LIGHT,
         name="store",
-    )(*pieces)
+    )(*pieces, out)
     return pl.pallas_call(
         finish_kernel,
         out_shape=jax.ShapeDtypeStruct(matrix.shape, dtype),

time: 28.2 us -> 28 us (level)
  waiting for transfers between devices: 0.95 us -> 0.39 us
  Pallas kernels: 11.9 us -> 12.2 us
    pallas_call x0 -> x1, Pallas kernels: none -> 0.73 us  [local(): pl.pallas_call(store_near_kernel, out_shape=(jax.ShapeDtypeStruct(matrix....]
    ppermute x3, waiting for transfers between devices: 0.94 us -> 0.28 us  [local(): lax.ppermute(packed[f], axes, swap)]
  transfers between devices with their start and end apart: 9 -> 9, of which waited for: 3 -> 2; matrix products, arithmetic and copies ran while one was open for 0% -> 0% of each run, Pallas kernels for 37% -> 38%
where the time goes in v9:
time: 28 us; the launch traced here: 27.7 us
  starting transfers between devices  15 us (54%)
  Pallas kernels  12.2 us (44%)
  waiting for transfers between devices  0.39 us (1%)
    ppermute x3, starting transfers between devices, local(): lax.ppermute(packed[f], axes, swap)  6.8 us
    ppermute x1, starting transfers between devices, local(): swap_rows = lax.ppermute(swap_edge, axes, swap)  3.31 us
    pallas_call x2, Pallas kernels, base(): pl.pallas_call(functools.partial(base_kernel, turn), out_shape=base_shape...  3.11 us
    ppermute x1, starting transfers between devices, local(): same_rows = lax.ppermute(same_edge, axes, same)  2.58 us
    pallas_call x1, Pallas kernels, local(): pl.pallas_call(functools.partial(near_kernel, far), out_shape=(panel_shap...  1.95 us
    ppermute x2, starting transfers between devices, local(): got[i] = lax.ppermute(leave, 'col', beside)  1.69 us
    pallas_call x2, Pallas kernels, local(): pl.pallas_call(functools.partial(far_kernel, far, i), out_shape=(panel_sh...  1.51 us
    pallas_call x1, Pallas kernels, local(): pl.pallas_call(pack_kernel, out_shape=tuple((jax.ShapeDtypeStruct((reach...  1.31 us
  transfers between devices with their start and end apart: 9, of which 2 were waited for; matrix products, arithmetic and copies ran while one was open for 0% of the time, Pallas kernels for 38%

profile of v9, /device:TPU:0, one launch (start us, length us, event | category | flops | bytes accessed | tf_op | source)
XLA Modules:
  0.0 27.7 jit_solution(14009053067279010613)
XLA Ops:
  0.0 0.9 %edge.1 = (bf16[528,128]{1,0:T(8,128)(2,1)S(1)}, bf16[512,128]{1,0:T(8,128)(2,1)S(1)}, s32[8,8]{1,0:T(8,128)S(1)}) custom-call(s32[8,8]{1,0:T(8,128)} %columns_ref.1, bf16[8,4,128,128]{3,2,1,0:T(8,128)(2,1)} %matrix_ref.7), custom_call_target="tpu_custom_call" | custom-call | tf_op jit(solution)/shard_map/edge/pallas_call | solution.py:389
  0.9 0.5 %collective-permute-start = (bf16[8,4,128,128]{3,2,1,0:T(8,128)(2,1)}, bf16[8,4,128,128]{3,2,1,0:T(8,128)(2,1)S(1)}, u32[]{:S(2)}, u32[]{:S(2)}) collective-permute-start(bf16[8,4,128,128]{3,2,1,0:T(8,128)(2,1)} %matrix_ref.7), channel_id=1, source_target_pairs={{0,1},{1,0},{2,3},{3,2},{4,5},{5,4},{6,7},{7,6},{8,9},{9,8},{10,11... | collective-permute-start | bytes 3145736 | tf_op jit(solution)/shard_map/ppermute | solution.py:406
  1.4 2.6 %collective-permute-start.1 = (bf16[528,128]{1,0:T(8,128)(2,1)S(1)}, bf16[528,128]{1,0:T(8,128)(2,1)S(1)}, u32[]{:S(2)}, u32[]{:S(2)}) collective-permute-start(bf16[528,128]{1,0:T(8,128)(2,1)S(1)} %get-tuple-element.45), channel_id=1, source_target_pairs={{0,2},{2,4},{4,6},{6,8},{8,10},{10,12},{12,14},{14,0},{1,15},{3,1}... | collective-permute-start | bytes 405512 | tf_op jit(solution)/shard_map/ppermute | solution.py:403
  4.0 3.3 %collective-permute-start.2 = (bf16[512,128]{1,0:T(8,128)(2,1)S(1)}, bf16[512,128]{1,0:T(8,128)(2,1)S(1)}, u32[]{:S(2)}, u32[]{:S(2)}) collective-permute-start(bf16[512,128]{1,0:T(8,128)(2,1)S(1)} %get-tuple-element.46), channel_id=1, source_target_pairs={{1,2},{3,4},{5,6},{7,8},{9,10},{11,12},{13,14},{15,0},{0,15},{2,1}... | collective-permute-start | bytes 393224 | tf_op jit(solution)/shard_map/ppermute | solution.py:404
  7.3 0.0 collective-permute-done.other_ref
  7.3 3.1 %base.2 = (bf16[1536,1664]{1,0:T(8,128)(2,1)S(1)}, f32[512,1536]{1,0:T(8,128)S(1)}, f32[48,128]{1,0:T(8,128)S(1)}, f32[144,128]{1,0:T(8,128)S(1)}) custom-call(s32[8,8]{1,0:T(8,128)S(1)} %get-tuple-element.37.held_ref, bf16[8,4,128,128]{3,2,1,0:T(8,128)(2,1)} %matrix_ref.7, bf16[8,4,128,128]{3,2,1,0:T(8,128)(2,1)S(1)} %collective-permute-done.other_ref), custom_call_target="tpu_custom_call" | custom-call | tf_op jit(solution)/shard_map/base/pallas_call | solution.py:420
  10.4 1.3 %pack.1 = (bf16[5,128,128]{2,1,0:T(8,128)(2,1)S(1)}, bf16[6,128,128]{2,1,0:T(8,128)(2,1)S(1)}, bf16[7,128,128]{2,1,0:T(8,128)(2,1)S(1)}) custom-call(s32[8,8]{1,0:T(8,128)S(1)} %get-tuple-element.37.held_ref, bf16[8,4,128,128]{3,2,1,0:T(8,128)(2,1)} %matrix_ref.7, bf16[8,4,128,128]{3,2,1,0:T(8,128)(2,1)S(1)} %collective-permute-done.other_ref, ...), custom_call_target="tpu_custom_call" | custom-call | tf_op jit(solution)/shard_map/pack/pallas_call | solution.py:438
  11.7 2.4 %collective-permute-start.3 = (bf16[7,128,128]{2,1,0:T(8,128)(2,1)S(1)}, bf16[7,128,128]{2,1,0:T(8,128)(2,1)S(1)}, u32[]{:S(2)}, u32[]{:S(2)}) collective-permute-start(bf16[7,128,128]{2,1,0:T(8,128)(2,1)S(1)} %get-tuple-element.51), channel_id=1, source_target_pairs={{1,2},{3,4},{5,6},{7,8},{9,10},{11,12},{13,14},{15,0},{0,15},{2,1}... | collective-permute-start | bytes 688136 | tf_op jit(solution)/shard_map/ppermute | solution.py:454
  14.1 2.1 %collective-permute-start.5 = (bf16[6,128,128]{2,1,0:T(8,128)(2,1)S(1)}, bf16[6,128,128]{2,1,0:T(8,128)(2,1)S(1)}, u32[]{:S(2)}, u32[]{:S(2)}) collective-permute-start(bf16[6,128,128]{2,1,0:T(8,128)(2,1)S(1)} %get-tuple-element.58), channel_id=1, source_target_pairs={{1,2},{3,4},{5,6},{7,8},{9,10},{11,12},{13,14},{15,0},{0,15},{2,1}... | collective-permute-start | bytes 589832 | tf_op jit(solution)/shard_map/ppermute | solution.py:454
  16.3 2.3 %collective-permute-start.4 = (bf16[5,128,128]{2,1,0:T(8,128)(2,1)S(1)}, bf16[5,128,128]{2,1,0:T(8,128)(2,1)S(1)}, u32[]{:S(2)}, u32[]{:S(2)}) collective-permute-start(bf16[5,128,128]{2,1,0:T(8,128)(2,1)S(1)} %get-tuple-element.55), channel_id=1, source_target_pairs={{1,2},{3,4},{5,6},{7,8},{9,10},{11,12},{13,14},{15,0},{0,15},{2,1}... | collective-permute-start | bytes 491528 | tf_op jit(solution)/shard_map/ppermute | solution.py:454
  18.6 0.0 collective-permute-done.1.same_ref
  18.6 1.2 %lead.1 = (bf16[1536,1664]{1,0:T(8,128)(2,1)S(1)}, f32[512,1536]{1,0:T(8,128)S(1)}) custom-call(bf16[528,128]{1,0:T(8,128)(2,1)S(1)} %collective-permute-done.1.same_ref, bf16[512,128]{1,0:T(8,128)(2,1)S(1)} %collective-permute-done.2.swap_ref, bf16[1536,1664]{1,0:T(8,128)(2,1)S(1)} %get-tuple-element.47.before_panel, ...), custom_call_target="tpu_custom_call", output_to_operand_aliasing={{0}: (2, {}), {1}: (3, {})} | custom-call | flops 1200000000 | tf_op jit(solution)/shard_map/lead/pallas_call | solution.py:457
  19.8 0.3 %collective-permute-done.3.refs_0_ = bf16[7,128,128]{2,1,0:T(8,128)(2,1)S(1)} collective-permute-done((bf16[7,128,128]{2,1,0:T(8,128)(2,1)S(1)}, bf16[7,128,128]{2,1,0:T(8,128)(2,1)S(1)}, u32[]{:S(2)}, u32[]{:S(2)}) %collective-permute-start.3) | collective-permute-done | bytes 229408 | tf_op jit(solution)/shard_map/ppermute | solution.py:454
  20.1 2.0 %near.1 = (bf16[1536,1664]{1,0:T(8,128)(2,1)S(1)}, bf16[2,4,128,128]{3,2,1,0:T(8,128)(2,1)S(1)}, bf16[2,4,128,128]{3,2,1,0:T(8,128)(2,1)S(1)}, f32[256,768]{1,0:...) custom-call(s32[8,8]{1,0:T(8,128)S(1)} %get-tuple-element.37.held_ref, ...), custom_call_target="tpu_custom_call", output_to_operand_aliasing={{0}: (3, {})} | custom-call | flops 500000000 | tf_op jit(solution)/shard_map/near/pallas_call | solution.py:474
  22.0 0.1 collective-permute-start.7
  22.1 0.7 %store_near.1 = (bf16[8,4,128,128]{3,2,1,0:T(8,128)(2,1)}, f32[8,128]{1,0:T(8,128)S(1)}) custom-call(bf16[2,4,128,128]{3,2,1,0:T(8,128)(2,1)S(1)} %get-tuple-element.56.near_ref), custom_call_target="tpu_custom_call" | custom-call | tf_op jit(solution)/shard_map/store_near/pallas_call | solution.py:499
  22.8 0.8 %far.2 = (bf16[1536,1664]{1,0:T(8,128)(2,1)S(1)}, bf16[1,4,128,128]{3,2,1,0:T(8,128)(2,1)S(1)}, bf16[1,4,128,128]{3,2,1,0:T(8,128)(2,1)S(1)}) custom-call(f32[48,128]{1,0:T(8,128)S(1)} %get-tuple-element.43.mask_ref, f32[144,128]{1,0:T(8,128)S(1)} %get-tuple-element.44.spot_ref, ...), custom_call_target="tpu_custom_call", output_to_operand_aliasing={{0}: (7, {})} | custom-call | flops 20000000000 | tf_op jit(solution)/shard_map/far/pallas_call | solution.py:513
  23.7 0.5 %collective-permute-start.8 = (bf16[1,4,128,128]{3,2,1,0:T(8,128)(2,1)S(1)}, bf16[1,4,128,128]{3,2,1,0:T(8,128)(2,1)S(1)}, u32[]{:S(2)}, u32[]{:S(2)}) collective-permute-start(bf16[1,4,128,128]{3,2,1,0:T(8,128)(2,1)S(1)} %get-tuple-element.65), channel_id=1, source_target_pairs={{0,1},{1,0},{2,3},{3,2},{4,5},{5,4},{6,7},{7,6},{8,9},{9,8},{10,11... | collective-permute-start | bytes 393224 | tf_op jit(solution)/shard_map/ppermute | solution.py:527
  24.2 0.0 collective-permute-done.4.row_ref
  24.2 0.7 %far.3 = (bf16[1536,1664]{1,0:T(8,128)(2,1)S(1)}, bf16[128,1280]{1,0:T(8,128)(2,1)S(1)}, bf16[1,4,128,128]{3,2,1,0:T(8,128)(2,1)S(1)}) custom-call(f32[48,128]{1,0:T(8,128)S(1)} %get-tuple-element.43.mask_ref, f32[144,128]{1,0:T(8,128)S(1)} %get-tuple-element.44.spot_ref, ...), custom_call_target="tpu_custom_call", output_to_operand_aliasing={{0}: (7, {})} | custom-call | tf_op jit(solution)/shard_map/far/pallas_call | solution.py:513
  24.9 1.1 %collective-permute-start.6 = (bf16[1,4,128,128]{3,2,1,0:T(8,128)(2,1)S(1)}, bf16[1,4,128,128]{3,2,1,0:T(8,128)(2,1)S(1)}, u32[]{:S(2)}, u32[]{:S(2)}) collective-permute-start(bf16[1,4,128,128]{3,2,1,0:T(8,128)(2,1)S(1)} %get-tuple-element.61), channel_id=1, source_target_pairs={{0,1},{1,0},{2,3},{3,2},{4,5},{5,4},{6,7},{7,6},{8,9},{9,8},{10,11... | collective-permute-start | bytes 393224 | tf_op jit(solution)/shard_map/ppermute | solution.py:527
  26.1 0.9 %store.1.before_ref = bf16[8,4,128,128]{3,2,1,0:T(8,128)(2,1)} custom-call(bf16[128,1280]{1,0:T(8,128)(2,1)S(1)} %get-tuple-element.62.result_ref, f32[144,128]{1,0:T(8,128)S(1)} %get-tuple-element.44.spot_ref, bf16[2,4,128,128]{3,2,1,0:T(8,128)(2,1)S(1)} %collective-permute-done.7.got_near_ref, ...), custom_call_target="tpu_custom_call", output_to_operand_aliasing={{}: (5, {})} | custom-call | tf_op jit(solution)/shard_map/store/pallas_call | solution.py:530
  27.0 0.1 collective-permute-done.6.got_ref
  27.0 0.7 %finish.1 = bf16[8,4,128,128]{3,2,1,0:T(8,128)(2,1)} custom-call(bf16[1,4,128,128]{3,2,1,0:T(8,128)(2,1)S(1)} %collective-permute-done.6.got_ref, bf16[8,4,128,128]{3,2,1,0:T(8,128)(2,1)} %store.1.before_ref), custom_call_target="tpu_custom_call", output_to_operand_aliasing={{}: (1, {})} | custom-call | tf_op jit(solution)/shard_map/finish/pallas_call | solution.py:544
  (5 shorter events, 0.0 us)
Async XLA Ops:
  0.9 6.4 %collective-permute-start = (bf16[8,4,128,128]{3,2,1,0:T(8,128)(2,1)}, bf16[8,4,128,128]{3,2,1,0:T(8,128)(2,1)S(1)}, u32[]{:S(2)}, u32[]{:S(2)}) collective-permute-start(bf16[8,4,128,128]{3,2,1,0:T(8,128)(2,1)} %matrix_ref.7), channel_id=1, source_target_pairs={{0,1},{1,0},{2,3},{3,2},{4,5},{5,4},{6,7},{7,6},{8,9},{9,8},{10,11... | collective-permute-start | bytes 3145736 | tf_op jit(solution)/shard_map/ppermute | solution.py:406
  1.4 17.2 %collective-permute-start.1 = (bf16[528,128]{1,0:T(8,128)(2,1)S(1)}, bf16[528,128]{1,0:T(8,128)(2,1)S(1)}, u32[]{:S(2)}, u32[]{:S(2)}) collective-permute-start(bf16[528,128]{1,0:T(8,128)(2,1)S(1)} %get-tuple-element.45), channel_id=1, source_target_pairs={{0,2},{2,4},{4,6},{6,8},{8,10},{10,12},{12,14},{14,0},{1,15},{3,1}... | collective-permute-start | bytes 405512 | tf_op jit(solution)/shard_map/ppermute | solution.py:403
  4.0 14.6 %collective-permute-start.2 = (bf16[512,128]{1,0:T(8,128)(2,1)S(1)}, bf16[512,128]{1,0:T(8,128)(2,1)S(1)}, u32[]{:S(2)}, u32[]{:S(2)}) collective-permute-start(bf16[512,128]{1,0:T(8,128)(2,1)S(1)} %get-tuple-element.46), channel_id=1, source_target_pairs={{1,2},{3,4},{5,6},{7,8},{9,10},{11,12},{13,14},{15,0},{0,15},{2,1}... | collective-permute-start | bytes 393224 | tf_op jit(solution)/shard_map/ppermute | solution.py:404
  11.7 8.3 %collective-permute-start.3 = (bf16[7,128,128]{2,1,0:T(8,128)(2,1)S(1)}, bf16[7,128,128]{2,1,0:T(8,128)(2,1)S(1)}, u32[]{:S(2)}, u32[]{:S(2)}) collective-permute-start(bf16[7,128,128]{2,1,0:T(8,128)(2,1)S(1)} %get-tuple-element.51), channel_id=1, source_target_pairs={{1,2},{3,4},{5,6},{7,8},{9,10},{11,12},{13,14},{15,0},{0,15},{2,1}... | collective-permute-start | bytes 688136 | tf_op jit(solution)/shard_map/ppermute | solution.py:454
  14.1 8.7 %collective-permute-start.5 = (bf16[6,128,128]{2,1,0:T(8,128)(2,1)S(1)}, bf16[6,128,128]{2,1,0:T(8,128)(2,1)S(1)}, u32[]{:S(2)}, u32[]{:S(2)}) collective-permute-start(bf16[6,128,128]{2,1,0:T(8,128)(2,1)S(1)} %get-tuple-element.58), channel_id=1, source_target_pairs={{1,2},{3,4},{5,6},{7,8},{9,10},{11,12},{13,14},{15,0},{0,15},{2,1}... | collective-permute-start | bytes 589832 | tf_op jit(solution)/shard_map/ppermute | solution.py:454
  16.3 8.0 %collective-permute-start.4 = (bf16[5,128,128]{2,1,0:T(8,128)(2,1)S(1)}, bf16[5,128,128]{2,1,0:T(8,128)(2,1)S(1)}, u32[]{:S(2)}, u32[]{:S(2)}) collective-permute-start(bf16[5,128,128]{2,1,0:T(8,128)(2,1)S(1)} %get-tuple-element.55), channel_id=1, source_target_pairs={{1,2},{3,4},{5,6},{7,8},{9,10},{11,12},{13,14},{15,0},{0,15},{2,1}... | collective-permute-start | bytes 491528 | tf_op jit(solution)/shard_map/ppermute | solution.py:454
  22.0 4.0 %collective-permute-start.7 = (bf16[2,4,128,128]{3,2,1,0:T(8,128)(2,1)S(1)}, bf16[2,4,128,128]{3,2,1,0:T(8,128)(2,1)S(1)}, u32[]{:S(2)}, u32[]{:S(2)}) collective-permute-start(bf16[2,4,128,128]{3,2,1,0:T(8,128)(2,1)S(1)} %get-tuple-element.63), channel_id=1, source_target_pairs={{0,1},{1,0},{2,3},{3,2},{4,5},{5,4},{6,7},{7,6},{8,9},{9,8},{10,11... | collective-permute-start | bytes 786440 | tf_op jit(solution)/shard_map/ppermute | solution.py:497
  23.7 2.4 %collective-permute-start.8 = (bf16[1,4,128,128]{3,2,1,0:T(8,128)(2,1)S(1)}, bf16[1,4,128,128]{3,2,1,0:T(8,128)(2,1)S(1)}, u32[]{:S(2)}, u32[]{:S(2)}) collective-permute-start(bf16[1,4,128,128]{3,2,1,0:T(8,128)(2,1)S(1)} %get-tuple-element.65), channel_id=1, source_target_pairs={{0,1},{1,0},{2,3},{3,2},{4,5},{5,4},{6,7},{7,6},{8,9},{9,8},{10,11... | collective-permute-start | bytes 393224 | tf_op jit(solution)/shard_map/ppermute | solution.py:527
  24.9 2.1 %collective-permute-start.6 = (bf16[1,4,128,128]{3,2,1,0:T(8,128)(2,1)S(1)}, bf16[1,4,128,128]{3,2,1,0:T(8,128)(2,1)S(1)}, u32[]{:S(2)}, u32[]{:S(2)}) collective-permute-start(bf16[1,4,128,128]{3,2,1,0:T(8,128)(2,1)S(1)} %get-tuple-element.61), channel_id=1, source_target_pairs={{0,1},{1,0},{2,3},{3,2},{4,5},{5,4},{6,7},{7,6},{8,9},{9,8},{10,11... | collective-permute-start | bytes 393224 | tf_op jit(solution)/shard_map/ppermute | solution.py:527

commit v10 on v9

--- a/solution.py
+++ b/solution.py
@@ -318,6 +318,8 @@
     window = 2 * REACH + 1
     block = jnp.zeros((size, size), result.dtype)
     for d in range(window):
+        if d == REACH and s % (slots // 2):
+            continue
         at = (i * slots + s) * window + d
         block = jnp.where(spot_ref[at : at + 1, :] > 0, result[:, blocks(i + d, i + d + 1, size)], block)
     return block

time: 28 us -> 28 us (level)
  transfers between devices with their start and end apart: 9 -> 9, of which waited for: 2 -> 2; matrix products, arithmetic and copies ran while one was open for 0% -> 0% of each run, Pallas kernels for 38% -> 39%
where the time goes in v10:
time: 28 us; the launch traced here: 27.7 us
  starting transfers between devices  14.9 us (53%)
  Pallas kernels  12.2 us (44%)
  waiting for transfers between devices  0.39 us (1%)
    ppermute x3, starting transfers between devices, local(): lax.ppermute(packed[f], axes, swap)  6.8 us
    ppermute x1, starting transfers between devices, local(): swap_rows = lax.ppermute(swap_edge, axes, swap)  3.31 us
    pallas_call x2, Pallas kernels, base(): pl.pallas_call(functools.partial(base_kernel, turn), out_shape=base_shape...  3.11 us
    ppermute x1, starting transfers between devices, local(): same_rows = lax.ppermute(same_edge, axes, same)  2.58 us
    pallas_call x1, Pallas kernels, local(): pl.pallas_call(functools.partial(near_kernel, far), out_shape=(panel_shap...  1.95 us
    ppermute x2, starting transfers between devices, local(): got[i] = lax.ppermute(leave, 'col', beside)  1.65 us
    pallas_call x2, Pallas kernels, local(): pl.pallas_call(functools.partial(far_kernel, far, i), out_shape=(panel_sh...  1.44 us
    pallas_call x1, Pallas kernels, local(): pl.pallas_call(pack_kernel, out_shape=tuple((jax.ShapeDtypeStruct((reach...  1.39 us
  transfers between devices with their start and end apart: 9, of which 2 were waited for; matrix products, arithmetic and copies ran while one was open for 0% of the time, Pallas kernels for 39%

profile of v10, /device:TPU:0, one launch (start us, length us, event | category | flops | bytes accessed | tf_op | source)
XLA Modules:
  0.0 27.7 jit_solution(13384821252216434657)
XLA Ops:
  0.0 0.9 %edge.1 = (bf16[528,128]{1,0:T(8,128)(2,1)S(1)}, bf16[512,128]{1,0:T(8,128)(2,1)S(1)}, s32[8,8]{1,0:T(8,128)S(1)}) custom-call(s32[8,8]{1,0:T(8,128)} %columns_ref.1, bf16[8,4,128,128]{3,2,1,0:T(8,128)(2,1)} %matrix_ref.7), custom_call_target="tpu_custom_call" | custom-call | tf_op jit(solution)/shard_map/edge/pallas_call | solution.py:391
  0.9 0.5 %collective-permute-start = (bf16[8,4,128,128]{3,2,1,0:T(8,128)(2,1)}, bf16[8,4,128,128]{3,2,1,0:T(8,128)(2,1)S(1)}, u32[]{:S(2)}, u32[]{:S(2)}) collective-permute-start(bf16[8,4,128,128]{3,2,1,0:T(8,128)(2,1)} %matrix_ref.7), channel_id=1, source_target_pairs={{0,1},{1,0},{2,3},{3,2},{4,5},{5,4},{6,7},{7,6},{8,9},{9,8},{10,11... | collective-permute-start | bytes 3145736 | tf_op jit(solution)/shard_map/ppermute | solution.py:408
  1.4 2.6 %collective-permute-start.1 = (bf16[528,128]{1,0:T(8,128)(2,1)S(1)}, bf16[528,128]{1,0:T(8,128)(2,1)S(1)}, u32[]{:S(2)}, u32[]{:S(2)}) collective-permute-start(bf16[528,128]{1,0:T(8,128)(2,1)S(1)} %get-tuple-element.45), channel_id=1, source_target_pairs={{0,2},{2,4},{4,6},{6,8},{8,10},{10,12},{12,14},{14,0},{1,15},{3,1}... | collective-permute-start | bytes 405512 | tf_op jit(solution)/shard_map/ppermute | solution.py:405
  4.0 3.3 %collective-permute-start.2 = (bf16[512,128]{1,0:T(8,128)(2,1)S(1)}, bf16[512,128]{1,0:T(8,128)(2,1)S(1)}, u32[]{:S(2)}, u32[]{:S(2)}) collective-permute-start(bf16[512,128]{1,0:T(8,128)(2,1)S(1)} %get-tuple-element.46), channel_id=1, source_target_pairs={{1,2},{3,4},{5,6},{7,8},{9,10},{11,12},{13,14},{15,0},{0,15},{2,1}... | collective-permute-start | bytes 393224 | tf_op jit(solution)/shard_map/ppermute | solution.py:406
  7.3 3.1 %base.2 = (bf16[1536,1664]{1,0:T(8,128)(2,1)S(1)}, f32[512,1536]{1,0:T(8,128)S(1)}, f32[48,128]{1,0:T(8,128)S(1)}, f32[144,128]{1,0:T(8,128)S(1)}) custom-call(s32[8,8]{1,0:T(8,128)S(1)} %get-tuple-element.37.held_ref, bf16[8,4,128,128]{3,2,1,0:T(8,128)(2,1)} %matrix_ref.7, bf16[8,4,128,128]{3,2,1,0:T(8,128)(2,1)S(1)} %collective-permute-done.other_ref), custom_call_target="tpu_custom_call" | custom-call | tf_op jit(solution)/shard_map/base/pallas_call | solution.py:422
  10.4 1.4 %pack.1 = (bf16[5,128,128]{2,1,0:T(8,128)(2,1)S(1)}, bf16[6,128,128]{2,1,0:T(8,128)(2,1)S(1)}, bf16[7,128,128]{2,1,0:T(8,128)(2,1)S(1)}) custom-call(s32[8,8]{1,0:T(8,128)S(1)} %get-tuple-element.37.held_ref, bf16[8,4,128,128]{3,2,1,0:T(8,128)(2,1)} %matrix_ref.7, bf16[8,4,128,128]{3,2,1,0:T(8,128)(2,1)S(1)} %collective-permute-done.other_ref, ...), custom_call_target="tpu_custom_call" | custom-call | tf_op jit(solution)/shard_map/pack/pallas_call | solution.py:440
  11.8 2.4 %collective-permute-start.3 = (bf16[7,128,128]{2,1,0:T(8,128)(2,1)S(1)}, bf16[7,128,128]{2,1,0:T(8,128)(2,1)S(1)}, u32[]{:S(2)}, u32[]{:S(2)}) collective-permute-start(bf16[7,128,128]{2,1,0:T(8,128)(2,1)S(1)} %get-tuple-element.51), channel_id=1, source_target_pairs={{1,2},{3,4},{5,6},{7,8},{9,10},{11,12},{13,14},{15,0},{0,15},{2,1}... | collective-permute-start | bytes 688136 | tf_op jit(solution)/shard_map/ppermute | solution.py:456
  14.2 2.1 %collective-permute-start.5 = (bf16[6,128,128]{2,1,0:T(8,128)(2,1)S(1)}, bf16[6,128,128]{2,1,0:T(8,128)(2,1)S(1)}, u32[]{:S(2)}, u32[]{:S(2)}) collective-permute-start(bf16[6,128,128]{2,1,0:T(8,128)(2,1)S(1)} %get-tuple-element.58), channel_id=1, source_target_pairs={{1,2},{3,4},{5,6},{7,8},{9,10},{11,12},{13,14},{15,0},{0,15},{2,1}... | collective-permute-start | bytes 589832 | tf_op jit(solution)/shard_map/ppermute | solution.py:456
  16.3 2.3 %collective-permute-start.4 = (bf16[5,128,128]{2,1,0:T(8,128)(2,1)S(1)}, bf16[5,128,128]{2,1,0:T(8,128)(2,1)S(1)}, u32[]{:S(2)}, u32[]{:S(2)}) collective-permute-start(bf16[5,128,128]{2,1,0:T(8,128)(2,1)S(1)} %get-tuple-element.55), channel_id=1, source_target_pairs={{1,2},{3,4},{5,6},{7,8},{9,10},{11,12},{13,14},{15,0},{0,15},{2,1}... | collective-permute-start | bytes 491528 | tf_op jit(solution)/shard_map/ppermute | solution.py:456
  18.7 0.0 collective-permute-done.2.swap_ref
  18.7 0.0 collective-permute-done.1.same_ref
  18.7 1.2 %lead.1 = (bf16[1536,1664]{1,0:T(8,128)(2,1)S(1)}, f32[512,1536]{1,0:T(8,128)S(1)}) custom-call(bf16[528,128]{1,0:T(8,128)(2,1)S(1)} %collective-permute-done.1.same_ref, bf16[512,128]{1,0:T(8,128)(2,1)S(1)} %collective-permute-done.2.swap_ref, bf16[1536,1664]{1,0:T(8,128)(2,1)S(1)} %get-tuple-element.47.before_panel, ...), custom_call_target="tpu_custom_call", output_to_operand_aliasing={{0}: (2, {}), {1}: (3, {})} | custom-call | flops 1200000000 | tf_op jit(solution)/shard_map/lead/pallas_call | solution.py:459
  19.9 0.3 %collective-permute-done.3.refs_0_ = bf16[7,128,128]{2,1,0:T(8,128)(2,1)S(1)} collective-permute-done((bf16[7,128,128]{2,1,0:T(8,128)(2,1)S(1)}, bf16[7,128,128]{2,1,0:T(8,128)(2,1)S(1)}, u32[]{:S(2)}, u32[]{:S(2)}) %collective-permute-start.3) | collective-permute-done | bytes 229408 | tf_op jit(solution)/shard_map/ppermute | solution.py:456
  20.1 2.0 %near.1 = (bf16[1536,1664]{1,0:T(8,128)(2,1)S(1)}, bf16[2,4,128,128]{3,2,1,0:T(8,128)(2,1)S(1)}, bf16[2,4,128,128]{3,2,1,0:T(8,128)(2,1)S(1)}, f32[256,768]{1,0:...) custom-call(s32[8,8]{1,0:T(8,128)S(1)} %get-tuple-element.37.held_ref, ...), custom_call_target="tpu_custom_call", output_to_operand_aliasing={{0}: (3, {})} | custom-call | flops 500000000 | tf_op jit(solution)/shard_map/near/pallas_call | solution.py:476
  22.1 0.1 collective-permute-start.7
  22.2 0.7 %store_near.1 = (bf16[8,4,128,128]{3,2,1,0:T(8,128)(2,1)}, f32[8,128]{1,0:T(8,128)S(1)}) custom-call(bf16[2,4,128,128]{3,2,1,0:T(8,128)(2,1)S(1)} %get-tuple-element.56.near_ref), custom_call_target="tpu_custom_call" | custom-call | tf_op jit(solution)/shard_map/store_near/pallas_call | solution.py:501
  22.9 0.0 collective-permute-done.5.row_ref
  22.9 0.8 %far.2 = (bf16[1536,1664]{1,0:T(8,128)(2,1)S(1)}, bf16[1,4,128,128]{3,2,1,0:T(8,128)(2,1)S(1)}, bf16[1,4,128,128]{3,2,1,0:T(8,128)(2,1)S(1)}) custom-call(f32[48,128]{1,0:T(8,128)S(1)} %get-tuple-element.43.mask_ref, f32[144,128]{1,0:T(8,128)S(1)} %get-tuple-element.44.spot_ref, ...), custom_call_target="tpu_custom_call", output_to_operand_aliasing={{0}: (7, {})} | custom-call | flops 20000000000 | tf_op jit(solution)/shard_map/far/pallas_call | solution.py:515
  23.7 0.6 %collective-permute-start.8 = (bf16[1,4,128,128]{3,2,1,0:T(8,128)(2,1)S(1)}, bf16[1,4,128,128]{3,2,1,0:T(8,128)(2,1)S(1)}, u32[]{:S(2)}, u32[]{:S(2)}) collective-permute-start(bf16[1,4,128,128]{3,2,1,0:T(8,128)(2,1)S(1)} %get-tuple-element.65), channel_id=1, source_target_pairs={{0,1},{1,0},{2,3},{3,2},{4,5},{5,4},{6,7},{7,6},{8,9},{9,8},{10,11... | collective-permute-start | bytes 393224 | tf_op jit(solution)/shard_map/ppermute | solution.py:529
  24.3 0.7 %far.3 = (bf16[1536,1664]{1,0:T(8,128)(2,1)S(1)}, bf16[128,1280]{1,0:T(8,128)(2,1)S(1)}, bf16[1,4,128,128]{3,2,1,0:T(8,128)(2,1)S(1)}) custom-call(f32[48,128]{1,0:T(8,128)S(1)} %get-tuple-element.43.mask_ref, f32[144,128]{1,0:T(8,128)S(1)} %get-tuple-element.44.spot_ref, ...), custom_call_target="tpu_custom_call", output_to_operand_aliasing={{0}: (7, {})} | custom-call | tf_op jit(solution)/shard_map/far/pallas_call | solution.py:515
  24.9 1.1 %collective-permute-start.6 = (bf16[1,4,128,128]{3,2,1,0:T(8,128)(2,1)S(1)}, bf16[1,4,128,128]{3,2,1,0:T(8,128)(2,1)S(1)}, u32[]{:S(2)}, u32[]{:S(2)}) collective-permute-start(bf16[1,4,128,128]{3,2,1,0:T(8,128)(2,1)S(1)} %get-tuple-element.61), channel_id=1, source_target_pairs={{0,1},{1,0},{2,3},{3,2},{4,5},{5,4},{6,7},{7,6},{8,9},{9,8},{10,11... | collective-permute-start | bytes 393224 | tf_op jit(solution)/shard_map/ppermute | solution.py:529
  26.0 0.9 %store.1.before_ref = bf16[8,4,128,128]{3,2,1,0:T(8,128)(2,1)} custom-call(bf16[128,1280]{1,0:T(8,128)(2,1)S(1)} %get-tuple-element.62.result_ref, f32[144,128]{1,0:T(8,128)S(1)} %get-tuple-element.44.spot_ref, bf16[2,4,128,128]{3,2,1,0:T(8,128)(2,1)S(1)} %collective-permute-done.7.got_near_ref, ...), custom_call_target="tpu_custom_call", output_to_operand_aliasing={{}: (5, {})} | custom-call | tf_op jit(solution)/shard_map/store/pallas_call | solution.py:532
  26.9 0.1 collective-permute-done.6.got_ref
  27.0 0.7 %finish.1 = bf16[8,4,128,128]{3,2,1,0:T(8,128)(2,1)} custom-call(bf16[1,4,128,128]{3,2,1,0:T(8,128)(2,1)S(1)} %collective-permute-done.6.got_ref, bf16[8,4,128,128]{3,2,1,0:T(8,128)(2,1)} %store.1.before_ref), custom_call_target="tpu_custom_call", output_to_operand_aliasing={{}: (1, {})} | custom-call | tf_op jit(solution)/shard_map/finish/pallas_call | solution.py:546
  (5 shorter events, 0.0 us)
Async XLA Ops:
  0.9 6.4 %collective-permute-start = (bf16[8,4,128,128]{3,2,1,0:T(8,128)(2,1)}, bf16[8,4,128,128]{3,2,1,0:T(8,128)(2,1)S(1)}, u32[]{:S(2)}, u32[]{:S(2)}) collective-permute-start(bf16[8,4,128,128]{3,2,1,0:T(8,128)(2,1)} %matrix_ref.7), channel_id=1, source_target_pairs={{0,1},{1,0},{2,3},{3,2},{4,5},{5,4},{6,7},{7,6},{8,9},{9,8},{10,11... | collective-permute-start | bytes 3145736 | tf_op jit(solution)/shard_map/ppermute | solution.py:408
  1.4 17.2 %collective-permute-start.1 = (bf16[528,128]{1,0:T(8,128)(2,1)S(1)}, bf16[528,128]{1,0:T(8,128)(2,1)S(1)}, u32[]{:S(2)}, u32[]{:S(2)}) collective-permute-start(bf16[528,128]{1,0:T(8,128)(2,1)S(1)} %get-tuple-element.45), channel_id=1, source_target_pairs={{0,2},{2,4},{4,6},{6,8},{8,10},{10,12},{12,14},{14,0},{1,15},{3,1}... | collective-permute-start | bytes 405512 | tf_op jit(solution)/shard_map/ppermute | solution.py:405
  4.0 14.6 %collective-permute-start.2 = (bf16[512,128]{1,0:T(8,128)(2,1)S(1)}, bf16[512,128]{1,0:T(8,128)(2,1)S(1)}, u32[]{:S(2)}, u32[]{:S(2)}) collective-permute-start(bf16[512,128]{1,0:T(8,128)(2,1)S(1)} %get-tuple-element.46), channel_id=1, source_target_pairs={{1,2},{3,4},{5,6},{7,8},{9,10},{11,12},{13,14},{15,0},{0,15},{2,1}... | collective-permute-start | bytes 393224 | tf_op jit(solution)/shard_map/ppermute | solution.py:406
  11.8 8.3 %collective-permute-start.3 = (bf16[7,128,128]{2,1,0:T(8,128)(2,1)S(1)}, bf16[7,128,128]{2,1,0:T(8,128)(2,1)S(1)}, u32[]{:S(2)}, u32[]{:S(2)}) collective-permute-start(bf16[7,128,128]{2,1,0:T(8,128)(2,1)S(1)} %get-tuple-element.51), channel_id=1, source_target_pairs={{1,2},{3,4},{5,6},{7,8},{9,10},{11,12},{13,14},{15,0},{0,15},{2,1}... | collective-permute-start | bytes 688136 | tf_op jit(solution)/shard_map/ppermute | solution.py:456
  14.2 8.7 %collective-permute-start.5 = (bf16[6,128,128]{2,1,0:T(8,128)(2,1)S(1)}, bf16[6,128,128]{2,1,0:T(8,128)(2,1)S(1)}, u32[]{:S(2)}, u32[]{:S(2)}) collective-permute-start(bf16[6,128,128]{2,1,0:T(8,128)(2,1)S(1)} %get-tuple-element.58), channel_id=1, source_target_pairs={{1,2},{3,4},{5,6},{7,8},{9,10},{11,12},{13,14},{15,0},{0,15},{2,1}... | collective-permute-start | bytes 589832 | tf_op jit(solution)/shard_map/ppermute | solution.py:456
  16.3 7.9 %collective-permute-start.4 = (bf16[5,128,128]{2,1,0:T(8,128)(2,1)S(1)}, bf16[5,128,128]{2,1,0:T(8,128)(2,1)S(1)}, u32[]{:S(2)}, u32[]{:S(2)}) collective-permute-start(bf16[5,128,128]{2,1,0:T(8,128)(2,1)S(1)} %get-tuple-element.55), channel_id=1, source_target_pairs={{1,2},{3,4},{5,6},{7,8},{9,10},{11,12},{13,14},{15,0},{0,15},{2,1}... | collective-permute-start | bytes 491528 | tf_op jit(solution)/shard_map/ppermute | solution.py:456
  22.1 3.9 %collective-permute-start.7 = (bf16[2,4,128,128]{3,2,1,0:T(8,128)(2,1)S(1)}, bf16[2,4,128,128]{3,2,1,0:T(8,128)(2,1)S(1)}, u32[]{:S(2)}, u32[]{:S(2)}) collective-permute-start(bf16[2,4,128,128]{3,2,1,0:T(8,128)(2,1)S(1)} %get-tuple-element.63), channel_id=1, source_target_pairs={{0,1},{1,0},{2,3},{3,2},{4,5},{5,4},{6,7},{7,6},{8,9},{9,8},{10,11... | collective-permute-start | bytes 786440 | tf_op jit(solution)/shard_map/ppermute | solution.py:499
  23.7 2.3 %collective-permute-start.8 = (bf16[1,4,128,128]{3,2,1,0:T(8,128)(2,1)S(1)}, bf16[1,4,128,128]{3,2,1,0:T(8,128)(2,1)S(1)}, u32[]{:S(2)}, u32[]{:S(2)}) collective-permute-start(bf16[1,4,128,128]{3,2,1,0:T(8,128)(2,1)S(1)} %get-tuple-element.65), channel_id=1, source_target_pairs={{0,1},{1,0},{2,3},{3,2},{4,5},{5,4},{6,7},{7,6},{8,9},{9,8},{10,11... | collective-permute-start | bytes 393224 | tf_op jit(solution)/shard_map/ppermute | solution.py:529
  24.9 2.1 %collective-permute-start.6 = (bf16[1,4,128,128]{3,2,1,0:T(8,128)(2,1)S(1)}, bf16[1,4,128,128]{3,2,1,0:T(8,128)(2,1)S(1)}, u32[]{:S(2)}, u32[]{:S(2)}) collective-permute-start(bf16[1,4,128,128]{3,2,1,0:T(8,128)(2,1)S(1)} %get-tuple-element.61), channel_id=1, source_target_pairs={{0,1},{1,0},{2,3},{3,2},{4,5},{5,4},{6,7},{7,6},{8,9},{9,8},{10,11... | collective-permute-start | bytes 393224 | tf_op jit(solution)/shard_map/ppermute | solution.py:529
